TPU v7x, 128 devices: a whole 4x4x4 slice. The times are simulated.
128 devices in a mesh: row: 8 (over z_hi, y), col: 16 (over x, z_lo, core).
Axes of the slice: x: 4, y: 4, z: 4 (z_hi: 2, z_lo: 2; z = z_hi * 2 + z_lo), core: 2. Of those that a mesh axis runs over, the one named last changes fastest.
Arguments:
- prompt: bfloat16 [1024, 16384], P(None, ('row', 'col')), may hold values from -0.031982422 to 0.031982422
- base_weight: bfloat16 [16384, 32768], P('row', 'col'), may hold values from -2 to 2
- factor_left: bfloat16 [16384, 64], P(('row', 'col')), may hold values from -0.046875 to 0.046875
- factor_right: bfloat16 [64, 32768], P('row', 'col'), may hold values from -0.75 to 0.75
- magnitude: float32 [32768], P('col'), may hold values from 64 to 512
Outputs:
- serving_weight: bfloat16 [8, 16384, 4096], P('row', None, 'col')
- prefill_out: bfloat16 [8, 1024, 4096], P('row', None, 'col')
All inputs are finite; a program needn't handle non-finite values.
Results may differ from a plain program's by a relative error of at most 0.005.
Values may be sent and summed in bfloat16 or wider, within the bound.
No kernel may reach another device: no remote copies, remote signals or barrier semaphores. Data moves between devices by JAX's collectives and lax.ppermute only.
A program may use at most 192 MiB of HBM per device.

v0:
```python
import jax
import jax.numpy as jnp
from jax import lax
from jax.sharding import PartitionSpec as P


def shards(prompt, base_weight, factor_left, factor_right, magnitude):
    left_rows = lax.all_gather(factor_left, "col", axis=0, tiled=True)
    right_cols = lax.all_gather(factor_right, "row", axis=0, tiled=True)
    update = jnp.dot(left_rows, right_cols, preferred_element_type=jnp.float32)
    combined = base_weight.astype(jnp.float32) + update
    squares = lax.psum(jnp.sum(combined * combined, axis=0), "row")
    merged = (combined * (magnitude / jnp.sqrt(squares + 1e-06))[None, :]).astype(jnp.bfloat16)
    serving = lax.all_to_all(merged, "row", split_axis=1, concat_axis=0, tiled=True)
    product = jnp.dot(
        lax.all_gather(prompt, ("row", "col"), axis=1, tiled=True),
        serving,
        preferred_element_type=jnp.float32,
    )
    return (serving[None], product.astype(jnp.bfloat16)[None])


def solution(mesh):
    in_specs = (
        P(None, ("row", "col")),
        P("row", "col"),
        P(("row", "col"), None),
        P("row", "col"),
        P("col"),
    )
    out_specs = (P("row", None, "col"), P("row", None, "col"))
    return jax.shard_map(shards, mesh=mesh, in_specs=in_specs, out_specs=out_specs, check_vma=False)
```

profile of v0, /device:TPU:0, one launch (start us, length us, event | category | flops | bytes accessed | tf_op | source)
XLA Modules:
  0.0 451.7 jit_solution(723757664946019490)
XLA Ops:
  7.2 0.0 copy-start
  7.2 0.0 copy-start.1
  7.2 0.0 all-gather.2.cloned.1.call-start
  7.2 0.7 all-gather.2.cloned.1.call-update
  7.9 12.2 %copy.10 = bf16[2048,2048]{0,1:T(8,128)(2,1)} copy(bf16[2048,2048]{1,0:T(8,128)(2,1)} %param.6) | data formatting | bytes 16777216 | tf_op args[1]
  20.2 0.0 copy-done
  20.2 36.0 %all_gather.10 = bf16[64,2048]{1,0:T(8,128)(2,1)S(1)} all-gather(bf16[8,2048]{1,0:T(8,128)(2,1)S(1)} %copy-done), channel_id=1, replica_groups=mesh['row'=8,'col'=16] {'row'}, dimensions={0}, use_global_device_ids=true | all-gather | bytes 294912 | tf_op jit(solution)/shard_map/all_gather | solution.py:9
  56.2 0.0 copy-done.1
  56.2 19.8 %all_gather.9 = bf16[2048,64]{0,1:T(8,128)(2,1)S(1)} all-gather(bf16[128,64]{0,1:T(8,128)(2,1)S(1)} %copy-done.1), channel_id=1, replica_groups=mesh['row'=8,'col'=16] {'col'}, dimensions={0}, use_global_device_ids=true | all-gather | bytes 278528 | tf_op jit(solution)/shard_map/all_gather | solution.py:8
  75.9 0.0 copy-start.2
  75.9 9.5 %multiply_reduce_fusion = (f32[2048]{0:T(1024)S(1)}, f32[2048,2048]{0,1:T(8,128)}) fusion(bf16[2048,2048]{0,1:T(8,128)(2,1)} %copy.10, bf16[2048,64]{0,1:T(8,128)(2,1)S(1)} %all_gather.9, bf16[64,2048]{1,0:T(8,128)(2,1)S(1)} %all_gather.10), kind=kOutput, calls=%fused_computation.1 | convolution fusion | flops 553646080 | bytes 25698304 | tf_op jit(solution)/shard_map/dot_general | solution.py:10
  85.5 24.7 %psum.7 = f32[2048]{0:T(1024)S(1)} all-reduce(f32[2048]{0:T(1024)S(1)} %get-tuple-element.6), channel_id=1, replica_groups=mesh['row'=8,'col'=16] {'row'}, use_global_device_ids=true, to_apply=%region_1.0 | all-reduce | flops 2048 | bytes 16384 | tf_op jit(solution)/shard_map/psum | solution.py:12
  110.2 0.0 copy-done.2
  110.2 12.6 %multiply_convert_fusion = bf16[2048,2048]{0,1:T(8,128)(2,1)} fusion(f32[2048,2048]{0,1:T(8,128)} %get-tuple-element.7, bf16[2048,2048]{0,1:T(8,128)(2,1)} %copy.10, f32[2048]{0:T(1024)S(1)} %rsqrt_multiply_fusion), kind=kLoop, calls=%fused_computation | loop fusion | flops 16777216 | bytes 33562624 | tf_op jit(solution)/shard_map/convert_element_type | solution.py:13
  122.9 11.5 %copy.11 = bf16[2048,8,256]{2,0,1:T(8,128)(2,1)} copy(bf16[2048,8,256]{0,2,1:T(8,128)(2,1)} %bitcast.14) | data formatting | bytes 16777216 | tf_op jit(solution)/shard_map/all_to_all | solution.py:14
  134.3 118.2 %all_to_all.19 = bf16[2048,8,256]{2,0,1:T(8,128)(2,1)} all-to-all(bf16[2048,8,256]{2,0,1:T(8,128)(2,1)} %copy.11), channel_id=1, replica_groups=mesh['row'=8,'col'=16] {'row'}, dimensions={1} | all-to-all | bytes 16777216 | tf_op jit(solution)/shard_map/all_to_all | solution.py:14
  252.5 167.6 %all-gather.2.cloned.1.call-done = bf16[1024,16384]{1,0:T(8,128)(2,1)} async-done(((bf16[1024,128]{1,0:T(8,128)(2,1)}), bf16[1024,16384]{1,0:T(8,128)(2,1)}) %all-gather.2.cloned.1.call-update) | async-done | bytes 33554448 | tf_op jit(solution)/shard_map/all_gather | solution.py:16
  420.1 16.6 %fusion = bf16[1,1024,256]{1,2,0:T(8,128)(2,1)S(1)} fusion(bf16[16384,256]{1,0:T(8,128)(2,1)} %bitcast.15, bf16[1024,16384]{1,0:T(8,128)(2,1)} %all-gather.2.cloned.1.call-done), kind=kOutput, calls=%fused_computation.4 | convolution fusion | flops 8590196736 | bytes 42467328 | tf_op jit(solution)/shard_map/dot_general | solution.py:15
  436.7 1.0 copy.12
  437.7 7.1 %copy.14 = bf16[1,16384,256]{2,1,0:T(8,128)(2,1)} copy(bf16[1,16384,256]{2,1,0:T(8,128)(2,1)} %bitcast.16) | data formatting | bytes 16777216
  (1 shorter events, 0.0 us)
Async XLA Ops:
  7.2 13.0 %copy-start = (bf16[8,2048]{1,0:T(8,128)(2,1)S(1)}, bf16[8,2048]{1,0:T(8,128)(2,1)}, u32[]{:S(2)}) copy-start(bf16[8,2048]{1,0:T(8,128)(2,1)} %param.8) | copy-start | bytes 98308
  7.2 49.0 %copy-start.1 = (bf16[128,64]{0,1:T(8,128)(2,1)S(1)}, bf16[128,64]{0,1:T(8,128)(2,1)}, u32[]{:S(2)}) copy-start(bf16[128,64]{0,1:T(8,128)(2,1)} %param.7) | copy-start | bytes 49156
  7.2 412.9 %all-gather.2.cloned.1.call-start = ((), (), s32[]{:S(2)}) async-start(), calls=%async_computation.1 | async-start | bytes 33816576 | tf_op jit(solution)/shard_map/all_gather | solution.py:16
  75.9 34.3 %copy-start.2 = (f32[2048]{0:T(1024)S(1)}, f32[2048]{0:T(1024)}, u32[]{:S(2)}) copy-start(f32[2048]{0:T(1024)} %param.9) | copy-start | bytes 24580
Sparse Core Ops, SparseCore 0:
  9.7 410.3 all-gather.1
where the time goes:
time: 454 us; the launch traced here: 452 us
  blocking collectives  199 us (44%)
  waiting for transfers between devices  168 us (37%)
  local copies, waits for them, and re-layouts  31.8 us (7%)
  matrix products  26.2 us (6%)
  between operations  14.1 us (3%)
  other arithmetic  12.6 us (3%)
    all_gather x1, waiting for transfers between devices, shards(): lax.all_gather(prompt, ('row', 'col'), axis=1, tiled=True)  168 us
    all_to_all x1, blocking collectives, shards(): lax.all_to_all(merged, 'row', split_axis=1, concat_axis=0, tiled=True)  118 us
    all_gather x1, blocking collectives, shards(): right_cols = lax.all_gather(factor_right, 'row', axis=0, tiled=True)  36 us
    psum x1, blocking collectives, shards(): squares = lax.psum(jnp.sum(combined * combined, axis=0), 'row')  24.7 us
    unnamed x9, local copies, waits for them, and re-layouts  20.4 us
    all_gather x1, blocking collectives, shards(): left_rows = lax.all_gather(factor_left, 'col', axis=0, tiled=True)  19.8 us
    dot_general x1, matrix products, shards(): jnp.dot(lax.all_gather(prompt, ('row', 'col'), axis=1, tiled=True), servi...  16.6 us
    convert_element_type x1, other arithmetic, shards(): (combined * (magnitude / jnp.sqrt(squares + 1e-06))[None, :]).astype(jnp....  12.6 us
  transfers between devices with their start and end apart: 1, of which 1 were waited for; matrix products, arithmetic and copies ran while one was open for 10% of the time, Pallas kernels for 0%

commit v1 on v0

v1 whole, which is shorter than its diff:
```python
import functools

import jax
import jax.numpy as jnp
from jax import lax
from jax.experimental import pallas as pl
from jax.experimental.pallas import tpu as pltpu
from jax.sharding import PartitionSpec as P

AXES = ("row", "col")
SHIFTS = (1, -1, 2)
BLOCK = 2048
WIDE = 256
TOK = 1024
N_COL = 16
MIB = 1024 * 1024
F32 = jnp.float32
BF16 = jnp.bfloat16


def move(a, dz=0, dy=0):
    pairs = []
    for r in range(8):
        zh, y = divmod(r, 4)
        to = ((zh + dz) % 2) * 4 + (y + dy) % 4
        pairs += [(r * N_COL + c, to * N_COL + c) for c in range(N_COL)]
    return lax.ppermute(a, AXES, pairs)


def after(x, dep):
    return lax.optimization_barrier((x, dep))[0]


def params(mib, **kw):
    return pltpu.CompilerParams(vmem_limit_bytes=mib * MIB, **kw)


def join_features(p_ref, whole):
    for c in range(N_COL):
        whole[:, c * 128 : (c + 1) * 128] = p_ref[c]


def own_kernel(idx, p_ref, w_ref, o_ref, whole):
    @pl.when(pl.program_id(0) == 0)
    def _():
        join_features(p_ref, whole)

    @pl.loop(0, 4)
    def _(m):
        rows = pl.ds(pl.multiple_of(m * 256, 256), 256)
        o_ref[0, rows, :] = jnp.dot(whole[rows, :], w_ref[...], preferred_element_type=F32)


def own_product(idx, gathered, base):
    return pl.pallas_call(
        own_kernel,
        out_shape=jax.ShapeDtypeStruct((4, TOK, WIDE), F32),
        grid_spec=pltpu.PrefetchScalarGridSpec(
            num_scalar_prefetch=1,
            grid=(4,),
            in_specs=[
                pl.BlockSpec((N_COL, TOK, 128), lambda g, idx: (0, 0, 0)),
                pl.BlockSpec((BLOCK, WIDE), lambda g, idx: (0, idx[g])),
            ],
            out_specs=pl.BlockSpec((1, TOK, WIDE), lambda g, idx: (g, 0, 0)),
            scratch_shapes=[pltpu.VMEM((TOK, BLOCK), BF16)],
        ),
        compiler_params=params(40),
        cost_estimate=pl.CostEstimate(flops=2 * TOK * BLOCK * 4 * WIDE, bytes_accessed=12 * MIB, transcendentals=0),
        name="own_product",
    )(idx, gathered, base)


def low_rank_kernel(p0_ref, p1_ref, l0_ref, l1_ref, o_ref, total):
    @pl.when(pl.program_id(0) == 0)
    def _():
        total[...] = jnp.zeros_like(total)

    acc = total[...]
    for p_ref, l_ref in ((p0_ref, l0_ref), (p1_ref, l1_ref)):
        packed = l_ref[0]
        left = jnp.concatenate([packed[:, :64], packed[:, 64:]], axis=0)
        acc += jnp.dot(p_ref[0], left, preferred_element_type=F32)
    total[...] = acc

    @pl.when(pl.program_id(0) == N_COL - 1)
    def _():
        o_ref[...] = acc.astype(BF16)


def low_rank(own, par, lefts):
    return pl.pallas_call(
        low_rank_kernel,
        out_shape=jax.ShapeDtypeStruct((TOK, 64), BF16),
        grid=(N_COL,),
        in_specs=[
            pl.BlockSpec((1, TOK, 128), lambda c: (c, 0, 0)),
            pl.BlockSpec((1, TOK, 128), lambda c: (c, 0, 0)),
            pl.BlockSpec((1, 64, 128), lambda c: (c, 0, 0)),
            pl.BlockSpec((1, 64, 128), lambda c: (c, 1, 0)),
        ],
        out_specs=pl.BlockSpec((TOK, 64), lambda c: (0, 0)),
        scratch_shapes=[pltpu.VMEM((TOK, 64), F32)],
        compiler_params=params(24),
        cost_estimate=pl.CostEstimate(flops=4 * TOK * BLOCK * 64, bytes_accessed=9 * MIB, transcendentals=0),
        name="low_rank",
    )(own, par, lefts, lefts)


def pair_kernel(n, idx, p_ref, t_ref, r_ref, part_ref, *refs):
    w_refs, o_refs, whole = refs[:n], refs[n : 2 * n], refs[2 * n]

    @pl.when(pl.program_id(0) == 0)
    def _():
        join_features(p_ref, whole)

    for j in range(n):

        @pl.when(pl.program_id(0) == j)
        def _(j=j):
            @pl.loop(0, 4)
            def _(m):
                rows = pl.ds(pl.multiple_of(m * 256, 256), 256)
                acc = jnp.dot(whole[rows, :], w_refs[j][...], preferred_element_type=F32)
                acc += jnp.dot(t_ref[rows, :], r_ref[...], preferred_element_type=F32)
                o_refs[j][rows, :] = (acc + part_ref[0, rows, :]).astype(o_refs[j].dtype)


def pair_product(idx, first, gathered, t, right, part, weights, dtype):
    n = len(weights)
    return pl.pallas_call(
        functools.partial(pair_kernel, n),
        out_shape=[jax.ShapeDtypeStruct((TOK, WIDE), dtype)] * n,
        grid_spec=pltpu.PrefetchScalarGridSpec(
            num_scalar_prefetch=1,
            grid=(n,),
            in_specs=[
                pl.BlockSpec((N_COL, TOK, 128), lambda g, idx: (0, 0, 0)),
                pl.BlockSpec((TOK, 64), lambda g, idx: (0, 0)),
                pl.BlockSpec((64, WIDE), lambda g, idx: (0, idx[first + g])),
                pl.BlockSpec((1, TOK, WIDE), lambda g, idx: (first + g, 0, 0)),
            ]
            + [pl.BlockSpec((BLOCK, WIDE), lambda g, idx: (0, 0))] * n,
            out_specs=[pl.BlockSpec((TOK, WIDE), lambda g, idx: (0, 0))] * n,
            scratch_shapes=[pltpu.VMEM((TOK, BLOCK), BF16)],
        ),
        compiler_params=params(48),
        cost_estimate=pl.CostEstimate(flops=2 * TOK * BLOCK * n * WIDE, bytes_accessed=(5 + 3 * n) * MIB, transcendentals=0),
        name="pair_product",
    )(idx, gathered, t, right, part, *weights)


def merge_kernel(idx, base, *refs):
    blocks, (lefts, rr_ref, mag_ref, out, scale_ref, raw, comb, left, sems, out_sems) = refs[:7], refs[7:]
    first = pltpu.make_async_copy(lefts, left, sems.at[8])
    first.start()
    col = pl.ds(pl.multiple_of(idx[0] * WIDE, WIDE), WIDE)
    pltpu.make_async_copy(base.at[:, col], raw.at[0], sems.at[0]).start()
    for j in range(7):
        pltpu.make_async_copy(blocks[j], raw.at[j + 1], sems.at[j + 1]).start()
    first.wait()

    def part(i, squares):
        j, h = i // 2, i % 2

        @pl.when(h == 0)
        def _():
            pltpu.make_async_copy(blocks[0], raw.at[j], sems.at[j]).wait()

        factor = left[pl.ds(h * 8, 8), pl.ds(pl.multiple_of(j * 64, 64), 64), :].reshape(512, 128)
        update = jnp.dot(factor, rr_ref[...], preferred_element_type=F32)
        for c in range(8):
            for k in range(2):
                rows = pl.ds(pl.multiple_of(h * 1024 + c * 128 + k * 64, 64), 64)
                value = raw[j, rows, :].astype(F32) + update[c * 64 : (c + 1) * 64, k * WIDE : (k + 1) * WIDE]
                comb[j, rows, :] = value
                squares += (value * value).reshape(8, 8, WIDE).sum(axis=0)
        return squares

    squares = lax.fori_loop(0, 16, part, jnp.zeros((8, WIDE), F32))
    scale = mag_ref[...] / jnp.sqrt(squares.sum(axis=0, keepdims=True) + 1e-6)
    scale_ref[...] = scale

    def out_copy(j):
        rows = pl.ds(pl.multiple_of(idx[4 + j] * BLOCK, BLOCK), BLOCK)
        return pltpu.make_async_copy(raw.at[j], out.at[rows, :], out_sems.at[j])

    @pl.loop(0, 8)
    def _(j):
        @pl.loop(0, 8)
        def _(m):
            rows = pl.ds(pl.multiple_of(m * 256, 256), 256)
            raw[j, rows, :] = (comb[j, rows, :] * scale).astype(BF16)

        out_copy(j).start()

    @pl.loop(0, 8)
    def _(j):
        out_copy(j).wait()


def merge(idx, base, blocks, lefts, rr, mag):
    any_space = pl.BlockSpec(memory_space=pl.ANY)
    vmem = pl.BlockSpec(memory_space=pltpu.VMEM)
    return pl.pallas_call(
        merge_kernel,
        out_shape=[jax.ShapeDtypeStruct((8 * BLOCK, WIDE), BF16), jax.ShapeDtypeStruct((1, WIDE), F32)],
        in_specs=[pl.BlockSpec(memory_space=pltpu.SMEM)] + [any_space] * 9 + [vmem] * 2,
        out_specs=[any_space, vmem],
        scratch_shapes=[
            pltpu.VMEM((8, BLOCK, WIDE), BF16),
            pltpu.VMEM((8, BLOCK, WIDE), F32),
            pltpu.VMEM((N_COL, 512, 128), BF16),
            pltpu.SemaphoreType.DMA((9,)),
            pltpu.SemaphoreType.DMA((8,)),
        ],
        compiler_params=params(48),
        cost_estimate=pl.CostEstimate(flops=2 * 128 * 512 * 8192, bytes_accessed=18 * MIB, transcendentals=0),
        name="merge",
    )(idx, base, *blocks, lefts, rr, mag)


def shards(prompt, base, factor_left, factor_right, magnitude):
    row = lax.axis_index("row").astype(jnp.int32)
    zh, y = row // 4, row % 4

    def served_by(dz, dy):
        return ((zh + dz) % 2) * 4 + (y + dy) % 4

    def cols(dz, dy):
        return lax.dynamic_slice(base, (0, served_by(dz, dy) * WIDE), (BLOCK, WIDE))

    prompt_own = lax.all_gather(prompt, "col", axis=0, tiled=False)

    left = jnp.concatenate([factor_left[:64], factor_left[64:]], axis=1)
    right = factor_right.reshape(8, 16, 128).transpose(1, 0, 2).reshape(128, 128)
    factors = jnp.concatenate([left, right], axis=0)
    from_partner = move(jnp.concatenate([prompt, factors], axis=0), dz=1)
    prompt_par = lax.all_gather(from_partner[:TOK], "col", axis=0, tiled=False)

    straight = {}
    for d in SHIFTS:
        straight[d] = move(cols(0, d), dy=d)

    both = jnp.concatenate([factors, from_partner[TOK:]], axis=0)
    got = {}
    previous = None
    for d in SHIFTS:
        got[d] = move(both if previous is None else after(both, previous), dy=d)
        previous = got[d]
    order = (0,) + SHIFTS
    got[0] = both
    lefts = jnp.concatenate([got[d][k * 192 : k * 192 + 64] for d in order for k in range(2)], axis=0)
    lefts = lax.all_gather(lefts, "col", axis=0, tiled=False)

    rights = jnp.stack([got[d].reshape(2, 192, 128)[:, 64:] for d in (0, -1, 2, 1)])
    rights = lax.dynamic_slice_in_dim(jnp.concatenate([rights, rights], axis=0), (4 - y) % 4, 4, 0)
    rights = lax.dynamic_slice_in_dim(jnp.concatenate([rights, rights[:, :1]], axis=1), zh, 2, 1)
    rights = rights.reshape(4, 2, 16, 8, 128).transpose(1, 0, 3, 2, 4).reshape(64, 2048)

    half = {}
    chain = [from_partner]
    for d in SHIFTS + (0,):
        dep = chain[-1] if len(chain) < 2 else (previous if len(chain) == 2 else chain[-2])
        half[d] = move(after(cols(1, d), dep), dz=1)
        chain.append(half[d])
    relayed = {}
    for d in SHIFTS:
        relayed[d] = move(after(half[d], straight[d]), dy=d)

    idx = jnp.stack([served_by(0, d) for d in order])
    part = own_product(idx, prompt_own, base)
    t = low_rank(prompt_own, prompt_par, lefts)
    sends = pair_product(idx, 1, prompt_par, t, rights, part, [half[d] for d in SHIFTS], BF16)
    (mine,) = pair_product(idx, 0, prompt_par, t, rights, part, [half[0]], F32)
    sums = [move(after(s, relayed[d]), dy=d) for s, d in zip(sends, SHIFTS)]

    places = jnp.stack([((zh + k) % 2) * 4 + (y - d) % 4 for d in order for k in range(2)])
    right_mine = lax.dynamic_slice(rights, (0, row * WIDE), (64, WIDE))
    rr = jnp.pad(right_mine, ((0, 64), (0, WIDE))) + jnp.pad(right_mine, ((64, 0), (WIDE, 0)))
    mag = lax.dynamic_slice(magnitude, (row * WIDE,), (WIDE,))[None]
    blocks = [half[0]]
    for d in SHIFTS:
        blocks += [straight[d], relayed[d]]
    serving, scale = merge(jnp.concatenate([idx, places]), base, blocks, lefts, rr, mag)

    product = mine
    for s in sums:
        product = product + s.astype(F32)
    return serving[None], (product * scale).astype(BF16)[None]


def solution(mesh):
    in_specs = (
        P(None, ("row", "col")),
        P("row", "col"),
        P(("row", "col"), None),
        P("row", "col"),
        P("col"),
    )
    out_specs = (P("row", None, "col"), P("row", None, "col"))
    return jax.shard_map(shards, mesh=mesh, in_specs=in_specs, out_specs=out_specs, check_vma=False)
```

time: 454 us -> 220 us (0.48)
  blocking collectives: 199 us -> 0 us
  waiting for transfers between devices: 168 us -> 103 us
  Pallas kernels: 0 us -> 44 us
  starting transfers between devices: 0.04 us -> 33.4 us
  matrix products: 26.2 us -> 0 us
  local copies, waits for them, and re-layouts: 31.8 us -> 20.9 us
  other arithmetic: 12.6 us -> 4.4 us
    all_gather x1 -> x3, waiting for transfers between devices: 168 us -> 0.01 us  [the longest x1 0.01 us: shards(): prompt_own = lax.all_gather(prompt, 'col', axis=0, tiled=False)]
    all_to_all x1 -> x0, blocking collectives: 118 us -> none  [shards(): lax.all_to_all(merged, 'row', split_axis=1, concat_axis=0, tiled=True)]
    ppermute x0 -> x17, waiting for transfers between devices: none -> 102 us  [move(): return lax.ppermute(a, AXES, pairs)]
    all_gather x2 -> x0, blocking collectives: 55.8 us -> none  [the longest x1 36 us: shards(): right_cols = lax.all_gather(factor_right, 'row', axis=0, tiled=True)]
    pallas_call x0 -> x5, Pallas kernels: none -> 44 us  [the longest x2 17.6 us: pair_product(): pl.pallas_call(functools.partial(pair_kernel, n), out_shape=[jax.ShapeDty...]
    ppermute x0 -> x17, starting transfers between devices: none -> 33.3 us  [move(): return lax.ppermute(a, AXES, pairs)]
    dot_general x2 -> x0, matrix products: 26.2 us -> none  [the longest x1 16.6 us: shards(): jnp.dot(lax.all_gather(prompt, ('row', 'col'), axis=1, tiled=True), servi...]
    psum x1 -> x0, blocking collectives: 24.7 us -> none  [shards(): squares = lax.psum(jnp.sum(combined * combined, axis=0), 'row')]
  transfers between devices with their start and end apart: 1 -> 20, of which waited for: 1 -> 8; matrix products, arithmetic and copies ran while one was open for 10% -> 5% of each run, Pallas kernels for 0% -> 20%
where the time goes in v1:
time: 220 us; the launch traced here: 219 us
  waiting for transfers between devices  103 us (47%)
  Pallas kernels  44 us (20%)
  starting transfers between devices  33.4 us (15%)
  local copies, waits for them, and re-layouts  20.9 us (10%)
  between operations  14.1 us (6%)
  other arithmetic  4.4 us (2%)
    ppermute x17, waiting for transfers between devices, move(): return lax.ppermute(a, AXES, pairs)  102 us
    ppermute x17, starting transfers between devices, move(): return lax.ppermute(a, AXES, pairs)  33.3 us
    pallas_call x2, Pallas kernels, pair_product(): pl.pallas_call(functools.partial(pair_kernel, n), out_shape=[jax.ShapeDty...  17.6 us
    unnamed x31, local copies, waits for them, and re-layouts  12.3 us
    pallas_call x1, Pallas kernels, merge(): pl.pallas_call(merge_kernel, out_shape=[jax.ShapeDtypeStruct((8 * BLOCK,...  10.6 us
    pallas_call x1, Pallas kernels, own_product(): pl.pallas_call(own_kernel, out_shape=jax.ShapeDtypeStruct((4, TOK, WIDE),...  10.1 us
    dynamic_slice x1, local copies, waits for them, and re-layouts, cols(): return lax.dynamic_slice(base, (0, served_by(dz, dy) * WIDE), (BLOCK, WIDE))  6.07 us
    pallas_call x1, Pallas kernels, low_rank(): pl.pallas_call(low_rank_kernel, out_shape=jax.ShapeDtypeStruct((TOK, 64),...  5.73 us
  transfers between devices with their start and end apart: 20, of which 8 were waited for; matrix products, arithmetic and copies ran while one was open for 5% of the time, Pallas kernels for 20%

profile of v1, /device:TPU:0, one launch (start us, length us, event | category | flops | bytes accessed | tf_op | source)
XLA Modules:
  0.0 219.4 jit_solution(14420734482276323286)
XLA Ops:
  10.1 4.0 %collective-permute-start = (bf16[1216,128]{1,0:T(8,128)(2,1)S(1)}, bf16[1216,128]{1,0:T(8,128)(2,1)S(1)}, u32[]{:S(2)}, u32[]{:S(2)}) collective-permute-start(bf16[1216,128]{1,0:T(8,128)(2,1)S(1)} %pad_maximum_fusion), channel_id=1, source_target_pairs={{0,64},{1,65},{2,66},{3,67},{4,68},{5,69},{6,70},{7,71},{8,72},{9,... | collective-permute-start | bytes 933896 | tf_op jit(solution)/shard_map/ppermute | solution.py:27
  14.2 7.3 %collective-permute-done = bf16[1216,128]{1,0:T(8,128)(2,1)S(1)} collective-permute-done((bf16[1216,128]{1,0:T(8,128)(2,1)S(1)}, bf16[1216,128]{1,0:T(8,128)(2,1)S(1)}, u32[]{:S(2)}, u32[]{:S(2)}) %collective-permute-start) | collective-permute-done | bytes 311328 | tf_op jit(solution)/shard_map/ppermute | solution.py:27
  23.9 4.2 %collective-permute-done.1 = bf16[384,128]{1,0:T(8,128)(2,1)S(1)} collective-permute-done((bf16[384,128]{1,0:T(8,128)(2,1)S(1)}, bf16[384,128]{1,0:T(8,128)(2,1)S(1)}, u32[]{:S(2)}, u32[]{:S(2)}) %collective-permute-start.1) | collective-permute-done | bytes 98336 | tf_op jit(solution)/shard_map/ppermute | solution.py:27
  29.9 2.8 %collective-permute-done.2 = bf16[384,128]{1,0:T(8,128)(2,1)S(1)} collective-permute-done((bf16[384,128]{1,0:T(8,128)(2,1)S(1)}, bf16[384,128]{1,0:T(8,128)(2,1)S(1)}, u32[]{:S(2)}, u32[]{:S(2)}) %collective-permute-start.2) | collective-permute-done | bytes 98336 | tf_op jit(solution)/shard_map/ppermute | solution.py:27
  34.7 4.1 %collective-permute-done.3 = bf16[384,128]{1,0:T(8,128)(2,1)S(1)} collective-permute-done((bf16[384,128]{1,0:T(8,128)(2,1)S(1)}, bf16[384,128]{1,0:T(8,128)(2,1)S(1)}, u32[]{:S(2)}, u32[]{:S(2)}) %collective-permute-start.3) | collective-permute-done | bytes 98336 | tf_op jit(solution)/shard_map/ppermute | solution.py:27
  40.5 6.1 %constant_dynamic-slice_fusion.3 = (bf16[2048,256]{1,0:T(8,128)(2,1)S(1)}, bf16[2048,256]{1,0:T(8,128)(2,1)}, bf16[2048,256]{1,0:T(8,128)(2,1)}, bf16[2048,256]{...) fusion(bf16[2048,2048]{1,0:T(8,128)(2,1)} %w_ref.1, ...), kind=kLoop, calls=%fused_computation.32 | loop fusion | bytes 14680092 | tf_op jit(solution)/shard_map/dynamic_slice | solution.py:231
  46.6 3.2 %collective-permute-start.7 = (bf16[2048,256]{1,0:T(8,128)(2,1)}, bf16[2048,256]{1,0:T(8,128)(2,1)S(1)}, u32[]{:S(2)}, u32[]{:S(2)}) collective-permute-start(bf16[2048,256]{1,0:T(8,128)(2,1)} %get-tuple-element.23), channel_id=1, source_target_pairs={{0,64},{1,65},{2,66},{3,67},{4,68},{5,69},{6,70},{7,71},{8,72},{9,... | collective-permute-start | bytes 3145736 | tf_op jit(solution)/shard_map/ppermute | solution.py:27
  54.4 28.7 %collective-permute-done.7.refs_0_ = bf16[2048,256]{1,0:T(8,128)(2,1)S(1)} collective-permute-done((bf16[2048,256]{1,0:T(8,128)(2,1)}, bf16[2048,256]{1,0:T(8,128)(2,1)S(1)}, u32[]{:S(2)}, u32[]{:S(2)}) %collective-permute-start.7) | collective-permute-done | bytes 1048608 | tf_op jit(solution)/shard_map/ppermute | solution.py:27
  83.1 3.9 %collective-permute-start.12 = (bf16[2048,256]{1,0:T(8,128)(2,1)S(1)}, bf16[2048,256]{1,0:T(8,128)(2,1)}, u32[]{:S(2)}, u32[]{:S(2)}) collective-permute-start(bf16[2048,256]{1,0:T(8,128)(2,1)S(1)} %get-tuple-element.26), channel_id=1, source_target_pairs={{0,64},{1,65},{2,66},{3,67},{4,68},{5,69},{6,70},{7,71},{8,72},{9,... | collective-permute-start | bytes 3145736 | tf_op jit(solution)/shard_map/ppermute | solution.py:27
  87.0 7.9 %collective-permute-done.6.refs_1_ = bf16[2048,256]{1,0:T(8,128)(2,1)} collective-permute-done((bf16[2048,256]{1,0:T(8,128)(2,1)}, bf16[2048,256]{1,0:T(8,128)(2,1)}, u32[]{:S(2)}, u32[]{:S(2)}) %collective-permute-start.6) | collective-permute-done | bytes 1048608 | tf_op jit(solution)/shard_map/ppermute | solution.py:27
  95.9 17.1 %collective-permute-done.4.refs_1_ = bf16[2048,256]{1,0:T(8,128)(2,1)} collective-permute-done((bf16[2048,256]{1,0:T(8,128)(2,1)}, bf16[2048,256]{1,0:T(8,128)(2,1)}, u32[]{:S(2)}, u32[]{:S(2)}) %collective-permute-start.4) | collective-permute-done | bytes 1048608 | tf_op jit(solution)/shard_map/ppermute | solution.py:27
  112.9 3.0 %collective-permute-start.10 = (bf16[2048,256]{1,0:T(8,128)(2,1)}, bf16[2048,256]{1,0:T(8,128)(2,1)}, u32[]{:S(2)}, u32[]{:S(2)}) collective-permute-start(bf16[2048,256]{1,0:T(8,128)(2,1)} %collective-permute-done.4.refs_1_), channel_id=1, source_target_pairs={{0,48},{1,49},{2,50},{3,51},{4,52},{5,53},{6,54},{7,55},{8,56},{9,... | collective-permute-start | bytes 3145736 | tf_op jit(solution)/shard_map/ppermute | solution.py:27
  116.0 29.7 %collective-permute-done.12.refs_2_ = bf16[2048,256]{1,0:T(8,128)(2,1)} collective-permute-done((bf16[2048,256]{1,0:T(8,128)(2,1)S(1)}, bf16[2048,256]{1,0:T(8,128)(2,1)}, u32[]{:S(2)}, u32[]{:S(2)}) %collective-permute-start.12) | collective-permute-done | bytes 1048608 | tf_op jit(solution)/shard_map/ppermute | solution.py:27
  145.7 2.4 %collective-permute-start.13 = (bf16[2048,256]{1,0:T(8,128)(2,1)}, bf16[2048,256]{1,0:T(8,128)(2,1)}, u32[]{:S(2)}, u32[]{:S(2)}) collective-permute-start(bf16[2048,256]{1,0:T(8,128)(2,1)} %collective-permute-done.12.refs_2_), channel_id=1, source_target_pairs={{0,32},{1,33},{2,34},{3,35},{4,36},{5,37},{6,38},{7,39},{8,40},{9,... | collective-permute-start | bytes 3145736 | tf_op jit(solution)/shard_map/ppermute | solution.py:27
  148.2 2.3 %collective-permute-start.5 = (bf16[2048,256]{1,0:T(8,128)(2,1)}, bf16[2048,256]{1,0:T(8,128)(2,1)S(1)}, u32[]{:S(2)}, u32[]{:S(2)}) collective-permute-start(bf16[2048,256]{1,0:T(8,128)(2,1)} %get-tuple-element.22), channel_id=1, source_target_pairs={{0,64},{1,65},{2,66},{3,67},{4,68},{5,69},{6,70},{7,71},{8,72},{9,... | collective-permute-start | bytes 3145736 | tf_op jit(solution)/shard_map/ppermute | solution.py:27
  150.5 2.2 copy-done.3
  152.7 10.1 %own_product.1.part_ref = f32[4,1024,256]{2,1,0:T(8,128)S(1)} custom-call(s32[4]{0:T(128)S(1)} %pad_add_fusion.1.idx, bf16[16,1024,128]{2,1,0:T(8,128)(2,1)S(1)} %bitcast.61, bf16[2048,2048]{1,0:T(8,128)(2,1)} %w_ref.1), custom_call_target="tpu_custom_call" | custom-call | flops 4294967296 | bytes 12582912 | tf_op jit(solution)/shard_map/own_product/pallas_call | solution.py:55
  164.8 2.2 copy-done
  170.8 5.7 %low_rank.1.t_ref = bf16[1024,64]{1,0:T(8,128)(2,1)S(1)} custom-call(bf16[16,1024,128]{2,1,0:T(8,128)(2,1)S(1)} %bitcast.62, bf16[16,1024,128]{2,1,0:T(8,128)(2,1)S(1)} %bitcast.57, bf16[16,512,128]{2,1,0:T(8,128)(2,1)S(1)} %bitcast.59, bf16[16,512,128]{2,1,0:T(8,128)(2,1)S(1)} %bitcast.60), custom_call_target="tpu_custom_call" | custom-call | flops 536870912 | bytes 9437184 | tf_op jit(solution)/shard_map/low_rank/pallas_call | solution.py:92
  176.5 11.5 %pair_product.3 = (bf16[1024,256]{1,0:T(8,128)(2,1)S(1)}, bf16[1024,256]{1,0:T(8,128)(2,1)}, bf16[1024,256]{1,0:T(8,128)(2,1)}) custom-call(s32[4]{0:T(128)S(1)} %pad_add_fusion.1.idx, bf16[16,1024,128]{2,1,0:T(8,128)(2,1)} %bitcast.55, bf16[1024,64]{1,0:T(8,128)(2,1)S(1)} %low_rank.1.t_ref, bf16[64,2048]{1,0:T(8,128)(2,1)S(1)} %bitcast.63, ...), custom_call_target="tpu_custom_call" | custom-call | flops 3221225472 | bytes 14680064 | tf_op jit(solution)/shard_map/pair_product/pallas_call | solution.py:131
  188.8 2.9 %collective-permute-start.15 = (bf16[1024,256]{1,0:T(8,128)(2,1)}, bf16[1024,256]{1,0:T(8,128)(2,1)}, u32[]{:S(2)}, u32[]{:S(2)}) collective-permute-start(bf16[1024,256]{1,0:T(8,128)(2,1)} %get-tuple-element.32), channel_id=1, source_target_pairs={{0,48},{1,49},{2,50},{3,51},{4,52},{5,53},{6,54},{7,55},{8,56},{9,... | collective-permute-start | bytes 1572872 | tf_op jit(solution)/shard_map/ppermute | solution.py:27
  193.9 10.6 %merge.1 = (bf16[16384,256]{1,0:T(8,128)(2,1)}, f32[1,256]{1,0:T(1,128)S(1)}) custom-call(s32[12]{0:T(128)S(1)} %concatenate.26.idx, bf16[2048,2048]{1,0:T(8,128)(2,1)} %w_ref.1, bf16[2048,256]{1,0:T(8,128)(2,1)S(1)} %collective-permute-done.5.refs_0_, bf16[2048,256]{1,0:T(8,128)(2,1)} %collective-permute-done.6.refs_1_, ...), custom_call_target="tpu_custom_call" | custom-call | flops 1073741824 | bytes 18874368 | tf_op jit(solution)/shard_map/merge/pallas_call | solution.py:205
  204.5 6.1 %pair_product.2 = f32[1024,256]{1,0:T(8,128)S(1)} custom-call(s32[4]{0:T(128)S(1)} %pad_add_fusion.1.idx, bf16[16,1024,128]{2,1,0:T(8,128)(2,1)} %bitcast.56, bf16[1024,64]{1,0:T(8,128)(2,1)S(1)} %low_rank.1.t_ref, bf16[64,2048]{1,0:T(8,128)(2,1)S(1)} %bitcast.65, f32[4,1024,256]{2,1,0:T(8,128)} %copy-done.1, ...), custom_call_target="tpu_custom_call" | custom-call | flops 1073741824 | bytes 8388608 | tf_op jit(solution)/shard_map/pair_product/pallas_call | solution.py:131
  210.6 2.3 %fusion = bf16[1,1024,256]{2,1,0:T(8,128)(2,1)} fusion(bf16[1024,256]{1,0:T(8,128)(2,1)} %collective-permute-done.16, bf16[1024,256]{1,0:T(8,128)(2,1)} %collective-permute-done.15, f32[1024,256]{1,0:T(8,128)S(1)} %pair_product.2, bf16[1024,256]{1,0:T(8,128)(2,1)S(1)} %collective-permute-done.14, f32[256]{0:T(256)S(1)} %bitcast.67), kind=kLoop, calls=%fused_computation.1 | loop fusion | flops 2097152 | bytes 3146752 | tf_op jit(solution)/shard_map/broadcast_in_dim | solution.py:290
  (74 shorter events, 25.0 us)
Async XLA Ops:
  7.2 143.4 %all-gather.11.cloned.1.call-start = ((), (), s32[]{:S(2)}) async-start(), calls=%async_computation.2 | async-start | bytes 4456448 | tf_op jit(solution)/shard_map/all_gather | solution.py:233
  7.9 156.9 %all-gather.7.cloned.1.call-start = ((), (), s32[]{:S(2)}) async-start(), calls=%async_computation | async-start | bytes 2228224 | tf_op jit(solution)/shard_map/all_gather | solution.py:254
  10.1 11.4 %collective-permute-start = (bf16[1216,128]{1,0:T(8,128)(2,1)S(1)}, bf16[1216,128]{1,0:T(8,128)(2,1)S(1)}, u32[]{:S(2)}, u32[]{:S(2)}) collective-permute-start(bf16[1216,128]{1,0:T(8,128)(2,1)S(1)} %pad_maximum_fusion), channel_id=1, source_target_pairs={{0,64},{1,65},{2,66},{3,67},{4,68},{5,69},{6,70},{7,71},{8,72},{9,... | collective-permute-start | bytes 933896 | tf_op jit(solution)/shard_map/ppermute | solution.py:27
  22.3 5.8 %collective-permute-start.1 = (bf16[384,128]{1,0:T(8,128)(2,1)S(1)}, bf16[384,128]{1,0:T(8,128)(2,1)S(1)}, u32[]{:S(2)}, u32[]{:S(2)}) collective-permute-start(bf16[384,128]{1,0:T(8,128)(2,1)S(1)} %pad_maximum_fusion.1), channel_id=1, source_target_pairs={{0,16},{1,17},{2,18},{3,19},{4,20},{5,21},{6,22},{7,23},{8,24},{9,... | collective-permute-start | bytes 294920 | tf_op jit(solution)/shard_map/ppermute | solution.py:27
  28.1 4.6 %collective-permute-start.2 = (bf16[384,128]{1,0:T(8,128)(2,1)S(1)}, bf16[384,128]{1,0:T(8,128)(2,1)S(1)}, u32[]{:S(2)}, u32[]{:S(2)}) collective-permute-start(bf16[384,128]{1,0:T(8,128)(2,1)S(1)} %pad_maximum_fusion.1), channel_id=1, source_target_pairs={{0,48},{1,49},{2,50},{3,51},{4,52},{5,53},{6,54},{7,55},{8,56},{9,... | collective-permute-start | bytes 294920 | tf_op jit(solution)/shard_map/ppermute | solution.py:27
  32.7 6.1 %collective-permute-start.3 = (bf16[384,128]{1,0:T(8,128)(2,1)S(1)}, bf16[384,128]{1,0:T(8,128)(2,1)S(1)}, u32[]{:S(2)}, u32[]{:S(2)}) collective-permute-start(bf16[384,128]{1,0:T(8,128)(2,1)S(1)} %pad_maximum_fusion.1), channel_id=1, source_target_pairs={{0,32},{1,33},{2,34},{3,35},{4,36},{5,37},{6,38},{7,39},{8,40},{9,... | collective-permute-start | bytes 294920 | tf_op jit(solution)/shard_map/ppermute | solution.py:27
  39.6 125.3 %all-gather.9.cloned.1.call-start = ((), (), s32[]{:S(2)}) async-start(), calls=%async_computation.1 | async-start | bytes 4456448 | tf_op jit(solution)/shard_map/all_gather | solution.py:239
  46.6 36.5 %collective-permute-start.7 = (bf16[2048,256]{1,0:T(8,128)(2,1)}, bf16[2048,256]{1,0:T(8,128)(2,1)S(1)}, u32[]{:S(2)}, u32[]{:S(2)}) collective-permute-start(bf16[2048,256]{1,0:T(8,128)(2,1)} %get-tuple-element.23), channel_id=1, source_target_pairs={{0,64},{1,65},{2,66},{3,67},{4,68},{5,69},{6,70},{7,71},{8,72},{9,... | collective-permute-start | bytes 3145736 | tf_op jit(solution)/shard_map/ppermute | solution.py:27
  49.8 66.2 %collective-permute-start.11 = (bf16[2048,256]{1,0:T(8,128)(2,1)}, bf16[2048,256]{1,0:T(8,128)(2,1)}, u32[]{:S(2)}, u32[]{:S(2)}) collective-permute-start(bf16[2048,256]{1,0:T(8,128)(2,1)} %get-tuple-element.37), channel_id=1, source_target_pairs={{0,32},{1,33},{2,34},{3,35},{4,36},{5,37},{6,38},{7,39},{8,40},{9,... | collective-permute-start | bytes 3145736 | tf_op jit(solution)/shard_map/ppermute | solution.py:27
  51.8 44.0 %collective-permute-start.9 = (bf16[2048,256]{1,0:T(8,128)(2,1)}, bf16[2048,256]{1,0:T(8,128)(2,1)S(1)}, u32[]{:S(2)}, u32[]{:S(2)}) collective-permute-start(bf16[2048,256]{1,0:T(8,128)(2,1)} %get-tuple-element.38), channel_id=1, source_target_pairs={{0,48},{1,49},{2,50},{3,51},{4,52},{5,53},{6,54},{7,55},{8,56},{9,... | collective-permute-start | bytes 3145736 | tf_op jit(solution)/shard_map/ppermute | solution.py:27
  52.9 42.0 %collective-permute-start.6 = (bf16[2048,256]{1,0:T(8,128)(2,1)}, bf16[2048,256]{1,0:T(8,128)(2,1)}, u32[]{:S(2)}, u32[]{:S(2)}) collective-permute-start(bf16[2048,256]{1,0:T(8,128)(2,1)} %get-tuple-element.40), channel_id=1, source_target_pairs={{0,16},{1,17},{2,18},{3,19},{4,20},{5,21},{6,22},{7,23},{8,24},{9,... | collective-permute-start | bytes 3145736 | tf_op jit(solution)/shard_map/ppermute | solution.py:27
  54.0 59.0 %collective-permute-start.4 = (bf16[2048,256]{1,0:T(8,128)(2,1)}, bf16[2048,256]{1,0:T(8,128)(2,1)}, u32[]{:S(2)}, u32[]{:S(2)}) collective-permute-start(bf16[2048,256]{1,0:T(8,128)(2,1)} %get-tuple-element.21), channel_id=1, source_target_pairs={{0,64},{1,65},{2,66},{3,67},{4,68},{5,69},{6,70},{7,71},{8,72},{9,... | collective-permute-start | bytes 3145736 | tf_op jit(solution)/shard_map/ppermute | solution.py:27
  83.1 62.6 %collective-permute-start.12 = (bf16[2048,256]{1,0:T(8,128)(2,1)S(1)}, bf16[2048,256]{1,0:T(8,128)(2,1)}, u32[]{:S(2)}, u32[]{:S(2)}) collective-permute-start(bf16[2048,256]{1,0:T(8,128)(2,1)S(1)} %get-tuple-element.26), channel_id=1, source_target_pairs={{0,64},{1,65},{2,66},{3,67},{4,68},{5,69},{6,70},{7,71},{8,72},{9,... | collective-permute-start | bytes 3145736 | tf_op jit(solution)/shard_map/ppermute | solution.py:27
  94.9 96.8 %collective-permute-start.8 = (bf16[2048,256]{1,0:T(8,128)(2,1)S(1)}, bf16[2048,256]{1,0:T(8,128)(2,1)}, u32[]{:S(2)}, u32[]{:S(2)}) collective-permute-start(bf16[2048,256]{1,0:T(8,128)(2,1)S(1)} %collective-permute-done.7.refs_0_), channel_id=1, source_target_pairs={{0,16},{1,17},{2,18},{3,19},{4,20},{5,21},{6,22},{7,23},{8,24},{9,... | collective-permute-start | bytes 3145736 | tf_op jit(solution)/shard_map/ppermute | solution.py:27
  95.9 52.4 %copy-start.5 = (bf16[2048,256]{1,0:T(8,128)(2,1)}, bf16[2048,256]{1,0:T(8,128)(2,1)S(1)}, u32[]{:S(2)}) copy-start(bf16[2048,256]{1,0:T(8,128)(2,1)S(1)} %collective-permute-done.9.refs_3_) | copy-start | bytes 3145732
  112.9 75.9 %collective-permute-start.10 = (bf16[2048,256]{1,0:T(8,128)(2,1)}, bf16[2048,256]{1,0:T(8,128)(2,1)}, u32[]{:S(2)}, u32[]{:S(2)}) collective-permute-start(bf16[2048,256]{1,0:T(8,128)(2,1)} %collective-permute-done.4.refs_1_), channel_id=1, source_target_pairs={{0,48},{1,49},{2,50},{3,51},{4,52},{5,53},{6,54},{7,55},{8,56},{9,... | collective-permute-start | bytes 3145736 | tf_op jit(solution)/shard_map/ppermute | solution.py:27
  145.7 42.3 %collective-permute-start.13 = (bf16[2048,256]{1,0:T(8,128)(2,1)}, bf16[2048,256]{1,0:T(8,128)(2,1)}, u32[]{:S(2)}, u32[]{:S(2)}) collective-permute-start(bf16[2048,256]{1,0:T(8,128)(2,1)} %collective-permute-done.12.refs_2_), channel_id=1, source_target_pairs={{0,32},{1,33},{2,34},{3,35},{4,36},{5,37},{6,38},{7,39},{8,40},{9,... | collective-permute-start | bytes 3145736 | tf_op jit(solution)/shard_map/ppermute | solution.py:27
  148.2 44.4 %collective-permute-start.5 = (bf16[2048,256]{1,0:T(8,128)(2,1)}, bf16[2048,256]{1,0:T(8,128)(2,1)S(1)}, u32[]{:S(2)}, u32[]{:S(2)}) collective-permute-start(bf16[2048,256]{1,0:T(8,128)(2,1)} %get-tuple-element.22), channel_id=1, source_target_pairs={{0,64},{1,65},{2,66},{3,67},{4,68},{5,69},{6,70},{7,71},{8,72},{9,... | collective-permute-start | bytes 3145736 | tf_op jit(solution)/shard_map/ppermute | solution.py:27
  150.5 2.2 copy-start.3
  164.8 2.2 copy-start
  168.6 2.2 copy-start.4
  188.0 22.6 %collective-permute-start.16 = (bf16[1024,256]{1,0:T(8,128)(2,1)}, bf16[1024,256]{1,0:T(8,128)(2,1)}, u32[]{:S(2)}, u32[]{:S(2)}) collective-permute-start(bf16[1024,256]{1,0:T(8,128)(2,1)} %get-tuple-element.34), channel_id=1, source_target_pairs={{0,32},{1,33},{2,34},{3,35},{4,36},{5,37},{6,38},{7,39},{8,40},{9,... | collective-permute-start | bytes 1572872 | tf_op jit(solution)/shard_map/ppermute | solution.py:27
  188.8 21.8 %collective-permute-start.15 = (bf16[1024,256]{1,0:T(8,128)(2,1)}, bf16[1024,256]{1,0:T(8,128)(2,1)}, u32[]{:S(2)}, u32[]{:S(2)}) collective-permute-start(bf16[1024,256]{1,0:T(8,128)(2,1)} %get-tuple-element.32), channel_id=1, source_target_pairs={{0,48},{1,49},{2,50},{3,51},{4,52},{5,53},{6,54},{7,55},{8,56},{9,... | collective-permute-start | bytes 1572872 | tf_op jit(solution)/shard_map/ppermute | solution.py:27
  191.7 18.9 %collective-permute-start.14 = (bf16[1024,256]{1,0:T(8,128)(2,1)S(1)}, bf16[1024,256]{1,0:T(8,128)(2,1)S(1)}, u32[]{:S(2)}, u32[]{:S(2)}) collective-permute-start(bf16[1024,256]{1,0:T(8,128)(2,1)S(1)} %get-tuple-element.30), channel_id=1, source_target_pairs={{0,16},{1,17},{2,18},{3,19},{4,20},{5,21},{6,22},{7,23},{8,24},{9,... | collective-permute-start | bytes 1572872 | tf_op jit(solution)/shard_map/ppermute | solution.py:27
  (4 other events, 5.5 us)
Sparse Core Ops, SparseCore 0:
  9.7 39.9 all-gather.10
  51.4 36.0 all-gather.6
  89.8 51.9 all-gather.8

commit v2 on v0

v2 whole, which is shorter than its diff:
```python
import functools

import jax
import jax.numpy as jnp
from jax import lax
from jax.experimental import pallas as pl
from jax.experimental.pallas import tpu as pltpu
from jax.sharding import PartitionSpec as P

AXES = ("row", "col")
SHIFTS = (1, -1, 2)
BLOCK = 2048
WIDE = 256
TOK = 1024
N_COL = 16
MIB = 1024 * 1024
F32 = jnp.float32
BF16 = jnp.bfloat16


def move(a, dz=0, dy=0):
    pairs = []
    for r in range(8):
        zh, y = divmod(r, 4)
        to = ((zh + dz) % 2) * 4 + (y + dy) % 4
        pairs += [(r * N_COL + c, to * N_COL + c) for c in range(N_COL)]
    return lax.ppermute(a, AXES, pairs)


def swap(a, bits):
    return lax.ppermute(a, AXES, [(i, i ^ bits) for i in range(128)])


def gather_x(a):
    groups = [[16 * r + 4 * x + k for x in range(4)] for r in range(8) for k in range(4)]
    return lax.all_gather(a, AXES, axis=0, tiled=False, axis_index_groups=groups)


def after(x, *deps):
    return lax.optimization_barrier((x, *deps))[0]


def params(mib, **kw):
    return pltpu.CompilerParams(vmem_limit_bytes=mib * MIB, **kw)


PART = TOK + 64
PLACE = dict(served=0, rows=4, zl=12, core=13)


def block_copies(idx, mine, other, whole, left, sem, left_sem):
    prompts, lefts = [], []
    for x in range(4):
        for h in range(2):
            for src, k in ((mine, idx[PLACE["core"]]), (other, 1 - idx[PLACE["core"]])):
                zl = idx[PLACE["zl"]] if h == 0 else 1 - idx[PLACE["zl"]]
                c = x * 4 + zl * 2 + k
                lanes = pl.ds(pl.multiple_of(c * 128, 128), 128)
                prompts.append(pltpu.make_async_copy(src.at[x, pl.ds(h * PART, TOK), :], whole.at[:, lanes], sem))
                if left is not None:
                    lefts.append(pltpu.make_async_copy(src.at[x, pl.ds(h * PART + TOK, 64), :], left.at[c], left_sem))
    return prompts, lefts


EXTRA = 96


def pack_kernel(n, idx, base, *refs):
    factors, outs, (stage, sems) = refs[:-n - 2], refs[-n - 2 : -2], refs[-2:]
    reads, writes = [], []
    for j in range(n):
        at = pl.ds(pl.multiple_of(idx[j] * WIDE, WIDE), WIDE)
        for h in range(2):
            rows = pl.ds(h * 1024, 1024)
            reads.append([pltpu.make_async_copy(base.at[rows, at], stage.at[j, rows, :], sems.at[0, j, h])])
            writes.append(pltpu.make_async_copy(stage.at[j, rows, :], outs[j].at[rows, :], sems.at[1, j, h]))
        if factors:
            rows = pl.ds(BLOCK, EXTRA)
            reads.append(
                [
                    pltpu.make_async_copy(
                        factors[0].at[pl.ds(h * EXTRA, EXTRA), :], stage.at[j, rows, pl.ds(h * 128, 128)], sems.at[0, j, 2]
                    )
                    for h in range(2)
                ]
            )
            writes.append(pltpu.make_async_copy(stage.at[j, rows, :], outs[j].at[rows, :], sems.at[1, j, 2]))
    for group in reads:
        for c in group:
            c.start()
    for group, w in zip(reads, writes):
        wait_all(group)
        w.start()
    wait_all(writes)


def pack(places, base, *factors):
    n, rows = len(places), BLOCK + (EXTRA if factors else 0)
    return pl.pallas_call(
        functools.partial(pack_kernel, n),
        out_shape=[jax.ShapeDtypeStruct((rows, WIDE), BF16)] * n,
        in_specs=specs("sh" + "h" * len(factors)),
        out_specs=specs("h" * n),
        scratch_shapes=[pltpu.VMEM((n, rows, WIDE), BF16), pltpu.SemaphoreType.DMA((2, n, 3))],
        compiler_params=params(56),
        cost_estimate=pl.CostEstimate(flops=0, bytes_accessed=2 * n * MIB, transcendentals=0),
        name="pack",
    )(jnp.stack(places), base, *factors)


def wait_all(copies):
    for c in copies:
        c.wait()


def specs(kinds):
    space = dict(h=pltpu.HBM, s=pltpu.SMEM, v=pltpu.VMEM)
    return [pl.BlockSpec(memory_space=space[k]) for k in kinds]


def dot(a, b):
    return jnp.dot(a, b, preferred_element_type=F32)


def unpacked(ref):
    value = ref[...]
    return jnp.concatenate([value[:, :, :64], value[:, :, 64:]], axis=1).reshape(BLOCK, 64)


def own_kernel(idx, mine, other, base, acc, t_ref, own, w, left, sems):
    prompts, lefts = block_copies(idx, mine, other, own, left, sems.at[4], sems.at[5])
    cols = []
    for j in range(4):
        at = pl.ds(pl.multiple_of(idx[j] * WIDE, WIDE), WIDE)
        cols.append(pltpu.make_async_copy(base.at[:, at], w.at[j], sems.at[j]))
    for c in lefts + prompts + cols:
        c.start()
    wait_all(lefts)
    factor = unpacked(left)
    wait_all(prompts)
    t_ref[...] = dot(own[...], factor)
    for j in range(4):
        cols[j].wait()
        acc[j] = dot(own[...], w[j])


def own_part(idx, mine, other, base):
    return pl.pallas_call(
        own_kernel,
        out_shape=[jax.ShapeDtypeStruct((4, TOK, WIDE), F32), jax.ShapeDtypeStruct((TOK, 64), F32)],
        in_specs=specs("shhh"),
        out_specs=specs("vv"),
        scratch_shapes=[
            pltpu.VMEM((TOK, BLOCK), BF16),
            pltpu.VMEM((4, BLOCK, WIDE), BF16),
            pltpu.VMEM((N_COL, 64, 128), BF16),
            pltpu.SemaphoreType.DMA((6,)),
        ],
        compiler_params=params(56),
        cost_estimate=pl.CostEstimate(flops=2 * TOK * BLOCK * 5 * WIDE, bytes_accessed=13 * MIB, transcendentals=0),
        name="own_part",
    )(idx, mine, other, base)


def partner_kernel(idx, mine, other, h1, h2, h3, r_ref, own_t, acc, o1, o2, o3, t_ref, par, w, part, left, sems):
    prompts, lefts = block_copies(idx, mine, other, par, left, sems.at[6], sems.at[7])
    halves = [pltpu.make_async_copy(h, w.at[i], sems.at[i]) for i, h in enumerate((h1, h2, h3))]
    parts = [pltpu.make_async_copy(acc.at[i + 1], part.at[i], sems.at[3 + i]) for i in range(3)]
    for c in lefts + prompts:
        c.start()
    for h, p in zip(halves, parts):
        h.start()
        p.start()
    wait_all(lefts)
    factor = unpacked(left)
    wait_all(prompts)
    t = (own_t[...] + dot(par[...], factor)).astype(BF16)
    t_ref[...] = t
    for i, o in enumerate((o1, o2, o3)):
        right = r_ref[:, pl.ds(pl.multiple_of(idx[1 + i] * WIDE, WIDE), WIDE)]
        halves[i].wait()
        parts[i].wait()
        o[...] = (dot(par[...], w[i]) + dot(t, right) + part[i]).astype(BF16)


def partner_part(idx, mine, other, halves, rights, own_t, acc):
    send = jax.ShapeDtypeStruct((TOK, WIDE), BF16)
    return pl.pallas_call(
        partner_kernel,
        out_shape=[send, send, send, jax.ShapeDtypeStruct((TOK, 64), BF16)],
        in_specs=specs("shhhhhvvh"),
        out_specs=specs("vvvv"),
        scratch_shapes=[
            pltpu.VMEM((TOK, BLOCK), BF16),
            pltpu.VMEM((3, BLOCK, WIDE), BF16),
            pltpu.VMEM((3, TOK, WIDE), F32),
            pltpu.VMEM((N_COL, 64, 128), BF16),
            pltpu.SemaphoreType.DMA((8,)),
        ],
        compiler_params=params(56),
        cost_estimate=pl.CostEstimate(flops=2 * TOK * BLOCK * 4 * WIDE, bytes_accessed=12 * MIB, transcendentals=0),
        name="partner_part",
    )(idx, mine, other, *halves, rights, own_t, acc)


def last_kernel(idx, mine, other, half, t_ref, r_ref, acc, o, par, w, part, sems):
    copies, _ = block_copies(idx, mine, other, par, None, sems.at[0], None)
    copies.append(pltpu.make_async_copy(half, w, sems.at[1]))
    copies.append(pltpu.make_async_copy(acc.at[0], part, sems.at[2]))
    for c in copies:
        c.start()
    wait_all(copies)
    right = r_ref[:, pl.ds(pl.multiple_of(idx[0] * WIDE, WIDE), WIDE)]
    o[...] = dot(par[...], w[...]) + dot(t_ref[...], right) + part[...]


def last_part(idx, mine, other, half, t, rights, acc):
    return pl.pallas_call(
        last_kernel,
        out_shape=jax.ShapeDtypeStruct((TOK, WIDE), F32),
        in_specs=specs("shhhvvh"),
        out_specs=specs("v")[0],
        scratch_shapes=[
            pltpu.VMEM((TOK, BLOCK), BF16),
            pltpu.VMEM((BLOCK, WIDE), BF16),
            pltpu.VMEM((TOK, WIDE), F32),
            pltpu.SemaphoreType.DMA((3,)),
        ],
        compiler_params=params(56),
        cost_estimate=pl.CostEstimate(flops=2 * TOK * BLOCK * WIDE, bytes_accessed=7 * MIB, transcendentals=0),
        name="last_part",
    )(idx, mine, other, half, t, rights, acc)


def merge_kernel(idx, base, *refs):
    blocks, (lefts, rr_ref, mag_ref, out, scale_ref, raw, comb, left, sems, out_sems) = refs[:7], refs[7:]
    first = [pltpu.make_async_copy(lefts, left, sems.at[8])]
    for c in first:
        c.start()
    col = pl.ds(pl.multiple_of(idx[0] * WIDE, WIDE), WIDE)
    pltpu.make_async_copy(base.at[:, col], raw.at[0], sems.at[0]).start()
    for j in range(7):
        pltpu.make_async_copy(blocks[j].at[pl.ds(0, BLOCK), :], raw.at[j + 1], sems.at[j + 1]).start()
    wait_all(first)

    def part(i, squares):
        j, h = i // 2, i % 2

        @pl.when(h == 0)
        def _():
            pltpu.make_async_copy(blocks[0], raw.at[j], sems.at[j]).wait()

        factor = left[pl.ds(h * 8, 8), pl.ds(pl.multiple_of(j * 64, 64), 64), :].reshape(512, 128)
        update = jnp.dot(factor, rr_ref[...], preferred_element_type=F32)
        for c in range(8):
            for k in range(2):
                rows = pl.ds(pl.multiple_of(h * 1024 + c * 128 + k * 64, 64), 64)
                value = raw[j, rows, :].astype(F32) + update[c * 64 : (c + 1) * 64, k * WIDE : (k + 1) * WIDE]
                comb[j, rows, :] = value
                squares += (value * value).reshape(8, 8, WIDE).sum(axis=0)
        return squares

    squares = lax.fori_loop(0, 16, part, jnp.zeros((8, WIDE), F32))
    scale = mag_ref[...] / jnp.sqrt(squares.sum(axis=0, keepdims=True) + 1e-6)
    scale_ref[...] = scale

    def out_copy(j):
        rows = pl.ds(pl.multiple_of(idx[PLACE["rows"] + j] * BLOCK, BLOCK), BLOCK)
        return pltpu.make_async_copy(raw.at[j], out.at[rows, :], out_sems.at[j])

    @pl.loop(0, 8)
    def _(j):
        @pl.loop(0, 8)
        def _(m):
            rows = pl.ds(pl.multiple_of(m * 256, 256), 256)
            raw[j, rows, :] = (comb[j, rows, :] * scale).astype(BF16)

        out_copy(j).start()

    @pl.loop(0, 8)
    def _(j):
        out_copy(j).wait()


def merge(idx, base, blocks, lefts, rr, mag):
    any_space = pl.BlockSpec(memory_space=pltpu.HBM)
    vmem = pl.BlockSpec(memory_space=pltpu.VMEM)
    return pl.pallas_call(
        merge_kernel,
        out_shape=[jax.ShapeDtypeStruct((8 * BLOCK, WIDE), BF16), jax.ShapeDtypeStruct((1, WIDE), F32)],
        in_specs=[pl.BlockSpec(memory_space=pltpu.SMEM)] + [any_space] * 9 + [vmem] * 2,
        out_specs=[any_space, vmem],
        scratch_shapes=[
            pltpu.VMEM((8, BLOCK, WIDE), BF16),
            pltpu.VMEM((8, BLOCK, WIDE), F32),
            pltpu.VMEM((N_COL, 512, 128), BF16),
            pltpu.SemaphoreType.DMA((9,)),
            pltpu.SemaphoreType.DMA((8,)),
        ],
        compiler_params=params(56),
        cost_estimate=pl.CostEstimate(flops=2 * 128 * 512 * 8192, bytes_accessed=18 * MIB, transcendentals=0),
        name="merge",
    )(idx, base, *blocks, lefts, rr, mag)


def shards(prompt, base, factor_left, factor_right, magnitude):
    row = lax.axis_index("row").astype(jnp.int32)
    zh, y = row // 4, row % 4
    order = (0,) + SHIFTS

    def served_by(dz, dy):
        return ((zh + dz) % 2) * 4 + (y + dy) % 4

    left = jnp.concatenate([factor_left[:64], factor_left[64:]], axis=1)
    right = factor_right.reshape(8, 16, 128).transpose(1, 0, 2).reshape(128, 128)
    factors = jnp.concatenate([left, right], axis=0)
    small = jnp.concatenate([prompt, left], axis=0)

    partner, beside, beside_partner = swap(small, 64), swap(small, 2), swap(small, 66)
    half, straight, relayed = {}, {}, {}
    packed = dict(zip(SHIFTS, pack([served_by(0, d) for d in SHIFTS], base, factors)))
    packed_half = dict(zip(SHIFTS + (0,), pack([served_by(1, d) for d in SHIFTS + (0,)], base)))

    wave = (partner, beside, beside_partner, packed[2], packed_half[2])
    beside, partner, *_ = wave_end = lax.optimization_barrier((beside, partner, beside_partner, packed[2], packed_half[2]))
    mine = gather_x(jnp.concatenate([small, beside], axis=0))
    mine_partner = gather_x(jnp.concatenate([partner, wave_end[2]], axis=0))
    for d in SHIFTS:
        straight[d] = move(after(packed[d], *wave), dy=d)
    for d in (1, -1):
        half[d] = move(after(packed_half[d], *wave), dz=1)

    wave = (half[1], half[-1], *(straight[d] for d in SHIFTS))
    for d in (1, -1):
        relayed[d] = move(after(half[d], *wave), dy=d)
    half[2] = move(after(packed_half[2], *wave), dz=1)
    got = [factors]
    for d in SHIFTS:
        below = straight[d][BLOCK:]
        got.append(jnp.concatenate([below[:, :128], below[:, 128:]], axis=0))
    got = jnp.stack(got)
    got = jnp.stack([got, move(after(got, *wave), dz=1)], axis=1)
    places = [((zh + k) % 2) * 4 + (y - d) % 4 for d in order for k in range(2)]
    at_col = lax.axis_index("col").astype(jnp.int32)
    idx = jnp.stack([served_by(0, d) for d in order] + places + [at_col // 2 % 2, at_col % 2])
    other = swap(after(mine, *wave), 1)
    acc, own_t = own_part(idx, mine, other, base)

    wave = (half[2], relayed[1], relayed[-1], got, own_t)
    relayed[2] = move(after(half[2], *wave), dy=2)
    half[0] = move(after(packed_half[0], *wave), dz=1)
    other_partner = swap(after(mine_partner, *wave), 1)
    lefts = lax.all_gather(got[:, :, :64].reshape(512, 128), "col", axis=0, tiled=False)

    rights = jnp.stack([got[j, :, 64:] for j in (0, 2, 3, 1)])
    rights = lax.dynamic_slice_in_dim(jnp.concatenate([rights, rights], axis=0), (4 - y) % 4, 4, 0)
    rights = lax.dynamic_slice_in_dim(jnp.concatenate([rights, rights[:, :1]], axis=1), zh, 2, 1)
    rights = rights.reshape(4, 2, 16, 8, 128).transpose(1, 0, 3, 2, 4).reshape(64, 2048)

    *sends, t = partner_part(idx, mine_partner, other_partner, [half[d] for d in SHIFTS], rights, own_t, acc)
    sums = [move(s, dy=d) for s, d in zip(sends, SHIFTS)]

    right_mine = lax.dynamic_slice(rights, (0, row * WIDE), (64, WIDE))
    rr = jnp.pad(right_mine, ((0, 64), (0, WIDE))) + jnp.pad(right_mine, ((64, 0), (WIDE, 0)))
    mag = lax.dynamic_slice(magnitude, (row * WIDE,), (WIDE,))[None]
    blocks = [half[0]]
    for d in SHIFTS:
        blocks += [straight[d], relayed[d]]
    serving, scale = merge(idx, base, blocks, lefts, rr, mag)

    product = last_part(idx, mine_partner, other_partner, half[0], t, rights, acc)
    for s in sums:
        product = product + s.astype(F32)
    return serving[None], (product * scale).astype(BF16)[None]


def solution(mesh):
    in_specs = (
        P(None, ("row", "col")),
        P("row", "col"),
        P(("row", "col"), None),
        P("row", "col"),
        P("col"),
    )
    out_specs = (P("row", None, "col"), P("row", None, "col"))
    return jax.shard_map(shards, mesh=mesh, in_specs=in_specs, out_specs=out_specs, check_vma=False)
```

time: 454 us -> 183 us (0.40)
  blocking collectives: 199 us -> 0 us
  waiting for transfers between devices: 168 us -> 63.4 us
  Pallas kernels: 0 us -> 56.6 us
  starting transfers between devices: 0.04 us -> 30.2 us
  matrix products: 26.2 us -> 0 us
  local copies, waits for them, and re-layouts: 31.8 us -> 7.44 us
    all_gather x1 -> x3, waiting for transfers between devices: 168 us -> 0.02 us  [the longest x2 0.02 us: gather_x(): lax.all_gather(a, AXES, axis=0, tiled=False, axis_index_groups=groups)]
    all_to_all x1 -> x0, blocking collectives: 118 us -> none  [shards(): lax.all_to_all(merged, 'row', split_axis=1, concat_axis=0, tiled=True)]
    ppermute x0 -> x19, waiting for transfers between devices: none -> 63.4 us  [the longest x14 62 us: move(): return lax.ppermute(a, AXES, pairs)]
    pallas_call x0 -> x6, Pallas kernels: none -> 56.6 us  [the longest x1 15.5 us: own_part(): pl.pallas_call(own_kernel, out_shape=[jax.ShapeDtypeStruct((4, TOK, WIDE)...]
    all_gather x2 -> x0, blocking collectives: 55.8 us -> none  [the longest x1 36 us: shards(): right_cols = lax.all_gather(factor_right, 'row', axis=0, tiled=True)]
    ppermute x0 -> x19, starting transfers between devices: none -> 30 us  [the longest x14 24.9 us: move(): return lax.ppermute(a, AXES, pairs)]
    dot_general x2 -> x0, matrix products: 26.2 us -> none  [the longest x1 16.6 us: shards(): jnp.dot(lax.all_gather(prompt, ('row', 'col'), axis=1, tiled=True), servi...]
    psum x1 -> x0, blocking collectives: 24.7 us -> none  [shards(): squares = lax.psum(jnp.sum(combined * combined, axis=0), 'row')]
  transfers between devices with their start and end apart: 1 -> 22, of which waited for: 1 -> 11; matrix products, arithmetic and copies ran while one was open for 10% -> 4% of each run, Pallas kernels for 0% -> 31%
where the time goes in v2:
time: 183 us; the launch traced here: 180 us
  waiting for transfers between devices  63.4 us (35%)
  Pallas kernels  56.6 us (31%)
  starting transfers between devices  30.2 us (17%)
  between operations  14 us (8%)
  other arithmetic  8.67 us (5%)
  local copies, waits for them, and re-layouts  7.44 us (4%)
    ppermute x14, waiting for transfers between devices, move(): return lax.ppermute(a, AXES, pairs)  62 us
    ppermute x14, starting transfers between devices, move(): return lax.ppermute(a, AXES, pairs)  24.9 us
    pallas_call x1, Pallas kernels, own_part(): pl.pallas_call(own_kernel, out_shape=[jax.ShapeDtypeStruct((4, TOK, WIDE)...  15.5 us
    pallas_call x1, Pallas kernels, partner_part(): pl.pallas_call(partner_kernel, out_shape=[send, send, send, jax.ShapeDtyp...  14.3 us
    pallas_call x1, Pallas kernels, merge(): pl.pallas_call(merge_kernel, out_shape=[jax.ShapeDtypeStruct((8 * BLOCK,...  11.5 us
    pallas_call x2, Pallas kernels, pack(): pl.pallas_call(functools.partial(pack_kernel, n), out_shape=[jax.ShapeDty...  9.11 us
    pallas_call x1, Pallas kernels, last_part(): pl.pallas_call(last_kernel, out_shape=jax.ShapeDtypeStruct((TOK, WIDE), F...  6.23 us
    ppermute x5, starting transfers between devices, swap(): return lax.ppermute(a, AXES, [(i, i ^ bits) for i in range(128)])  5.1 us
  transfers between devices with their start and end apart: 22, of which 11 were waited for; matrix products, arithmetic and copies ran while one was open for 4% of the time, Pallas kernels for 31%

profile of v2, /device:TPU:0, one launch (start us, length us, event | category | flops | bytes accessed | tf_op | source)
XLA Modules:
  0.0 180.4 jit_solution(15888960266936658569)
XLA Ops:
  9.3 4.0 %collective-permute-start = (bf16[1088,128]{1,0:T(8,128)(2,1)S(1)}, bf16[1088,128]{1,0:T(8,128)(2,1)S(1)}, u32[]{:S(2)}, u32[]{:S(2)}) collective-permute-start(bf16[1088,128]{1,0:T(8,128)(2,1)S(1)} %maximum_maximum_fusion), channel_id=1, source_target_pairs={{0,64},{1,65},{2,66},{3,67},{4,68},{5,69},{6,70},{7,71},{8,72},{9,... | collective-permute-start | bytes 835592 | tf_op jit(solution)/shard_map/ppermute | solution.py:31
  14.9 4.7 %pack.2 = (bf16[2048,256]{1,0:T(8,128)(2,1)}, bf16[2048,256]{1,0:T(8,128)(2,1)}, bf16[2048,256]{1,0:T(8,128)(2,1)}, bf16[2048,256]{1,0:T(8,128)(2,1)}) custom-call(s32[4]{0:T(128)} %pad_add_fusion.1.idx, bf16[2048,2048]{1,0:T(8,128)(2,1)} %base.7), custom_call_target="tpu_custom_call" | custom-call | bytes 8388608 | tf_op jit(solution)/shard_map/pack/pallas_call | solution.py:99
  20.9 4.4 %pack.3 = (bf16[2144,256]{1,0:T(8,128)(2,1)}, bf16[2144,256]{1,0:T(8,128)(2,1)}, bf16[2144,256]{1,0:T(8,128)(2,1)}) custom-call(s32[3]{0:T(128)} %pad_add_fusion.2.idx, bf16[2048,2048]{1,0:T(8,128)(2,1)} %base.7, bf16[192,128]{1,0:T(8,128)(2,1)} %pad_maximum_fusion.4.refs_0_), custom_call_target="tpu_custom_call" | custom-call | bytes 6291456 | tf_op jit(solution)/shard_map/pack/pallas_call | solution.py:99
  28.6 3.1 %collective-permute-start.6 = (bf16[2144,256]{1,0:T(8,128)(2,1)}, bf16[2144,256]{1,0:T(8,128)(2,1)S(1)}, u32[]{:S(2)}, u32[]{:S(2)}) collective-permute-start(bf16[2144,256]{1,0:T(8,128)(2,1)} %get-tuple-element.43), channel_id=1, source_target_pairs={{0,48},{1,49},{2,50},{3,51},{4,52},{5,53},{6,54},{7,55},{8,56},{9,... | collective-permute-start | bytes 3293192 | tf_op jit(solution)/shard_map/ppermute | solution.py:27
  31.7 2.2 %collective-permute-start.7 = (bf16[2144,256]{1,0:T(8,128)(2,1)}, bf16[2144,256]{1,0:T(8,128)(2,1)S(1)}, u32[]{:S(2)}, u32[]{:S(2)}) collective-permute-start(bf16[2144,256]{1,0:T(8,128)(2,1)} %get-tuple-element.44), channel_id=1, source_target_pairs={{0,32},{1,33},{2,34},{3,35},{4,36},{5,37},{6,38},{7,39},{8,40},{9,... | collective-permute-start | bytes 3293192 | tf_op jit(solution)/shard_map/ppermute | solution.py:27
  33.9 2.5 %collective-permute-start.4 = (bf16[2048,256]{1,0:T(8,128)(2,1)}, bf16[2048,256]{1,0:T(8,128)(2,1)}, u32[]{:S(2)}, u32[]{:S(2)}) collective-permute-start(bf16[2048,256]{1,0:T(8,128)(2,1)} %get-tuple-element.39), channel_id=1, source_target_pairs={{0,64},{1,65},{2,66},{3,67},{4,68},{5,69},{6,70},{7,71},{8,72},{9,... | collective-permute-start | bytes 3145736 | tf_op jit(solution)/shard_map/ppermute | solution.py:27
  37.5 24.4 %collective-permute-done.4.h2 = bf16[2048,256]{1,0:T(8,128)(2,1)} collective-permute-done((bf16[2048,256]{1,0:T(8,128)(2,1)}, bf16[2048,256]{1,0:T(8,128)(2,1)}, u32[]{:S(2)}, u32[]{:S(2)}) %collective-permute-start.4) | collective-permute-done | bytes 1048608 | tf_op jit(solution)/shard_map/ppermute | solution.py:27
  61.8 19.8 %collective-permute-done.3.h1 = bf16[2048,256]{1,0:T(8,128)(2,1)} collective-permute-done((bf16[2048,256]{1,0:T(8,128)(2,1)}, bf16[2048,256]{1,0:T(8,128)(2,1)}, u32[]{:S(2)}, u32[]{:S(2)}) %collective-permute-start.3) | collective-permute-done | bytes 1048608 | tf_op jit(solution)/shard_map/ppermute | solution.py:27
  82.7 3.3 %collective-permute-start.11 = (bf16[4,192,128]{2,1,0:T(8,128)(2,1)S(1)}, bf16[4,192,128]{2,1,0:T(8,128)(2,1)S(1)}, u32[]{:S(2)}, u32[]{:S(2)}) collective-permute-start(bf16[4,192,128]{2,1,0:T(8,128)(2,1)S(1)} %get-tuple-element.48), channel_id=1, source_target_pairs={{0,64},{1,65},{2,66},{3,67},{4,68},{5,69},{6,70},{7,71},{8,72},{9,... | collective-permute-start | bytes 589832 | tf_op jit(solution)/shard_map/ppermute | solution.py:27
  88.4 3.0 %collective-permute-done.11 = bf16[4,192,128]{2,1,0:T(8,128)(2,1)S(1)} collective-permute-done((bf16[4,192,128]{2,1,0:T(8,128)(2,1)S(1)}, bf16[4,192,128]{2,1,0:T(8,128)(2,1)S(1)}, u32[]{:S(2)}, u32[]{:S(2)}) %collective-permute-start.11) | collective-permute-done | bytes 196640 | tf_op jit(solution)/shard_map/ppermute | solution.py:27
  92.9 15.5 %own_part.1 = (f32[4,1024,256]{2,1,0:T(8,128)}, f32[1024,64]{1,0:T(8,128)}) custom-call(s32[14]{0:T(128)} %stack.90.idx, bf16[4,2176,128]{2,1,0:T(8,128)(2,1)} %bitcast.61, bf16[4,2176,128]{2,1,0:T(8,128)(2,1)} %collective-permute-done.12.other, bf16[2048,2048]{1,0:T(8,128)(2,1)} %base.7), custom_call_target="tpu_custom_call" | custom-call | flops 5368709120 | bytes 13631488 | tf_op jit(solution)/shard_map/own_part/pallas_call | solution.py:148
  108.4 2.7 %collective-permute-done.10.refs_4_ = bf16[2048,256]{1,0:T(8,128)(2,1)} collective-permute-done((bf16[2048,256]{1,0:T(8,128)(2,1)}, bf16[2048,256]{1,0:T(8,128)(2,1)}, u32[]{:S(2)}, u32[]{:S(2)}) %collective-permute-start.10) | collective-permute-done | bytes 1048608 | tf_op jit(solution)/shard_map/ppermute | solution.py:27
  111.1 2.1 %collective-permute-done.9.refs_2_ = bf16[2048,256]{1,0:T(8,128)(2,1)} collective-permute-done((bf16[2048,256]{1,0:T(8,128)(2,1)}, bf16[2048,256]{1,0:T(8,128)(2,1)}, u32[]{:S(2)}, u32[]{:S(2)}) %collective-permute-start.9) | collective-permute-done | bytes 1048608 | tf_op jit(solution)/shard_map/ppermute | solution.py:27
  113.2 4.7 %collective-permute-done.8.h3 = bf16[2048,256]{1,0:T(8,128)(2,1)} collective-permute-done((bf16[2048,256]{1,0:T(8,128)(2,1)}, bf16[2048,256]{1,0:T(8,128)(2,1)}, u32[]{:S(2)}, u32[]{:S(2)}) %collective-permute-start.8) | collective-permute-done | bytes 1048608 | tf_op jit(solution)/shard_map/ppermute | solution.py:27
  118.0 4.1 %collective-permute-start.13 = (bf16[2048,256]{1,0:T(8,128)(2,1)}, bf16[2048,256]{1,0:T(8,128)(2,1)S(1)}, u32[]{:S(2)}, u32[]{:S(2)}) collective-permute-start(bf16[2048,256]{1,0:T(8,128)(2,1)} %get-tuple-element.52), channel_id=1, source_target_pairs={{0,64},{1,65},{2,66},{3,67},{4,68},{5,69},{6,70},{7,71},{8,72},{9,... | collective-permute-start | bytes 3145736 | tf_op jit(solution)/shard_map/ppermute | solution.py:27
  124.9 14.3 %partner_part.1 = (bf16[1024,256]{1,0:T(8,128)(2,1)}, bf16[1024,256]{1,0:T(8,128)(2,1)}, bf16[1024,256]{1,0:T(8,128)(2,1)}, bf16[1024,64]{1,0:T(8,128)(2,1)}) custom-call(s32[14]{0:T(128)} %stack.90.idx, bf16[4,2176,128]{2,1,0:T(8,128)(2,1)} %bitcast.49, bf16[4,2176,128]{2,1,0:T(8,128)(2,1)} %copy-done.1, bf16[2048,256]{1,0:T(8,128)(2,1)} %collective-permute-done.3.h1, ...), custom_call_target="tpu_custom_call" | custom-call | flops 4294967296 | bytes 12582912 | tf_op jit(solution)/shard_map/partner_part/pallas_call | solution.py:188
  139.2 1.7 collective-permute-start.16
  140.9 2.7 %collective-permute-start.17 = (bf16[1024,256]{1,0:T(8,128)(2,1)}, bf16[1024,256]{1,0:T(8,128)(2,1)S(1)}, u32[]{:S(2)}, u32[]{:S(2)}) collective-permute-start(bf16[1024,256]{1,0:T(8,128)(2,1)} %get-tuple-element.61), channel_id=1, source_target_pairs={{0,48},{1,49},{2,50},{3,51},{4,52},{5,53},{6,54},{7,55},{8,56},{9,... | collective-permute-start | bytes 1572872 | tf_op jit(solution)/shard_map/ppermute | solution.py:27
  143.6 1.4 collective-permute-start.18
  147.7 2.0 %collective-permute-done.13.refs_0_.half = bf16[2048,256]{1,0:T(8,128)(2,1)S(1)} collective-permute-done((bf16[2048,256]{1,0:T(8,128)(2,1)}, bf16[2048,256]{1,0:T(8,128)(2,1)S(1)}, u32[]{:S(2)}, u32[]{:S(2)}) %collective-permute-start.13) | collective-permute-done | bytes 1048608 | tf_op jit(solution)/shard_map/ppermute | solution.py:27
  150.8 11.5 %merge.1 = (bf16[16384,256]{1,0:T(8,128)(2,1)}, f32[1,256]{1,0:T(1,128)}) custom-call(s32[14]{0:T(128)} %stack.90.idx, bf16[2048,2048]{1,0:T(8,128)(2,1)} %base.7, bf16[2048,256]{1,0:T(8,128)(2,1)} %copy-done, bf16[2144,256]{1,0:T(8,128)(2,1)} %copy-done.3, bf16[2048,256]{1,0:T(8,128)(2,1)} %collective-permute-done.9.refs_2_, bf16[2144,256]{1,0:T(8,128)(2,1)} %copy-done.2, ...), custom_call_target="tpu_custom_call" | custom-call | flops 1073741824 | bytes 18874368 | tf_op jit(solution)/shard_map/merge/pallas_call | solution.py:288
  162.3 6.2 %last_part.1 = f32[1024,256]{1,0:T(8,128)} custom-call(s32[14]{0:T(128)} %stack.90.idx, bf16[4,2176,128]{2,1,0:T(8,128)(2,1)} %bitcast.50, bf16[4,2176,128]{2,1,0:T(8,128)(2,1)} %copy-done.1, bf16[2048,256]{1,0:T(8,128)(2,1)} %copy-done, bf16[1024,64]{1,0:T(8,128)(2,1)} %get-tuple-element.59.t_ref, bf16[64,2048]{1,0:T(8,128)(2,1)} %bitcast.53, ...), custom_call_target="tpu_custom_call" | custom-call | flops 1073741824 | bytes 7340032 | tf_op jit(solution)/shard_map/last_part/pallas_call | solution.py:218
  168.6 3.0 %collective-permute-done.18 = bf16[1024,256]{1,0:T(8,128)(2,1)S(1)} collective-permute-done((bf16[1024,256]{1,0:T(8,128)(2,1)}, bf16[1024,256]{1,0:T(8,128)(2,1)S(1)}, u32[]{:S(2)}, u32[]{:S(2)}) %collective-permute-start.18) | collective-permute-done | bytes 524320 | tf_op jit(solution)/shard_map/ppermute | solution.py:27
  171.6 2.3 %fusion = bf16[1,1024,256]{2,1,0:T(8,128)(2,1)} fusion(bf16[1024,256]{1,0:T(8,128)(2,1)S(1)} %collective-permute-done.18, bf16[1024,256]{1,0:T(8,128)(2,1)S(1)} %collective-permute-done.17, f32[1024,256]{1,0:T(8,128)} %last_part.1, bf16[1024,256]{1,0:T(8,128)(2,1)S(1)} %collective-permute-done.16, f32[256]{0:T(256)S(1)} %bitcast.58), kind=kLoop, calls=%fused_computation.12 | loop fusion | flops 2097152 | bytes 3146752 | tf_op jit(solution)/shard_map/broadcast_in_dim | solution.py:374
  (77 shorter events, 20.7 us)
Async XLA Ops:
  7.2 74.6 %all-gather.8.cloned.1.call-start = ((), (), s32[]{:S(2)}) async-start(), calls=%async_computation.1 | async-start | bytes 2785280 | tf_op jit(solution)/shard_map/all_gather | solution.py:36
  9.3 16.0 %collective-permute-start = (bf16[1088,128]{1,0:T(8,128)(2,1)S(1)}, bf16[1088,128]{1,0:T(8,128)(2,1)S(1)}, u32[]{:S(2)}, u32[]{:S(2)}) collective-permute-start(bf16[1088,128]{1,0:T(8,128)(2,1)S(1)} %maximum_maximum_fusion), channel_id=1, source_target_pairs={{0,64},{1,65},{2,66},{3,67},{4,68},{5,69},{6,70},{7,71},{8,72},{9,... | collective-permute-start | bytes 835592 | tf_op jit(solution)/shard_map/ppermute | solution.py:31
  13.3 13.4 %collective-permute-start.1 = (bf16[1088,128]{1,0:T(8,128)(2,1)S(1)}, bf16[1088,128]{1,0:T(8,128)(2,1)S(1)}, u32[]{:S(2)}, u32[]{:S(2)}) collective-permute-start(bf16[1088,128]{1,0:T(8,128)(2,1)S(1)} %maximum_maximum_fusion), channel_id=1, source_target_pairs={{0,2},{1,3},{2,0},{3,1},{4,6},{5,7},{6,4},{7,5},{8,10},{9,11},{10,... | collective-permute-start | bytes 835592 | tf_op jit(solution)/shard_map/ppermute | solution.py:31
  14.3 12.4 %collective-permute-start.2 = (bf16[1088,128]{1,0:T(8,128)(2,1)S(1)}, bf16[1088,128]{1,0:T(8,128)(2,1)S(1)}, u32[]{:S(2)}, u32[]{:S(2)}) collective-permute-start(bf16[1088,128]{1,0:T(8,128)(2,1)S(1)} %maximum_maximum_fusion), channel_id=1, source_target_pairs={{0,66},{1,67},{2,64},{3,65},{4,70},{5,71},{6,68},{7,69},{8,74},{9,... | collective-permute-start | bytes 835592 | tf_op jit(solution)/shard_map/ppermute | solution.py:31
  27.6 90.2 %all-gather.10.cloned.1.call-start = ((), (), s32[]{:S(2)}) async-start(), calls=%async_computation.2 | async-start | bytes 2785280 | tf_op jit(solution)/shard_map/all_gather | solution.py:36
  28.6 119.1 %all-gather.6.cloned.1.call-start = ((), (), s32[]{:S(2)}) async-start(), calls=%async_computation | async-start | bytes 2228224 | tf_op jit(solution)/shard_map/all_gather | solution.py:353
  28.6 53.0 %collective-permute-start.6 = (bf16[2144,256]{1,0:T(8,128)(2,1)}, bf16[2144,256]{1,0:T(8,128)(2,1)S(1)}, u32[]{:S(2)}, u32[]{:S(2)}) collective-permute-start(bf16[2144,256]{1,0:T(8,128)(2,1)} %get-tuple-element.43), channel_id=1, source_target_pairs={{0,48},{1,49},{2,50},{3,51},{4,52},{5,53},{6,54},{7,55},{8,56},{9,... | collective-permute-start | bytes 3293192 | tf_op jit(solution)/shard_map/ppermute | solution.py:27
  31.7 50.0 %collective-permute-start.5 = (bf16[2144,256]{1,0:T(8,128)(2,1)}, bf16[2144,256]{1,0:T(8,128)(2,1)S(1)}, u32[]{:S(2)}, u32[]{:S(2)}) collective-permute-start(bf16[2144,256]{1,0:T(8,128)(2,1)} %get-tuple-element.41), channel_id=1, source_target_pairs={{0,16},{1,17},{2,18},{3,19},{4,20},{5,21},{6,22},{7,23},{8,24},{9,... | collective-permute-start | bytes 3293192 | tf_op jit(solution)/shard_map/ppermute | solution.py:27
  31.7 50.0 %collective-permute-start.7 = (bf16[2144,256]{1,0:T(8,128)(2,1)}, bf16[2144,256]{1,0:T(8,128)(2,1)S(1)}, u32[]{:S(2)}, u32[]{:S(2)}) collective-permute-start(bf16[2144,256]{1,0:T(8,128)(2,1)} %get-tuple-element.44), channel_id=1, source_target_pairs={{0,32},{1,33},{2,34},{3,35},{4,36},{5,37},{6,38},{7,39},{8,40},{9,... | collective-permute-start | bytes 3293192 | tf_op jit(solution)/shard_map/ppermute | solution.py:27
  33.9 27.9 %collective-permute-start.4 = (bf16[2048,256]{1,0:T(8,128)(2,1)}, bf16[2048,256]{1,0:T(8,128)(2,1)}, u32[]{:S(2)}, u32[]{:S(2)}) collective-permute-start(bf16[2048,256]{1,0:T(8,128)(2,1)} %get-tuple-element.39), channel_id=1, source_target_pairs={{0,64},{1,65},{2,66},{3,67},{4,68},{5,69},{6,70},{7,71},{8,72},{9,... | collective-permute-start | bytes 3145736 | tf_op jit(solution)/shard_map/ppermute | solution.py:27
  36.4 45.3 %collective-permute-start.3 = (bf16[2048,256]{1,0:T(8,128)(2,1)}, bf16[2048,256]{1,0:T(8,128)(2,1)}, u32[]{:S(2)}, u32[]{:S(2)}) collective-permute-start(bf16[2048,256]{1,0:T(8,128)(2,1)} %get-tuple-element.37), channel_id=1, source_target_pairs={{0,64},{1,65},{2,66},{3,67},{4,68},{5,69},{6,70},{7,71},{8,72},{9,... | collective-permute-start | bytes 3145736 | tf_op jit(solution)/shard_map/ppermute | solution.py:27
  81.7 10.4 %copy-start.3 = (bf16[2144,256]{1,0:T(8,128)(2,1)}, bf16[2144,256]{1,0:T(8,128)(2,1)S(1)}, u32[]{:S(2)}) copy-start(bf16[2144,256]{1,0:T(8,128)(2,1)S(1)} %collective-permute-done.5.refs_1_) | copy-start | bytes 3293188
  81.7 10.4 %copy-start.4 = (bf16[2144,256]{1,0:T(8,128)(2,1)}, bf16[2144,256]{1,0:T(8,128)(2,1)S(1)}, u32[]{:S(2)}) copy-start(bf16[2144,256]{1,0:T(8,128)(2,1)S(1)} %collective-permute-done.7.refs_5_) | copy-start | bytes 3293188
  81.8 11.1 %collective-permute-start.12 = (bf16[4,2176,128]{2,1,0:T(8,128)(2,1)}, bf16[4,2176,128]{2,1,0:T(8,128)(2,1)}, u32[]{:S(2)}, u32[]{:S(2)}) collective-permute-start(bf16[4,2176,128]{2,1,0:T(8,128)(2,1)} %bitcast.60), channel_id=1, source_target_pairs={{0,1},{1,0},{2,3},{3,2},{4,5},{5,4},{6,7},{7,6},{8,9},{9,8},{10,11... | collective-permute-start | bytes 6684680 | tf_op jit(solution)/shard_map/ppermute | solution.py:31
  82.7 8.6 %collective-permute-start.11 = (bf16[4,192,128]{2,1,0:T(8,128)(2,1)S(1)}, bf16[4,192,128]{2,1,0:T(8,128)(2,1)S(1)}, u32[]{:S(2)}, u32[]{:S(2)}) collective-permute-start(bf16[4,192,128]{2,1,0:T(8,128)(2,1)S(1)} %get-tuple-element.48), channel_id=1, source_target_pairs={{0,64},{1,65},{2,66},{3,67},{4,68},{5,69},{6,70},{7,71},{8,72},{9,... | collective-permute-start | bytes 589832 | tf_op jit(solution)/shard_map/ppermute | solution.py:27
  86.1 25.0 %collective-permute-start.10 = (bf16[2048,256]{1,0:T(8,128)(2,1)}, bf16[2048,256]{1,0:T(8,128)(2,1)}, u32[]{:S(2)}, u32[]{:S(2)}) collective-permute-start(bf16[2048,256]{1,0:T(8,128)(2,1)} %collective-permute-done.4.h2), channel_id=1, source_target_pairs={{0,48},{1,49},{2,50},{3,51},{4,52},{5,53},{6,54},{7,55},{8,56},{9,... | collective-permute-start | bytes 3145736 | tf_op jit(solution)/shard_map/ppermute | solution.py:27
  87.4 25.8 %collective-permute-start.9 = (bf16[2048,256]{1,0:T(8,128)(2,1)}, bf16[2048,256]{1,0:T(8,128)(2,1)}, u32[]{:S(2)}, u32[]{:S(2)}) collective-permute-start(bf16[2048,256]{1,0:T(8,128)(2,1)} %collective-permute-done.3.h1), channel_id=1, source_target_pairs={{0,16},{1,17},{2,18},{3,19},{4,20},{5,21},{6,22},{7,23},{8,24},{9,... | collective-permute-start | bytes 3145736 | tf_op jit(solution)/shard_map/ppermute | solution.py:27
  88.1 29.8 %collective-permute-start.8 = (bf16[2048,256]{1,0:T(8,128)(2,1)}, bf16[2048,256]{1,0:T(8,128)(2,1)}, u32[]{:S(2)}, u32[]{:S(2)}) collective-permute-start(bf16[2048,256]{1,0:T(8,128)(2,1)} %get-tuple-element.45), channel_id=1, source_target_pairs={{0,64},{1,65},{2,66},{3,67},{4,68},{5,69},{6,70},{7,71},{8,72},{9,... | collective-permute-start | bytes 3145736 | tf_op jit(solution)/shard_map/ppermute | solution.py:27
  117.9 5.6 %collective-permute-start.15 = (bf16[4,2176,128]{2,1,0:T(8,128)(2,1)}, bf16[4,2176,128]{2,1,0:T(8,128)(2,1)S(1)}, u32[]{:S(2)}, u32[]{:S(2)}) collective-permute-start(bf16[4,2176,128]{2,1,0:T(8,128)(2,1)} %bitcast.48), channel_id=1, source_target_pairs={{0,1},{1,0},{2,3},{3,2},{4,5},{5,4},{6,7},{7,6},{8,9},{9,8},{10,11... | collective-permute-start | bytes 6684680 | tf_op jit(solution)/shard_map/ppermute | solution.py:31
  118.0 31.7 %collective-permute-start.13 = (bf16[2048,256]{1,0:T(8,128)(2,1)}, bf16[2048,256]{1,0:T(8,128)(2,1)S(1)}, u32[]{:S(2)}, u32[]{:S(2)}) collective-permute-start(bf16[2048,256]{1,0:T(8,128)(2,1)} %get-tuple-element.52), channel_id=1, source_target_pairs={{0,64},{1,65},{2,66},{3,67},{4,68},{5,69},{6,70},{7,71},{8,72},{9,... | collective-permute-start | bytes 3145736 | tf_op jit(solution)/shard_map/ppermute | solution.py:27
  122.1 27.9 %collective-permute-start.14 = (bf16[2048,256]{1,0:T(8,128)(2,1)}, bf16[2048,256]{1,0:T(8,128)(2,1)}, u32[]{:S(2)}, u32[]{:S(2)}) collective-permute-start(bf16[2048,256]{1,0:T(8,128)(2,1)} %collective-permute-done.8.h3), channel_id=1, source_target_pairs={{0,32},{1,33},{2,34},{3,35},{4,36},{5,37},{6,38},{7,39},{8,40},{9,... | collective-permute-start | bytes 3145736 | tf_op jit(solution)/shard_map/ppermute | solution.py:27
  139.2 29.4 %collective-permute-start.16 = (bf16[1024,256]{1,0:T(8,128)(2,1)}, bf16[1024,256]{1,0:T(8,128)(2,1)S(1)}, u32[]{:S(2)}, u32[]{:S(2)}) collective-permute-start(bf16[1024,256]{1,0:T(8,128)(2,1)} %get-tuple-element.60), channel_id=1, source_target_pairs={{0,16},{1,17},{2,18},{3,19},{4,20},{5,21},{6,22},{7,23},{8,24},{9,... | collective-permute-start | bytes 1572872 | tf_op jit(solution)/shard_map/ppermute | solution.py:27
  140.9 27.7 %collective-permute-start.17 = (bf16[1024,256]{1,0:T(8,128)(2,1)}, bf16[1024,256]{1,0:T(8,128)(2,1)S(1)}, u32[]{:S(2)}, u32[]{:S(2)}) collective-permute-start(bf16[1024,256]{1,0:T(8,128)(2,1)} %get-tuple-element.61), channel_id=1, source_target_pairs={{0,48},{1,49},{2,50},{3,51},{4,52},{5,53},{6,54},{7,55},{8,56},{9,... | collective-permute-start | bytes 1572872 | tf_op jit(solution)/shard_map/ppermute | solution.py:27
  143.6 28.0 %collective-permute-start.18 = (bf16[1024,256]{1,0:T(8,128)(2,1)}, bf16[1024,256]{1,0:T(8,128)(2,1)S(1)}, u32[]{:S(2)}, u32[]{:S(2)}) collective-permute-start(bf16[1024,256]{1,0:T(8,128)(2,1)} %get-tuple-element.62), channel_id=1, source_target_pairs={{0,32},{1,33},{2,34},{3,35},{4,36},{5,37},{6,38},{7,39},{8,40},{9,... | collective-permute-start | bytes 1572872 | tf_op jit(solution)/shard_map/ppermute | solution.py:27
  (6 other events, 23.8 us)
Sparse Core Ops, SparseCore 0:
  27.8 32.8 all-gather.7
  62.3 31.9 all-gather.9
  96.6 35.7 all-gather.5

commit v3 on v2

v3 whole, which is shorter than its diff:
```python
import functools

import jax
import jax.numpy as jnp
from jax import lax
from jax.experimental import pallas as pl
from jax.experimental.pallas import tpu as pltpu
from jax.sharding import PartitionSpec as P

AXES = ("row", "col")
SHIFTS = (1, -1, 2)
BLOCK = 2048
WIDE = 256
TOK = 1024
N_COL = 16
MIB = 1024 * 1024
F32 = jnp.float32
BF16 = jnp.bfloat16


def move(a, dz=0, dy=0):
    pairs = []
    for r in range(8):
        zh, y = divmod(r, 4)
        to = ((zh + dz) % 2) * 4 + (y + dy) % 4
        pairs += [(r * N_COL + c, to * N_COL + c) for c in range(N_COL)]
    return lax.ppermute(a, AXES, pairs)


def swap(a, bits):
    return lax.ppermute(a, AXES, [(i, i ^ bits) for i in range(128)])


def gather_x(a):
    groups = [[16 * r + 4 * x + 2 * zl + k for x in range(4) for k in range(2)] for r in range(8) for zl in range(2)]
    return lax.all_gather(a, AXES, axis=0, tiled=False, axis_index_groups=groups)


def after(x, *deps):
    return lax.optimization_barrier((x, *deps))[0]


def params(mib, **kw):
    return pltpu.CompilerParams(vmem_limit_bytes=mib * MIB, **kw)


PART = TOK + 64
PLACE = dict(served=0, rows=4, zl=12)


def block_copies(idx, gathered, whole, left, sem, left_sem):
    prompts, lefts = [], []
    for j in range(8):
        for h in range(2):
            zl = idx[PLACE["zl"]] if h == 0 else 1 - idx[PLACE["zl"]]
            c = j // 2 * 4 + zl * 2 + j % 2
            lanes = pl.ds(pl.multiple_of(c * 128, 128), 128)
            prompts.append(pltpu.make_async_copy(gathered.at[j, pl.ds(h * PART, TOK), :], whole.at[:, lanes], sem))
            if left is not None:
                lefts.append(pltpu.make_async_copy(gathered.at[j, pl.ds(h * PART + TOK, 64), :], left.at[c], left_sem))
    return prompts, lefts


EXTRA = 128


def pack_kernel(n, idx, base, *refs):
    outs, (stage, sems) = refs[:-2], refs[-2:]
    reads, writes = [], []
    for j in range(n):
        at = pl.ds(pl.multiple_of(idx[j] * WIDE, WIDE), WIDE)
        for h in range(2):
            rows = pl.ds(h * 1024, 1024)
            reads.append(pltpu.make_async_copy(base.at[rows, at], stage.at[j, rows, :], sems.at[0, j, h]))
            writes.append(pltpu.make_async_copy(stage.at[j, rows, :], outs[j].at[rows, :], sems.at[1, j, h]))
    for c in reads:
        c.start()
    for r, w in zip(reads, writes):
        r.wait()
        w.start()
    wait_all(writes)


def pack(places, base, extra):
    n = len(places)
    return pl.pallas_call(
        functools.partial(pack_kernel, n),
        out_shape=[jax.ShapeDtypeStruct((BLOCK + EXTRA * (j < extra), WIDE), BF16) for j in range(n)],
        in_specs=specs("sh"),
        out_specs=specs("h" * n),
        scratch_shapes=[pltpu.VMEM((n, BLOCK, WIDE), BF16), pltpu.SemaphoreType.DMA((2, n, 2))],
        compiler_params=params(56),
        cost_estimate=pl.CostEstimate(flops=0, bytes_accessed=2 * n * MIB, transcendentals=0),
        name="pack",
    )(jnp.stack(places), base)


def append_kernel(left, beside, right, a1, a2, a3, o1, o2, o3, sem):
    copies = []
    for o in (o1, o2, o3):
        for src, row, lane in ((left, 0, 0), (beside.at[pl.ds(TOK, 64), :], 64, 0), (right, 0, 128)):
            dst = o.at[pl.ds(BLOCK + row, src.shape[0]), pl.ds(lane, 128)]
            copies.append(pltpu.make_async_copy(src, dst, sem))
    for c in copies:
        c.start()
    wait_all(copies)


def append(left, beside, right, blocks):
    return pl.pallas_call(
        append_kernel,
        out_shape=[jax.ShapeDtypeStruct(b.shape, b.dtype) for b in blocks],
        in_specs=specs("vvvhhh"),
        out_specs=specs("hhh"),
        scratch_shapes=[pltpu.SemaphoreType.DMA],
        input_output_aliases={3: 0, 4: 1, 5: 2},
        compiler_params=params(56),
        cost_estimate=pl.CostEstimate(flops=0, bytes_accessed=MIB, transcendentals=0),
        name="append",
    )(left, beside, right, *blocks)


def wait_all(copies):
    for c in copies:
        c.wait()


def specs(kinds):
    space = dict(h=pltpu.HBM, s=pltpu.SMEM, v=pltpu.VMEM)
    return [pl.BlockSpec(memory_space=space[k]) for k in kinds]


def dot(a, b):
    return jnp.dot(a, b, preferred_element_type=F32)


def unpacked(ref):
    value = ref[...]
    return jnp.concatenate([value[:, :, :64], value[:, :, 64:]], axis=1).reshape(BLOCK, 64)


def own_kernel(idx, gathered, base, acc, t_ref, own, w, left, sems):
    prompts, lefts = block_copies(idx, gathered, own, left, sems.at[4], sems.at[5])
    cols = []
    for j in range(4):
        at = pl.ds(pl.multiple_of(idx[j] * WIDE, WIDE), WIDE)
        cols.append(pltpu.make_async_copy(base.at[:, at], w.at[j], sems.at[j]))
    for c in lefts + prompts + cols:
        c.start()
    wait_all(lefts)
    factor = unpacked(left)
    wait_all(prompts)
    t_ref[...] = dot(own[...], factor)
    for j in range(4):
        cols[j].wait()
        acc[j] = dot(own[...], w[j])


def own_part(idx, gathered, base):
    return pl.pallas_call(
        own_kernel,
        out_shape=[jax.ShapeDtypeStruct((4, TOK, WIDE), F32), jax.ShapeDtypeStruct((TOK, 64), F32)],
        in_specs=specs("shh"),
        out_specs=specs("vv"),
        scratch_shapes=[
            pltpu.VMEM((TOK, BLOCK), BF16),
            pltpu.VMEM((4, BLOCK, WIDE), BF16),
            pltpu.VMEM((N_COL, 64, 128), BF16),
            pltpu.SemaphoreType.DMA((6,)),
        ],
        compiler_params=params(56),
        cost_estimate=pl.CostEstimate(flops=2 * TOK * BLOCK * 5 * WIDE, bytes_accessed=13 * MIB, transcendentals=0),
        name="own_part",
    )(idx, gathered, base)


def partner_kernel(idx, gathered, h1, h2, h3, r_ref, own_t, acc, o1, o2, o3, t_ref, par, w, part, left, sems):
    prompts, lefts = block_copies(idx, gathered, par, left, sems.at[6], sems.at[7])
    halves = [pltpu.make_async_copy(h, w.at[i], sems.at[i]) for i, h in enumerate((h1, h2, h3))]
    parts = [pltpu.make_async_copy(acc.at[i + 1], part.at[i], sems.at[3 + i]) for i in range(3)]
    for c in lefts + prompts:
        c.start()
    for h, p in zip(halves, parts):
        h.start()
        p.start()
    wait_all(lefts)
    factor = unpacked(left)
    wait_all(prompts)
    t = (own_t[...] + dot(par[...], factor)).astype(BF16)
    t_ref[...] = t
    for i, o in enumerate((o1, o2, o3)):
        right = r_ref[:, pl.ds(pl.multiple_of(idx[1 + i] * WIDE, WIDE), WIDE)]
        halves[i].wait()
        parts[i].wait()
        o[...] = (dot(par[...], w[i]) + dot(t, right) + part[i]).astype(BF16)


def partner_part(idx, gathered, halves, rights, own_t, acc):
    send = jax.ShapeDtypeStruct((TOK, WIDE), BF16)
    return pl.pallas_call(
        partner_kernel,
        out_shape=[send, send, send, jax.ShapeDtypeStruct((TOK, 64), BF16)],
        in_specs=specs("shhhhvvh"),
        out_specs=specs("vvvv"),
        scratch_shapes=[
            pltpu.VMEM((TOK, BLOCK), BF16),
            pltpu.VMEM((3, BLOCK, WIDE), BF16),
            pltpu.VMEM((3, TOK, WIDE), F32),
            pltpu.VMEM((N_COL, 64, 128), BF16),
            pltpu.SemaphoreType.DMA((8,)),
        ],
        compiler_params=params(56),
        cost_estimate=pl.CostEstimate(flops=2 * TOK * BLOCK * 4 * WIDE, bytes_accessed=12 * MIB, transcendentals=0),
        name="partner_part",
    )(idx, gathered, *halves, rights, own_t, acc)


def merge_kernel(idx, base, *refs):
    blocks, refs = refs[:7], refs[7:]
    lefts, gathered, acc, rr_ref, mag_ref, t_ref, r_ref = refs[:7]
    out, scale_ref, product, raw, comb, left, par, sems, out_sems = refs[7:]
    prompts, _ = block_copies(idx, gathered, par, None, sems.at[9], None)
    prompts.append(pltpu.make_async_copy(acc.at[0], product, sems.at[10]))
    first = []
    for j in range(8):
        for h in range(2):
            zl = idx[PLACE["zl"]] if h == 0 else 1 - idx[PLACE["zl"]]
            c = j // 2 * 4 + zl * 2 + j % 2
            for k in range(2):
                rows = pl.ds((2 * h + k) * 256, 256)
                first.append(pltpu.make_async_copy(lefts.at[j, rows, :], left.at[c, k], sems.at[8]))
    for c in first:
        c.start()
    col = pl.ds(pl.multiple_of(idx[0] * WIDE, WIDE), WIDE)
    pltpu.make_async_copy(base.at[:, col], raw.at[0], sems.at[0]).start()
    for j in range(7):
        pltpu.make_async_copy(blocks[j].at[pl.ds(0, BLOCK), :], raw.at[j + 1], sems.at[j + 1]).start()
    for c in prompts:
        c.start()
    wait_all(first)

    def part(i, squares):
        j, h = i // 2, i % 2

        @pl.when(h == 0)
        def _():
            pltpu.make_async_copy(blocks[0], raw.at[j], sems.at[j]).wait()

        factor = left[pl.ds(h * 8, 8), j % 2, pl.ds(pl.multiple_of(j // 2 * 64, 64), 64), :].reshape(512, 128)
        update = jnp.dot(factor, rr_ref[...], preferred_element_type=F32)
        for c in range(8):
            for k in range(2):
                rows = pl.ds(pl.multiple_of(h * 1024 + c * 128 + k * 64, 64), 64)
                value = raw[j, rows, :].astype(F32) + update[c * 64 : (c + 1) * 64, k * WIDE : (k + 1) * WIDE]
                comb[j, rows, :] = value
                squares += (value * value).reshape(8, 8, WIDE).sum(axis=0)
        return squares

    squares = lax.fori_loop(0, 16, part, jnp.zeros((8, WIDE), F32))
    scale = mag_ref[...] / jnp.sqrt(squares.sum(axis=0, keepdims=True) + 1e-6)
    scale_ref[...] = scale
    wait_all(prompts)
    product[...] += dot(par[...], raw[1]) + dot(t_ref[...], r_ref[...])

    def out_copy(j):
        rows = pl.ds(pl.multiple_of(idx[PLACE["rows"] + j] * BLOCK, BLOCK), BLOCK)
        return pltpu.make_async_copy(raw.at[j], out.at[rows, :], out_sems.at[j])

    @pl.loop(0, 8)
    def _(j):
        @pl.loop(0, 8)
        def _(m):
            rows = pl.ds(pl.multiple_of(m * 256, 256), 256)
            raw[j, rows, :] = (comb[j, rows, :] * scale).astype(BF16)

        out_copy(j).start()

    @pl.loop(0, 8)
    def _(j):
        out_copy(j).wait()


def merge(idx, base, blocks, lefts, gathered, acc, rr, mag, t, right):
    any_space = pl.BlockSpec(memory_space=pltpu.HBM)
    vmem = pl.BlockSpec(memory_space=pltpu.VMEM)
    return pl.pallas_call(
        merge_kernel,
        out_shape=[
            jax.ShapeDtypeStruct((8 * BLOCK, WIDE), BF16),
            jax.ShapeDtypeStruct((1, WIDE), F32),
            jax.ShapeDtypeStruct((TOK, WIDE), F32),
        ],
        in_specs=[pl.BlockSpec(memory_space=pltpu.SMEM)] + [any_space] * 11 + [vmem] * 4,
        out_specs=[any_space, vmem, vmem],
        scratch_shapes=[
            pltpu.VMEM((8, BLOCK, WIDE), BF16),
            pltpu.VMEM((8, BLOCK, WIDE), F32),
            pltpu.VMEM((N_COL, 2, 256, 128), BF16),
            pltpu.VMEM((TOK, BLOCK), BF16),
            pltpu.SemaphoreType.DMA((11,)),
            pltpu.SemaphoreType.DMA((8,)),
        ],
        compiler_params=params(56),
        cost_estimate=pl.CostEstimate(flops=2 * 128 * 512 * 8192, bytes_accessed=18 * MIB, transcendentals=0),
        name="merge",
    )(idx, base, *blocks, lefts, gathered, acc, rr, mag, t, right)


def shards(prompt, base, factor_left, factor_right, magnitude):
    row = lax.axis_index("row").astype(jnp.int32)
    zh, y = row // 4, row % 4
    order = (0,) + SHIFTS

    def served_by(dz, dy):
        return ((zh + dz) % 2) * 4 + (y + dy) % 4

    left = jnp.concatenate([factor_left[:64], factor_left[64:]], axis=1)
    right = factor_right.reshape(8, 16, 128).transpose(1, 0, 2).reshape(128, 128)
    small = jnp.concatenate([prompt, left], axis=0)

    partner, beside, beside_partner = swap(small, 64), swap(small, 2), swap(small, 66)
    relayed = {}
    places = [served_by(0, d) for d in SHIFTS] + [served_by(1, d) for d in SHIFTS + (0,)]
    slices = pack(places, base, 3)
    packed, packed_half = dict(zip(SHIFTS, slices)), dict(zip(SHIFTS + (0,), slices[3:]))

    wave = (partner, beside, beside_partner, packed[2])
    partner, beside, beside_partner, _ = lax.optimization_barrier(wave)
    gathered = gather_x(jnp.concatenate([small, beside], axis=0))
    gathered_partner = gather_x(jnp.concatenate([partner, beside_partner], axis=0))
    half = {d: move(after(packed_half[d], *wave), dz=1) for d in (-1, 1)}
    factors = jnp.concatenate([left, beside[TOK:], right], axis=0)
    straight = {}
    for d, block in zip(SHIFTS, append(left, beside, right, [packed[d] for d in SHIFTS])):
        straight[d] = move(block, dy=d)

    wave = (*(straight[d] for d in SHIFTS), half[-1], half[1])
    for d in (1, -1):
        relayed[d] = move(after(half[d], *wave), dy=d)
    half[2] = move(after(packed_half[2], *wave), dz=1)
    got = [factors]
    for d in SHIFTS:
        below = straight[d][BLOCK:]
        got.append(jnp.concatenate([below[:, :128], below[:, 128:]], axis=0))
    got = jnp.stack(got)
    places = [((zh + k) % 2) * 4 + (y - d) % 4 for d in order for k in range(2)]
    at_col = lax.axis_index("col").astype(jnp.int32)
    idx = jnp.stack([served_by(0, d) for d in order] + places + [at_col // 2 % 2])
    acc, own_t = own_part(idx, after(gathered, *wave), base)
    got_partner = swap(after(got, *wave, own_t), 64)

    wave = (half[2], relayed[1], relayed[-1], own_t)
    half[0] = move(after(packed_half[0], *wave), dz=1)
    relayed[2] = move(after(half[2], *wave), dy=2)
    lefts = jnp.stack([got[:, :64], got_partner[:, :64], got[:, 64:128], got_partner[:, 64:128]]).reshape(1024, 128)
    lefts = gather_x(after(lefts, *wave))

    rights = jnp.stack([jnp.stack([got[j, 128:], got_partner[j, 128:]]) for j in (0, 2, 3, 1)])
    rights = lax.dynamic_slice_in_dim(jnp.concatenate([rights, rights], axis=0), (4 - y) % 4, 4, 0)
    rights = lax.dynamic_slice_in_dim(jnp.concatenate([rights, rights[:, :1]], axis=1), zh, 2, 1)
    rights = rights.reshape(4, 2, 16, 8, 128).transpose(1, 0, 3, 2, 4).reshape(64, 2048)

    *sends, t = partner_part(idx, gathered_partner, [half[d] for d in SHIFTS], rights, own_t, acc)
    sums = [move(s, dy=d) for s, d in zip(sends, SHIFTS)]

    right_mine = lax.dynamic_slice(rights, (0, row * WIDE), (64, WIDE))
    rr = jnp.pad(right_mine, ((0, 64), (0, WIDE))) + jnp.pad(right_mine, ((64, 0), (WIDE, 0)))
    mag = lax.dynamic_slice(magnitude, (row * WIDE,), (WIDE,))[None]
    blocks = [half[0]]
    for d in SHIFTS:
        blocks += [straight[d], relayed[d]]
    serving, scale, product = merge(
        idx, base, blocks, lefts, gathered_partner, acc, rr, mag, t, right_mine
    )

    for s in sums:
        product = product + s.astype(F32)
    return serving[None], (product * scale).astype(BF16)[None]


def solution(mesh):
    in_specs = (
        P(None, ("row", "col")),
        P("row", "col"),
        P(("row", "col"), None),
        P("row", "col"),
        P("col"),
    )
    out_specs = (P("row", None, "col"), P("row", None, "col"))
    return jax.shard_map(shards, mesh=mesh, in_specs=in_specs, out_specs=out_specs, check_vma=False)
```

time: 183 us -> 173 us (0.945)
  Pallas kernels: 56.6 us -> 52.1 us
  waiting for transfers between devices: 63.4 us -> 61.2 us
    ppermute x14 -> x13, waiting for transfers between devices: 62 us -> 50 us  [move(): return lax.ppermute(a, AXES, pairs)]
    ppermute x5 -> x4, waiting for transfers between devices: 1.37 us -> 11.2 us  [swap(): return lax.ppermute(a, AXES, [(i, i ^ bits) for i in range(128)])]
    pallas_call x1, Pallas kernels: 6.23 us -> 1.7 us  [append(): pl.pallas_call(append_kernel, out_shape=[jax.ShapeDtypeStruct(b.shape, b....]
    ppermute x14 -> x13, starting transfers between devices: 24.9 us -> 21.4 us  [move(): return lax.ppermute(a, AXES, pairs)]
    pallas_call x2 -> x1, Pallas kernels: 9.11 us -> 6.72 us  [pack(): pl.pallas_call(functools.partial(pack_kernel, n), out_shape=[jax.ShapeDty...]
    ppermute x5 -> x4, starting transfers between devices: 5.1 us -> 7.37 us  [swap(): return lax.ppermute(a, AXES, [(i, i ^ bits) for i in range(128)])]
    pallas_call x1, Pallas kernels: 11.5 us -> 13.6 us  [merge(): pl.pallas_call(merge_kernel, out_shape=[jax.ShapeDtypeStruct((8 * BLOCK,...]
  transfers between devices with their start and end apart: 22 -> 20, of which waited for: 11 -> 7; matrix products, arithmetic and copies ran while one was open for 4% -> 5% of each run, Pallas kernels for 31% -> 30%
where the time goes in v3:
time: 173 us; the launch traced here: 172 us
  waiting for transfers between devices  61.2 us (35%)
  Pallas kernels  52.1 us (30%)
  starting transfers between devices  28.9 us (17%)
  between operations  14.1 us (8%)
  other arithmetic  8.4 us (5%)
  local copies, waits for them, and re-layouts  7.46 us (4%)
    ppermute x13, waiting for transfers between devices, move(): return lax.ppermute(a, AXES, pairs)  50 us
    ppermute x13, starting transfers between devices, move(): return lax.ppermute(a, AXES, pairs)  21.4 us
    pallas_call x1, Pallas kernels, own_part(): pl.pallas_call(own_kernel, out_shape=[jax.ShapeDtypeStruct((4, TOK, WIDE)...  15.8 us
    pallas_call x1, Pallas kernels, partner_part(): pl.pallas_call(partner_kernel, out_shape=[send, send, send, jax.ShapeDtyp...  14.3 us
    pallas_call x1, Pallas kernels, merge(): pl.pallas_call(merge_kernel, out_shape=[jax.ShapeDtypeStruct((8 * BLOCK,...  13.6 us
    ppermute x4, waiting for transfers between devices, swap(): return lax.ppermute(a, AXES, [(i, i ^ bits) for i in range(128)])  11.2 us
    ppermute x4, starting transfers between devices, swap(): return lax.ppermute(a, AXES, [(i, i ^ bits) for i in range(128)])  7.37 us
    pallas_call x1, Pallas kernels, pack(): pl.pallas_call(functools.partial(pack_kernel, n), out_shape=[jax.ShapeDty...  6.72 us
  transfers between devices with their start and end apart: 20, of which 7 were waited for; matrix products, arithmetic and copies ran while one was open for 5% of the time, Pallas kernels for 30%

profile of v3, /device:TPU:0, one launch (start us, length us, event | category | flops | bytes accessed | tf_op | source)
XLA Modules:
  0.0 172.2 jit_solution(15871652084512847857)
XLA Ops:
  9.3 4.2 %collective-permute-start.2 = (bf16[1088,128]{1,0:T(8,128)(2,1)S(1)}, bf16[1088,128]{1,0:T(8,128)(2,1)S(1)}, u32[]{:S(2)}, u32[]{:S(2)}) collective-permute-start(bf16[1088,128]{1,0:T(8,128)(2,1)S(1)} %maximum_maximum_fusion), channel_id=1, source_target_pairs={{0,66},{1,67},{2,64},{3,65},{4,70},{5,71},{6,68},{7,69},{8,74},{9,... | collective-permute-start | bytes 835592 | tf_op jit(solution)/shard_map/ppermute | solution.py:31
  13.5 1.6 collective-permute-start
  15.7 6.7 %pack.1 = (bf16[2176,256]{1,0:T(8,128)(2,1)}, bf16[2176,256]{1,0:T(8,128)(2,1)}, bf16[2176,256]{1,0:T(8,128)(2,1)}, bf16[2048,256]{1,0:T(8,128)(2,1)}, bf16[2048...) custom-call(s32[7]{0:T(128)} %stack.115.idx, bf16[2048,2048]{1,0:T(8,128)(2,1)} %base.5), custom_call_target="tpu_custom_call" | custom-call | bytes 14680064 | tf_op jit(solution)/shard_map/pack/pallas_call | solution.py:86
  23.1 4.3 %collective-permute-done = bf16[1088,128]{1,0:T(8,128)(2,1)S(1)} collective-permute-done((bf16[1088,128]{1,0:T(8,128)(2,1)S(1)}, bf16[1088,128]{1,0:T(8,128)(2,1)S(1)}, u32[]{:S(2)}, u32[]{:S(2)}) %collective-permute-start) | collective-permute-done | bytes 278560 | tf_op jit(solution)/shard_map/ppermute | solution.py:31
  30.0 1.7 append.1
  31.7 1.6 collective-permute-start.3
  33.4 1.7 collective-permute-start.4
  35.0 2.0 %collective-permute-start.5 = (bf16[2176,256]{1,0:T(8,128)(2,1)}, bf16[2176,256]{1,0:T(8,128)(2,1)S(1)}, u32[]{:S(2)}, u32[]{:S(2)}) collective-permute-start(bf16[2176,256]{1,0:T(8,128)(2,1)} %get-tuple-element.42), channel_id=1, source_target_pairs={{0,32},{1,33},{2,34},{3,35},{4,36},{5,37},{6,38},{7,39},{8,40},{9,... | collective-permute-start | bytes 3342344 | tf_op jit(solution)/shard_map/ppermute | solution.py:27
  37.0 2.0 %collective-permute-start.7 = (bf16[2048,256]{1,0:T(8,128)(2,1)}, bf16[2048,256]{1,0:T(8,128)(2,1)}, u32[]{:S(2)}, u32[]{:S(2)}) collective-permute-start(bf16[2048,256]{1,0:T(8,128)(2,1)} %get-tuple-element.46), channel_id=1, source_target_pairs={{0,64},{1,65},{2,66},{3,67},{4,68},{5,69},{6,70},{7,71},{8,72},{9,... | collective-permute-start | bytes 3145736 | tf_op jit(solution)/shard_map/ppermute | solution.py:27
  39.0 1.6 collective-permute-start.6
  41.3 23.7 %collective-permute-done.7.h1 = bf16[2048,256]{1,0:T(8,128)(2,1)} collective-permute-done((bf16[2048,256]{1,0:T(8,128)(2,1)}, bf16[2048,256]{1,0:T(8,128)(2,1)}, u32[]{:S(2)}, u32[]{:S(2)}) %collective-permute-start.7) | collective-permute-done | bytes 1048608 | tf_op jit(solution)/shard_map/ppermute | solution.py:27
  64.9 19.6 %collective-permute-done.6.h2 = bf16[2048,256]{1,0:T(8,128)(2,1)} collective-permute-done((bf16[2048,256]{1,0:T(8,128)(2,1)}, bf16[2048,256]{1,0:T(8,128)(2,1)}, u32[]{:S(2)}, u32[]{:S(2)}) %collective-permute-start.6) | collective-permute-done | bytes 1048608 | tf_op jit(solution)/shard_map/ppermute | solution.py:27
  84.5 2.1 %collective-permute-start.8 = (bf16[2048,256]{1,0:T(8,128)(2,1)}, bf16[2048,256]{1,0:T(8,128)(2,1)}, u32[]{:S(2)}, u32[]{:S(2)}) collective-permute-start(bf16[2048,256]{1,0:T(8,128)(2,1)} %get-tuple-element.47), channel_id=1, source_target_pairs={{0,64},{1,65},{2,66},{3,67},{4,68},{5,69},{6,70},{7,71},{8,72},{9,... | collective-permute-start | bytes 3145736 | tf_op jit(solution)/shard_map/ppermute | solution.py:27
  87.3 2.6 %collective-permute-start.10 = (bf16[2048,256]{1,0:T(8,128)(2,1)}, bf16[2048,256]{1,0:T(8,128)(2,1)}, u32[]{:S(2)}, u32[]{:S(2)}) collective-permute-start(bf16[2048,256]{1,0:T(8,128)(2,1)} %collective-permute-done.6.h2), channel_id=1, source_target_pairs={{0,48},{1,49},{2,50},{3,51},{4,52},{5,53},{6,54},{7,55},{8,56},{9,... | collective-permute-start | bytes 3145736 | tf_op jit(solution)/shard_map/ppermute | solution.py:27
  91.9 15.8 %own_part.1 = (f32[4,1024,256]{2,1,0:T(8,128)}, f32[1024,64]{1,0:T(8,128)}) custom-call(s32[13]{0:T(128)} %stack.113.idx, bf16[8,2176,128]{2,1,0:T(8,128)(2,1)} %bitcast.81, bf16[2048,2048]{1,0:T(8,128)(2,1)} %base.5), custom_call_target="tpu_custom_call" | custom-call | flops 5368709120 | bytes 13631488 | tf_op jit(solution)/shard_map/own_part/pallas_call | solution.py:160
  107.7 1.7 collective-permute-start.13
  109.4 6.3 %collective-permute-done.13 = bf16[4,256,128]{2,1,0:T(8,128)(2,1)S(1)} collective-permute-done((bf16[4,256,128]{2,1,0:T(8,128)(2,1)S(1)}, bf16[4,256,128]{2,1,0:T(8,128)(2,1)S(1)}, u32[]{:S(2)}, u32[]{:S(2)}) %collective-permute-start.13) | collective-permute-done | bytes 262176 | tf_op jit(solution)/shard_map/ppermute | solution.py:31
  116.6 1.7 collective-permute-start.11
  120.0 14.3 %partner_part.1 = (bf16[1024,256]{1,0:T(8,128)(2,1)}, bf16[1024,256]{1,0:T(8,128)(2,1)}, bf16[1024,256]{1,0:T(8,128)(2,1)}, bf16[1024,64]{1,0:T(8,128)(2,1)}) custom-call(s32[13]{0:T(128)} %stack.113.idx, bf16[8,2176,128]{2,1,0:T(8,128)(2,1)} %bitcast.70, bf16[2048,256]{1,0:T(8,128)(2,1)} %collective-permute-done.7.h1, ...), custom_call_target="tpu_custom_call" | custom-call | flops 4294967296 | bytes 12582912 | tf_op jit(solution)/shard_map/partner_part/pallas_call | solution.py:200
  134.7 3.0 %collective-permute-start.15 = (bf16[1024,256]{1,0:T(8,128)(2,1)}, bf16[1024,256]{1,0:T(8,128)(2,1)S(1)}, u32[]{:S(2)}, u32[]{:S(2)}) collective-permute-start(bf16[1024,256]{1,0:T(8,128)(2,1)} %get-tuple-element.63), channel_id=1, source_target_pairs={{0,48},{1,49},{2,50},{3,51},{4,52},{5,53},{6,54},{7,55},{8,56},{9,... | collective-permute-start | bytes 1572872 | tf_op jit(solution)/shard_map/ppermute | solution.py:27
  141.9 3.9 %collective-permute-done.12.refs_6_ = bf16[2048,256]{1,0:T(8,128)(2,1)S(1)} collective-permute-done((bf16[2048,256]{1,0:T(8,128)(2,1)}, bf16[2048,256]{1,0:T(8,128)(2,1)S(1)}, u32[]{:S(2)}, u32[]{:S(2)}) %collective-permute-start.12) | collective-permute-done | bytes 1048608 | tf_op jit(solution)/shard_map/ppermute | solution.py:27
  146.8 13.6 %merge.1 = (bf16[16384,256]{1,0:T(8,128)(2,1)}, f32[1,256]{1,0:T(1,128)}, f32[1024,256]{1,0:T(8,128)}) custom-call(s32[13]{0:T(128)} %stack.113.idx, bf16[2048,2048]{1,0:T(8,128)(2,1)} %base.5, bf16[2048,256]{1,0:T(8,128)(2,1)} %copy-done.4, bf16[2176,256]{1,0:T(8,128)(2,1)} %copy-done, bf16[2048,256]{1,0:T(8,128)(2,1)} %collective-permute-done.9.refs_2_, ...), custom_call_target="tpu_custom_call" | custom-call | flops 1073741824 | bytes 18874368 | tf_op jit(solution)/shard_map/merge/pallas_call | solution.py:286
  160.4 2.8 %collective-permute-done.16 = bf16[1024,256]{1,0:T(8,128)(2,1)} collective-permute-done((bf16[1024,256]{1,0:T(8,128)(2,1)}, bf16[1024,256]{1,0:T(8,128)(2,1)}, u32[]{:S(2)}, u32[]{:S(2)}) %collective-permute-start.16) | collective-permute-done | bytes 524320 | tf_op jit(solution)/shard_map/ppermute | solution.py:27
  163.3 2.4 %fusion = bf16[1,1024,256]{2,1,0:T(8,128)(2,1)} fusion(bf16[1024,256]{1,0:T(8,128)(2,1)} %collective-permute-done.16, bf16[1024,256]{1,0:T(8,128)(2,1)S(1)} %collective-permute-done.15, f32[1024,256]{1,0:T(8,128)} %get-tuple-element.61, bf16[1024,256]{1,0:T(8,128)(2,1)S(1)} %collective-permute-done.14, f32[256]{0:T(256)} %bitcast.79), kind=kLoop, calls=%fused_computation.3 | loop fusion | flops 2097152 | bytes 3146752 | tf_op jit(solution)/shard_map/broadcast_in_dim | solution.py:378
  (95 shorter events, 17.5 us)
Async XLA Ops:
  7.2 84.7 %all-gather.7.cloned.1.call-start = ((), (), s32[]{:S(2)}) async-start(), calls=%async_computation | async-start | bytes 5013504 | tf_op jit(solution)/shard_map/all_gather | solution.py:36
  9.3 13.1 %collective-permute-start.2 = (bf16[1088,128]{1,0:T(8,128)(2,1)S(1)}, bf16[1088,128]{1,0:T(8,128)(2,1)S(1)}, u32[]{:S(2)}, u32[]{:S(2)}) collective-permute-start(bf16[1088,128]{1,0:T(8,128)(2,1)S(1)} %maximum_maximum_fusion), channel_id=1, source_target_pairs={{0,66},{1,67},{2,64},{3,65},{4,70},{5,71},{6,68},{7,69},{8,74},{9,... | collective-permute-start | bytes 835592 | tf_op jit(solution)/shard_map/ppermute | solution.py:31
  13.5 9.6 %collective-permute-start.1 = (bf16[1088,128]{1,0:T(8,128)(2,1)S(1)}, bf16[1088,128]{1,0:T(8,128)(2,1)S(1)}, u32[]{:S(2)}, u32[]{:S(2)}) collective-permute-start(bf16[1088,128]{1,0:T(8,128)(2,1)S(1)} %maximum_maximum_fusion), channel_id=1, source_target_pairs={{0,2},{1,3},{2,0},{3,1},{4,6},{5,7},{6,4},{7,5},{8,10},{9,11},{10,... | collective-permute-start | bytes 835592 | tf_op jit(solution)/shard_map/ppermute | solution.py:31
  13.5 13.9 %collective-permute-start = (bf16[1088,128]{1,0:T(8,128)(2,1)S(1)}, bf16[1088,128]{1,0:T(8,128)(2,1)S(1)}, u32[]{:S(2)}, u32[]{:S(2)}) collective-permute-start(bf16[1088,128]{1,0:T(8,128)(2,1)S(1)} %maximum_maximum_fusion), channel_id=1, source_target_pairs={{0,64},{1,65},{2,66},{3,67},{4,68},{5,69},{6,70},{7,71},{8,72},{9,... | collective-permute-start | bytes 835592 | tf_op jit(solution)/shard_map/ppermute | solution.py:31
  28.3 91.7 %all-gather.11.cloned.1.call-start = ((), (), s32[]{:S(2)}) async-start(), calls=%async_computation.2 | async-start | bytes 5013504 | tf_op jit(solution)/shard_map/all_gather | solution.py:36
  29.3 116.5 %all-gather.9.cloned.1.call-start = ((), (), s32[]{:S(2)}) async-start(), calls=%async_computation.1 | async-start | bytes 2359296 | tf_op jit(solution)/shard_map/all_gather | solution.py:36
  31.7 52.8 %collective-permute-start.3 = (bf16[2176,256]{1,0:T(8,128)(2,1)}, bf16[2176,256]{1,0:T(8,128)(2,1)S(1)}, u32[]{:S(2)}, u32[]{:S(2)}) collective-permute-start(bf16[2176,256]{1,0:T(8,128)(2,1)} %get-tuple-element.40), channel_id=1, source_target_pairs={{0,16},{1,17},{2,18},{3,19},{4,20},{5,21},{6,22},{7,23},{8,24},{9,... | collective-permute-start | bytes 3342344 | tf_op jit(solution)/shard_map/ppermute | solution.py:27
  33.4 51.1 %collective-permute-start.4 = (bf16[2176,256]{1,0:T(8,128)(2,1)}, bf16[2176,256]{1,0:T(8,128)(2,1)S(1)}, u32[]{:S(2)}, u32[]{:S(2)}) collective-permute-start(bf16[2176,256]{1,0:T(8,128)(2,1)} %get-tuple-element.41), channel_id=1, source_target_pairs={{0,48},{1,49},{2,50},{3,51},{4,52},{5,53},{6,54},{7,55},{8,56},{9,... | collective-permute-start | bytes 3342344 | tf_op jit(solution)/shard_map/ppermute | solution.py:27
  35.0 49.5 %collective-permute-start.5 = (bf16[2176,256]{1,0:T(8,128)(2,1)}, bf16[2176,256]{1,0:T(8,128)(2,1)S(1)}, u32[]{:S(2)}, u32[]{:S(2)}) collective-permute-start(bf16[2176,256]{1,0:T(8,128)(2,1)} %get-tuple-element.42), channel_id=1, source_target_pairs={{0,32},{1,33},{2,34},{3,35},{4,36},{5,37},{6,38},{7,39},{8,40},{9,... | collective-permute-start | bytes 3342344 | tf_op jit(solution)/shard_map/ppermute | solution.py:27
  37.0 27.9 %collective-permute-start.7 = (bf16[2048,256]{1,0:T(8,128)(2,1)}, bf16[2048,256]{1,0:T(8,128)(2,1)}, u32[]{:S(2)}, u32[]{:S(2)}) collective-permute-start(bf16[2048,256]{1,0:T(8,128)(2,1)} %get-tuple-element.46), channel_id=1, source_target_pairs={{0,64},{1,65},{2,66},{3,67},{4,68},{5,69},{6,70},{7,71},{8,72},{9,... | collective-permute-start | bytes 3145736 | tf_op jit(solution)/shard_map/ppermute | solution.py:27
  39.0 45.5 %collective-permute-start.6 = (bf16[2048,256]{1,0:T(8,128)(2,1)}, bf16[2048,256]{1,0:T(8,128)(2,1)}, u32[]{:S(2)}, u32[]{:S(2)}) collective-permute-start(bf16[2048,256]{1,0:T(8,128)(2,1)} %get-tuple-element.44), channel_id=1, source_target_pairs={{0,64},{1,65},{2,66},{3,67},{4,68},{5,69},{6,70},{7,71},{8,72},{9,... | collective-permute-start | bytes 3145736 | tf_op jit(solution)/shard_map/ppermute | solution.py:27
  84.5 23.2 %copy-start = (bf16[2176,256]{1,0:T(8,128)(2,1)}, bf16[2176,256]{1,0:T(8,128)(2,1)S(1)}, u32[]{:S(2)}) copy-start(bf16[2176,256]{1,0:T(8,128)(2,1)S(1)} %collective-permute-done.3.refs_1_) | copy-start | bytes 3342340
  84.5 23.2 %copy-start.1 = (bf16[2176,256]{1,0:T(8,128)(2,1)}, bf16[2176,256]{1,0:T(8,128)(2,1)S(1)}, u32[]{:S(2)}) copy-start(bf16[2176,256]{1,0:T(8,128)(2,1)S(1)} %collective-permute-done.4.refs_3_) | copy-start | bytes 3342340
  84.5 23.2 %copy-start.2 = (bf16[2176,256]{1,0:T(8,128)(2,1)}, bf16[2176,256]{1,0:T(8,128)(2,1)S(1)}, u32[]{:S(2)}) copy-start(bf16[2176,256]{1,0:T(8,128)(2,1)S(1)} %collective-permute-done.5.refs_5_) | copy-start | bytes 3342340
  84.5 31.9 %collective-permute-start.8 = (bf16[2048,256]{1,0:T(8,128)(2,1)}, bf16[2048,256]{1,0:T(8,128)(2,1)}, u32[]{:S(2)}, u32[]{:S(2)}) collective-permute-start(bf16[2048,256]{1,0:T(8,128)(2,1)} %get-tuple-element.47), channel_id=1, source_target_pairs={{0,64},{1,65},{2,66},{3,67},{4,68},{5,69},{6,70},{7,71},{8,72},{9,... | collective-permute-start | bytes 3145736 | tf_op jit(solution)/shard_map/ppermute | solution.py:27
  86.6 29.8 %collective-permute-start.9 = (bf16[2048,256]{1,0:T(8,128)(2,1)}, bf16[2048,256]{1,0:T(8,128)(2,1)}, u32[]{:S(2)}, u32[]{:S(2)}) collective-permute-start(bf16[2048,256]{1,0:T(8,128)(2,1)} %collective-permute-done.7.h1), channel_id=1, source_target_pairs={{0,16},{1,17},{2,18},{3,19},{4,20},{5,21},{6,22},{7,23},{8,24},{9,... | collective-permute-start | bytes 3145736 | tf_op jit(solution)/shard_map/ppermute | solution.py:27
  87.3 29.2 %collective-permute-start.10 = (bf16[2048,256]{1,0:T(8,128)(2,1)}, bf16[2048,256]{1,0:T(8,128)(2,1)}, u32[]{:S(2)}, u32[]{:S(2)}) collective-permute-start(bf16[2048,256]{1,0:T(8,128)(2,1)} %collective-permute-done.6.h2), channel_id=1, source_target_pairs={{0,48},{1,49},{2,50},{3,51},{4,52},{5,53},{6,54},{7,55},{8,56},{9,... | collective-permute-start | bytes 3145736 | tf_op jit(solution)/shard_map/ppermute | solution.py:27
  91.8 15.8 %copy-start.7 = (bf16[4,256,128]{2,1,0:T(8,128)(2,1)S(1)}, bf16[4,256,128]{2,1,0:T(8,128)(2,1)}, u32[]{:S(2)}) copy-start(bf16[4,256,128]{2,1,0:T(8,128)(2,1)} %pad_maximum_fusion.2) | copy-start | bytes 786436
  107.7 8.0 %collective-permute-start.13 = (bf16[4,256,128]{2,1,0:T(8,128)(2,1)S(1)}, bf16[4,256,128]{2,1,0:T(8,128)(2,1)S(1)}, u32[]{:S(2)}, u32[]{:S(2)}) collective-permute-start(bf16[4,256,128]{2,1,0:T(8,128)(2,1)S(1)} %copy-done.7), channel_id=1, source_target_pairs={{0,64},{1,65},{2,66},{3,67},{4,68},{5,69},{6,70},{7,71},{8,72},{9,... | collective-permute-start | bytes 786440 | tf_op jit(solution)/shard_map/ppermute | solution.py:31
  116.6 25.4 %collective-permute-start.11 = (bf16[2048,256]{1,0:T(8,128)(2,1)}, bf16[2048,256]{1,0:T(8,128)(2,1)S(1)}, u32[]{:S(2)}, u32[]{:S(2)}) collective-permute-start(bf16[2048,256]{1,0:T(8,128)(2,1)} %get-tuple-element.52), channel_id=1, source_target_pairs={{0,64},{1,65},{2,66},{3,67},{4,68},{5,69},{6,70},{7,71},{8,72},{9,... | collective-permute-start | bytes 3145736 | tf_op jit(solution)/shard_map/ppermute | solution.py:27
  118.2 27.6 %collective-permute-start.12 = (bf16[2048,256]{1,0:T(8,128)(2,1)}, bf16[2048,256]{1,0:T(8,128)(2,1)S(1)}, u32[]{:S(2)}, u32[]{:S(2)}) collective-permute-start(bf16[2048,256]{1,0:T(8,128)(2,1)} %collective-permute-done.8.h3), channel_id=1, source_target_pairs={{0,32},{1,33},{2,34},{3,35},{4,36},{5,37},{6,38},{7,39},{8,40},{9,... | collective-permute-start | bytes 3145736 | tf_op jit(solution)/shard_map/ppermute | solution.py:27
  134.3 26.1 %collective-permute-start.14 = (bf16[1024,256]{1,0:T(8,128)(2,1)}, bf16[1024,256]{1,0:T(8,128)(2,1)S(1)}, u32[]{:S(2)}, u32[]{:S(2)}) collective-permute-start(bf16[1024,256]{1,0:T(8,128)(2,1)} %get-tuple-element.62), channel_id=1, source_target_pairs={{0,16},{1,17},{2,18},{3,19},{4,20},{5,21},{6,22},{7,23},{8,24},{9,... | collective-permute-start | bytes 1572872 | tf_op jit(solution)/shard_map/ppermute | solution.py:27
  134.7 25.8 %collective-permute-start.15 = (bf16[1024,256]{1,0:T(8,128)(2,1)}, bf16[1024,256]{1,0:T(8,128)(2,1)S(1)}, u32[]{:S(2)}, u32[]{:S(2)}) collective-permute-start(bf16[1024,256]{1,0:T(8,128)(2,1)} %get-tuple-element.63), channel_id=1, source_target_pairs={{0,48},{1,49},{2,50},{3,51},{4,52},{5,53},{6,54},{7,55},{8,56},{9,... | collective-permute-start | bytes 1572872 | tf_op jit(solution)/shard_map/ppermute | solution.py:27
  137.6 25.6 %collective-permute-start.16 = (bf16[1024,256]{1,0:T(8,128)(2,1)}, bf16[1024,256]{1,0:T(8,128)(2,1)}, u32[]{:S(2)}, u32[]{:S(2)}) collective-permute-start(bf16[1024,256]{1,0:T(8,128)(2,1)} %get-tuple-element.64), channel_id=1, source_target_pairs={{0,32},{1,33},{2,34},{3,35},{4,36},{5,37},{6,38},{7,39},{8,40},{9,... | collective-permute-start | bytes 1572872 | tf_op jit(solution)/shard_map/ppermute | solution.py:27
  (11 other events, 68.5 us)
Sparse Core Ops, SparseCore 0:
  28.4 34.3 all-gather.6
  64.5 33.1 all-gather.10
  116.6 22.8 all-gather.8

commit v4 on v3

--- a/solution.py
+++ b/solution.py
@@ -95,8 +95,11 @@
     )(jnp.stack(places), base)
 
 
-def append_kernel(left, beside, right, a1, a2, a3, o1, o2, o3, sem):
+def join_kernel(left, right, small, beside, partner, beside_partner, a1, a2, a3, o1, o2, o3, own, par, sem):
     copies = []
+    for out, parts in ((own, (small, beside)), (par, (partner, beside_partner))):
+        for h in range(2):
+            copies.append(pltpu.make_async_copy(parts[h], out.at[pl.ds(h * PART, PART), :], sem))
     for o in (o1, o2, o3):
         for src, row, lane in ((left, 0, 0), (beside.at[pl.ds(TOK, 64), :], 64, 0), (right, 0, 128)):
             dst = o.at[pl.ds(BLOCK + row, src.shape[0]), pl.ds(lane, 128)]
@@ -106,18 +109,19 @@
     wait_all(copies)
 
 
-def append(left, beside, right, blocks):
-    return pl.pallas_call(
-        append_kernel,
-        out_shape=[jax.ShapeDtypeStruct(b.shape, b.dtype) for b in blocks],
-        in_specs=specs("vvvhhh"),
-        out_specs=specs("hhh"),
+def join(left, right, small, beside, partner, beside_partner, blocks):
+    pair = jax.ShapeDtypeStruct((2 * PART, 128), BF16)
+    return pl.pallas_call(
+        join_kernel,
+        out_shape=[jax.ShapeDtypeStruct(b.shape, b.dtype) for b in blocks] + [pair, pair],
+        in_specs=specs("vvvvvvhhh"),
+        out_specs=specs("hhhhh"),
         scratch_shapes=[pltpu.SemaphoreType.DMA],
-        input_output_aliases={3: 0, 4: 1, 5: 2},
-        compiler_params=params(56),
-        cost_estimate=pl.CostEstimate(flops=0, bytes_accessed=MIB, transcendentals=0),
-        name="append",
-    )(left, beside, right, *blocks)
+        input_output_aliases={6: 0, 7: 1, 8: 2},
+        compiler_params=params(56),
+        cost_estimate=pl.CostEstimate(flops=0, bytes_accessed=3 * MIB, transcendentals=0),
+        name="join",
+    )(left, right, small, beside, partner, beside_partner, *blocks)
 
 
 def wait_all(copies):
@@ -189,7 +193,7 @@
     t = (own_t[...] + dot(par[...], factor)).astype(BF16)
     t_ref[...] = t
     for i, o in enumerate((o1, o2, o3)):
-        right = r_ref[:, pl.ds(pl.multiple_of(idx[1 + i] * WIDE, WIDE), WIDE)]
+        right = r_ref[:, pl.ds(pl.multiple_of(idx[1 + i] % 4 * WIDE, WIDE), WIDE)]
         halves[i].wait()
         parts[i].wait()
         o[...] = (dot(par[...], w[i]) + dot(t, right) + part[i]).astype(BF16)
@@ -315,8 +319,8 @@
         return ((zh + dz) % 2) * 4 + (y + dy) % 4
 
     left = jnp.concatenate([factor_left[:64], factor_left[64:]], axis=1)
+    small = jnp.concatenate([prompt, left], axis=0)
     right = factor_right.reshape(8, 16, 128).transpose(1, 0, 2).reshape(128, 128)
-    small = jnp.concatenate([prompt, left], axis=0)
 
     partner, beside, beside_partner = swap(small, 64), swap(small, 2), swap(small, 66)
     relayed = {}
@@ -326,19 +330,18 @@
 
     wave = (partner, beside, beside_partner, packed[2])
     partner, beside, beside_partner, _ = lax.optimization_barrier(wave)
-    gathered = gather_x(jnp.concatenate([small, beside], axis=0))
-    gathered_partner = gather_x(jnp.concatenate([partner, beside_partner], axis=0))
     half = {d: move(after(packed_half[d], *wave), dz=1) for d in (-1, 1)}
-    factors = jnp.concatenate([left, beside[TOK:], right], axis=0)
-    straight = {}
-    for d, block in zip(SHIFTS, append(left, beside, right, [packed[d] for d in SHIFTS])):
-        straight[d] = move(block, dy=d)
-
-    wave = (*(straight[d] for d in SHIFTS), half[-1], half[1])
+    *blocks, prompts, prompts_partner = join(
+        left, right, small, beside, partner, beside_partner, [packed[d] for d in SHIFTS]
+    )
+    gathered, gathered_partner = gather_x(prompts), gather_x(prompts_partner)
+    straight = {d: move(block, dy=d) for d, block in zip(SHIFTS, blocks)}
+
+    wave = (half[-1], half[1])
     for d in (1, -1):
         relayed[d] = move(after(half[d], *wave), dy=d)
     half[2] = move(after(packed_half[2], *wave), dz=1)
-    got = [factors]
+    got = [jnp.concatenate([left, beside[TOK:], right], axis=0)]
     for d in SHIFTS:
         below = straight[d][BLOCK:]
         got.append(jnp.concatenate([below[:, :128], below[:, 128:]], axis=0))
@@ -347,7 +350,11 @@
     at_col = lax.axis_index("col").astype(jnp.int32)
     idx = jnp.stack([served_by(0, d) for d in order] + places + [at_col // 2 % 2])
     acc, own_t = own_part(idx, after(gathered, *wave), base)
-    got_partner = swap(after(got, *wave, own_t), 64)
+    def rights_for(half_of_row):
+        return lax.dynamic_slice_in_dim(got, 128 + half_of_row * 64, 64, 1)
+
+    to_partner = jnp.concatenate([got[:, :128], rights_for(1 - zh)], axis=1)
+    got_partner = swap(after(to_partner, *wave, own_t), 64)
 
     wave = (half[2], relayed[1], relayed[-1], own_t)
     half[0] = move(after(packed_half[0], *wave), dz=1)
@@ -355,15 +362,15 @@
     lefts = jnp.stack([got[:, :64], got_partner[:, :64], got[:, 64:128], got_partner[:, 64:128]]).reshape(1024, 128)
     lefts = gather_x(after(lefts, *wave))
 
-    rights = jnp.stack([jnp.stack([got[j, 128:], got_partner[j, 128:]]) for j in (0, 2, 3, 1)])
+    rights = jnp.stack([jnp.stack([rights_for(zh)[j], got_partner[j, 128:]]) for j in (0, 2, 3, 1)])
     rights = lax.dynamic_slice_in_dim(jnp.concatenate([rights, rights], axis=0), (4 - y) % 4, 4, 0)
     rights = lax.dynamic_slice_in_dim(jnp.concatenate([rights, rights[:, :1]], axis=1), zh, 2, 1)
-    rights = rights.reshape(4, 2, 16, 8, 128).transpose(1, 0, 3, 2, 4).reshape(64, 2048)
+    rights = rights.reshape(4, 2, 8, 8, 128).transpose(1, 0, 3, 2, 4).reshape(64, 1024)
 
     *sends, t = partner_part(idx, gathered_partner, [half[d] for d in SHIFTS], rights, own_t, acc)
     sums = [move(s, dy=d) for s, d in zip(sends, SHIFTS)]
 
-    right_mine = lax.dynamic_slice(rights, (0, row * WIDE), (64, WIDE))
+    right_mine = lax.dynamic_slice(rights, (0, y * WIDE), (64, WIDE))
     rr = jnp.pad(right_mine, ((0, 64), (0, WIDE))) + jnp.pad(right_mine, ((64, 0), (WIDE, 0)))
     mag = lax.dynamic_slice(magnitude, (row * WIDE,), (WIDE,))[None]
     blocks = [half[0]]
@@ -373,8 +380,7 @@
         idx, base, blocks, lefts, gathered_partner, acc, rr, mag, t, right_mine
     )
 
-    for s in sums:
-        product = product + s.astype(F32)
+    product = lax.optimization_barrier(product + sums[0].astype(F32) + sums[1].astype(F32)) + sums[2].astype(F32)
     return serving[None], (product * scale).astype(BF16)[None]
 
 

time: 173 us -> 170 us (0.983)
  waiting for transfers between devices: 61.2 us -> 58.5 us
    ppermute x13, waiting for transfers between devices: 50 us -> 47.7 us  [move(): return lax.ppermute(a, AXES, pairs)]
    concatenate x2 -> x1, other arithmetic: 1.82 us -> 0.02 us  [shards(): to_partner = jnp.concatenate([got[:, :128], rights_for(1 - zh)], axis=1)]
where the time goes in v4:
time: 170 us
  waiting for transfers between devices  58.5 us (34%)
  Pallas kernels  52.5 us (31%)
  starting transfers between devices  30 us (18%)
  between operations  14.1 us (8%)
  local copies, waits for them, and re-layouts  7.82 us (5%)
  other arithmetic  6.75 us (4%)
    ppermute x13, waiting for transfers between devices, move(): return lax.ppermute(a, AXES, pairs)  47.7 us
    ppermute x13, starting transfers between devices, move(): return lax.ppermute(a, AXES, pairs)  22.5 us
    pallas_call x1, Pallas kernels, own_part(): pl.pallas_call(own_kernel, out_shape=[jax.ShapeDtypeStruct((4, TOK, WIDE)...  15.7 us
    pallas_call x1, Pallas kernels, partner_part(): pl.pallas_call(partner_kernel, out_shape=[send, send, send, jax.ShapeDtyp...  14.2 us
    pallas_call x1, Pallas kernels, merge(): pl.pallas_call(merge_kernel, out_shape=[jax.ShapeDtypeStruct((8 * BLOCK,...  13.7 us
    ppermute x4, waiting for transfers between devices, swap(): return lax.ppermute(a, AXES, [(i, i ^ bits) for i in range(128)])  9.99 us
    ppermute x4, starting transfers between devices, swap(): return lax.ppermute(a, AXES, [(i, i ^ bits) for i in range(128)])  7.38 us
    pallas_call x1, Pallas kernels, pack(): pl.pallas_call(functools.partial(pack_kernel, n), out_shape=[jax.ShapeDty...  6.59 us
  transfers between devices with their start and end apart: 20, of which 7 were waited for; matrix products, arithmetic and copies ran while one was open for 5% of the time, Pallas kernels for 30%

profile of v4, /device:TPU:0, one launch (start us, length us, event | category | flops | bytes accessed | tf_op | source)
XLA Modules:
  0.0 169.6 jit_solution(3960887466738052802)
XLA Ops:
  9.3 4.2 %collective-permute-start.2 = (bf16[1088,128]{1,0:T(8,128)(2,1)S(1)}, bf16[1088,128]{1,0:T(8,128)(2,1)S(1)}, u32[]{:S(2)}, u32[]{:S(2)}) collective-permute-start(bf16[1088,128]{1,0:T(8,128)(2,1)S(1)} %maximum_maximum_fusion.small), channel_id=1, source_target_pairs={{0,66},{1,67},{2,64},{3,65},{4,70},{5,71},{6,68},{7,69},{8,74},{9,... | collective-permute-start | bytes 835592 | tf_op jit(solution)/shard_map/ppermute | solution.py:31
  15.8 6.6 %pack.1 = (bf16[2176,256]{1,0:T(8,128)(2,1)}, bf16[2176,256]{1,0:T(8,128)(2,1)}, bf16[2176,256]{1,0:T(8,128)(2,1)}, bf16[2048,256]{1,0:T(8,128)(2,1)}, bf16[2048...) custom-call(s32[7]{0:T(128)} %stack.115.idx, bf16[2048,2048]{1,0:T(8,128)(2,1)} %base.5), custom_call_target="tpu_custom_call" | custom-call | bytes 14680064 | tf_op jit(solution)/shard_map/pack/pallas_call | solution.py:86
  23.1 4.3 %collective-permute-done.partner = bf16[1088,128]{1,0:T(8,128)(2,1)S(1)} collective-permute-done((bf16[1088,128]{1,0:T(8,128)(2,1)S(1)}, bf16[1088,128]{1,0:T(8,128)(2,1)S(1)}, u32[]{:S(2)}, u32[]{:S(2)}) %collective-permute-start) | collective-permute-done | bytes 278560 | tf_op jit(solution)/shard_map/ppermute | solution.py:31
  28.1 2.3 %join.1 = (bf16[2176,256]{1,0:T(8,128)(2,1)}, bf16[2176,256]{1,0:T(8,128)(2,1)}, bf16[2176,256]{1,0:T(8,128)(2,1)}, bf16[2176,128]{1,0:T(8,128)(2,1)}, bf16[2176,128]{1,0:T(8,128)(2,1)}) custom-call(bf16[64,128]{1,0:T(8,128)(2,1)} %pad_maximum_fusion.3.left, bf16[128,128]{1,0:T(8,128)(2,1)} %bitcast.76, ...), custom_call_target="tpu_custom_call", output_to_operand_aliasing={{0}: (6, {}), {1}: (7, {}), {2}: (8, {})} | custom-call | bytes 3145728 | tf_op jit(solution)/shard_map/join/pallas_call | solution.py:114
  31.3 3.3 %collective-permute-start.11 = (bf16[2176,256]{1,0:T(8,128)(2,1)}, bf16[2176,256]{1,0:T(8,128)(2,1)S(1)}, u32[]{:S(2)}, u32[]{:S(2)}) collective-permute-start(bf16[2176,256]{1,0:T(8,128)(2,1)} %get-tuple-element.57), channel_id=1, source_target_pairs={{0,32},{1,33},{2,34},{3,35},{4,36},{5,37},{6,38},{7,39},{8,40},{9,... | collective-permute-start | bytes 3342344 | tf_op jit(solution)/shard_map/ppermute | solution.py:27
  34.5 2.0 %collective-permute-start.4 = (bf16[2048,256]{1,0:T(8,128)(2,1)}, bf16[2048,256]{1,0:T(8,128)(2,1)}, u32[]{:S(2)}, u32[]{:S(2)}) collective-permute-start(bf16[2048,256]{1,0:T(8,128)(2,1)} %get-tuple-element.42), channel_id=1, source_target_pairs={{0,64},{1,65},{2,66},{3,67},{4,68},{5,69},{6,70},{7,71},{8,72},{9,... | collective-permute-start | bytes 3145736 | tf_op jit(solution)/shard_map/ppermute | solution.py:27
  36.5 1.6 collective-permute-start.3
  38.8 2.6 %collective-permute-start.10 = (bf16[2176,256]{1,0:T(8,128)(2,1)}, bf16[2176,256]{1,0:T(8,128)(2,1)}, u32[]{:S(2)}, u32[]{:S(2)}) collective-permute-start(bf16[2176,256]{1,0:T(8,128)(2,1)} %get-tuple-element.56), channel_id=1, source_target_pairs={{0,48},{1,49},{2,50},{3,51},{4,52},{5,53},{6,54},{7,55},{8,56},{9,... | collective-permute-start | bytes 3342344 | tf_op jit(solution)/shard_map/ppermute | solution.py:27
  42.1 20.4 %collective-permute-done.4.h1 = bf16[2048,256]{1,0:T(8,128)(2,1)} collective-permute-done((bf16[2048,256]{1,0:T(8,128)(2,1)}, bf16[2048,256]{1,0:T(8,128)(2,1)}, u32[]{:S(2)}, u32[]{:S(2)}) %collective-permute-start.4) | collective-permute-done | bytes 1048608 | tf_op jit(solution)/shard_map/ppermute | solution.py:27
  62.5 20.1 %collective-permute-done.3.h2 = bf16[2048,256]{1,0:T(8,128)(2,1)} collective-permute-done((bf16[2048,256]{1,0:T(8,128)(2,1)}, bf16[2048,256]{1,0:T(8,128)(2,1)}, u32[]{:S(2)}, u32[]{:S(2)}) %collective-permute-start.3) | collective-permute-done | bytes 1048608 | tf_op jit(solution)/shard_map/ppermute | solution.py:27
  82.6 2.0 %collective-permute-start.5 = (bf16[2048,256]{1,0:T(8,128)(2,1)}, bf16[2048,256]{1,0:T(8,128)(2,1)}, u32[]{:S(2)}, u32[]{:S(2)}) collective-permute-start(bf16[2048,256]{1,0:T(8,128)(2,1)} %get-tuple-element.43), channel_id=1, source_target_pairs={{0,64},{1,65},{2,66},{3,67},{4,68},{5,69},{6,70},{7,71},{8,72},{9,... | collective-permute-start | bytes 3145736 | tf_op jit(solution)/shard_map/ppermute | solution.py:27
  85.2 2.6 %collective-permute-start.7 = (bf16[2048,256]{1,0:T(8,128)(2,1)}, bf16[2048,256]{1,0:T(8,128)(2,1)}, u32[]{:S(2)}, u32[]{:S(2)}) collective-permute-start(bf16[2048,256]{1,0:T(8,128)(2,1)} %collective-permute-done.3.h2), channel_id=1, source_target_pairs={{0,48},{1,49},{2,50},{3,51},{4,52},{5,53},{6,54},{7,55},{8,56},{9,... | collective-permute-start | bytes 3145736 | tf_op jit(solution)/shard_map/ppermute | solution.py:27
  88.9 15.7 %own_part.1 = (f32[4,1024,256]{2,1,0:T(8,128)}, f32[1024,64]{1,0:T(8,128)}) custom-call(s32[13]{0:T(128)} %stack.113.idx, bf16[8,2176,128]{2,1,0:T(8,128)(2,1)} %bitcast.81, bf16[2048,2048]{1,0:T(8,128)(2,1)} %base.5), custom_call_target="tpu_custom_call" | custom-call | flops 5368709120 | bytes 13631488 | tf_op jit(solution)/shard_map/own_part/pallas_call | solution.py:164
  104.6 1.6 collective-permute-start.13
  106.2 5.6 %collective-permute-done.13 = bf16[4,192,128]{2,1,0:T(8,128)(2,1)S(1)} collective-permute-done((bf16[4,192,128]{2,1,0:T(8,128)(2,1)S(1)}, bf16[4,192,128]{2,1,0:T(8,128)(2,1)S(1)}, u32[]{:S(2)}, u32[]{:S(2)}) %collective-permute-start.13) | collective-permute-done | bytes 196640 | tf_op jit(solution)/shard_map/ppermute | solution.py:31
  112.7 1.6 collective-permute-start.8
  115.5 14.2 %partner_part.1 = (bf16[1024,256]{1,0:T(8,128)(2,1)}, bf16[1024,256]{1,0:T(8,128)(2,1)}, bf16[1024,256]{1,0:T(8,128)(2,1)}, bf16[1024,64]{1,0:T(8,128)(2,1)}) custom-call(s32[13]{0:T(128)} %stack.113.idx, bf16[8,2176,128]{2,1,0:T(8,128)(2,1)} %bitcast.70, bf16[2048,256]{1,0:T(8,128)(2,1)} %collective-permute-done.4.h1, ...), custom_call_target="tpu_custom_call" | custom-call | flops 4294967296 | bytes 12582912 | tf_op jit(solution)/shard_map/partner_part/pallas_call | solution.py:204
  129.8 1.6 collective-permute-start.14
  131.3 1.7 %collective-permute-start.15 = (bf16[1024,256]{1,0:T(8,128)(2,1)}, bf16[1024,256]{1,0:T(8,128)(2,1)S(1)}, u32[]{:S(2)}, u32[]{:S(2)}) collective-permute-start(bf16[1024,256]{1,0:T(8,128)(2,1)} %get-tuple-element.67), channel_id=1, source_target_pairs={{0,48},{1,49},{2,50},{3,51},{4,52},{5,53},{6,54},{7,55},{8,56},{9,... | collective-permute-start | bytes 1572872 | tf_op jit(solution)/shard_map/ppermute | solution.py:27
  134.4 2.0 %collective-permute-start.16 = (bf16[1024,256]{1,0:T(8,128)(2,1)}, bf16[1024,256]{1,0:T(8,128)(2,1)}, u32[]{:S(2)}, u32[]{:S(2)}) collective-permute-start(bf16[1024,256]{1,0:T(8,128)(2,1)} %get-tuple-element.68), channel_id=1, source_target_pairs={{0,32},{1,33},{2,34},{3,35},{4,36},{5,37},{6,38},{7,39},{8,40},{9,... | collective-permute-start | bytes 1572872 | tf_op jit(solution)/shard_map/ppermute | solution.py:27
  137.9 4.3 %collective-permute-done.12.refs_6_ = bf16[2048,256]{1,0:T(8,128)(2,1)S(1)} collective-permute-done((bf16[2048,256]{1,0:T(8,128)(2,1)}, bf16[2048,256]{1,0:T(8,128)(2,1)S(1)}, u32[]{:S(2)}, u32[]{:S(2)}) %collective-permute-start.12) | collective-permute-done | bytes 1048608 | tf_op jit(solution)/shard_map/ppermute | solution.py:27
  143.2 13.7 %merge.1 = (bf16[16384,256]{1,0:T(8,128)(2,1)}, f32[1,256]{1,0:T(1,128)}, f32[1024,256]{1,0:T(8,128)}) custom-call(s32[13]{0:T(128)} %stack.113.idx, bf16[2048,2048]{1,0:T(8,128)(2,1)} %base.5, bf16[2048,256]{1,0:T(8,128)(2,1)} %copy-done.4, bf16[2176,256]{1,0:T(8,128)(2,1)} %copy-done.1, bf16[2048,256]{1,0:T(8,128)(2,1)} %collective-permute-done.6.refs_2_, ...), custom_call_target="tpu_custom_call" | custom-call | flops 1073741824 | bytes 18874368 | tf_op jit(solution)/shard_map/merge/pallas_call | solution.py:290
  158.3 2.9 %collective-permute-done.16 = bf16[1024,256]{1,0:T(8,128)(2,1)} collective-permute-done((bf16[1024,256]{1,0:T(8,128)(2,1)}, bf16[1024,256]{1,0:T(8,128)(2,1)}, u32[]{:S(2)}, u32[]{:S(2)}) %collective-permute-start.16) | collective-permute-done | bytes 524320 | tf_op jit(solution)/shard_map/ppermute | solution.py:27
  161.2 2.0 %fusion = bf16[1,1024,256]{2,1,0:T(8,128)(2,1)} fusion(f32[1024,256]{1,0:T(8,128)S(1)} %convert_add_fusion, bf16[1024,256]{1,0:T(8,128)(2,1)} %collective-permute-done.16, f32[256]{0:T(256)S(1)} %bitcast.79), kind=kLoop, calls=%fused_computation.2 | loop fusion | flops 1048576 | bytes 2098176 | tf_op jit(solution)/shard_map/broadcast_in_dim | solution.py:384
  (88 shorter events, 16.7 us)
Async XLA Ops:
  7.2 81.7 %all-gather.7.cloned.1.call-start = ((), (), s32[]{:S(2)}) async-start(), calls=%async_computation | async-start | bytes 5013504 | tf_op jit(solution)/shard_map/all_gather | solution.py:36
  9.3 13.0 %copy-start.2 = (bf16[1088,128]{1,0:T(8,128)(2,1)}, bf16[1088,128]{1,0:T(8,128)(2,1)S(1)}, u32[]{:S(2)}) copy-start(bf16[1088,128]{1,0:T(8,128)(2,1)S(1)} %maximum_maximum_fusion.small) | copy-start | bytes 835588
  9.3 13.7 %collective-permute-start.2 = (bf16[1088,128]{1,0:T(8,128)(2,1)S(1)}, bf16[1088,128]{1,0:T(8,128)(2,1)S(1)}, u32[]{:S(2)}, u32[]{:S(2)}) collective-permute-start(bf16[1088,128]{1,0:T(8,128)(2,1)S(1)} %maximum_maximum_fusion.small), channel_id=1, source_target_pairs={{0,66},{1,67},{2,64},{3,65},{4,70},{5,71},{6,68},{7,69},{8,74},{9,... | collective-permute-start | bytes 835592 | tf_op jit(solution)/shard_map/ppermute | solution.py:31
  13.5 9.6 %collective-permute-start.1 = (bf16[1088,128]{1,0:T(8,128)(2,1)S(1)}, bf16[1088,128]{1,0:T(8,128)(2,1)S(1)}, u32[]{:S(2)}, u32[]{:S(2)}) collective-permute-start(bf16[1088,128]{1,0:T(8,128)(2,1)S(1)} %maximum_maximum_fusion.small), channel_id=1, source_target_pairs={{0,2},{1,3},{2,0},{3,1},{4,6},{5,7},{6,4},{7,5},{8,10},{9,11},{10,... | collective-permute-start | bytes 835592 | tf_op jit(solution)/shard_map/ppermute | solution.py:31
  13.5 13.9 %collective-permute-start = (bf16[1088,128]{1,0:T(8,128)(2,1)S(1)}, bf16[1088,128]{1,0:T(8,128)(2,1)S(1)}, u32[]{:S(2)}, u32[]{:S(2)}) collective-permute-start(bf16[1088,128]{1,0:T(8,128)(2,1)S(1)} %maximum_maximum_fusion.small), channel_id=1, source_target_pairs={{0,64},{1,65},{2,66},{3,67},{4,68},{5,69},{6,70},{7,71},{8,72},{9,... | collective-permute-start | bytes 835592 | tf_op jit(solution)/shard_map/ppermute | solution.py:31
  30.4 11.6 %slice-start = ((bf16[1088,128]{1,0:T(8,128)(2,1)}), bf16[64,128]{1,0:T(8,128)(2,1)S(1)}, s32[]{:S(2)}) async-start(bf16[1088,128]{1,0:T(8,128)(2,1)} %copy-done.6), calls=%async_computation.3 | async-start | bytes 32768 | tf_op jit(solution)/shard_map/slice | solution.py:344
  30.4 11.6 %copy-start.10 = (bf16[8,2048]{1,0:T(8,128)(2,1)S(1)}, bf16[8,2048]{1,0:T(8,128)(2,1)}, u32[]{:S(2)}) copy-start(bf16[8,2048]{1,0:T(8,128)(2,1)} %param.8) | copy-start | bytes 98308
  30.5 85.1 %all-gather.11.cloned.1.call-start = ((), (), s32[]{:S(2)}) async-start(), calls=%async_computation.2 | async-start | bytes 5013504 | tf_op jit(solution)/shard_map/all_gather | solution.py:36
  31.2 111.0 %all-gather.9.cloned.1.call-start = ((), (), s32[]{:S(2)}) async-start(), calls=%async_computation.1 | async-start | bytes 2359296 | tf_op jit(solution)/shard_map/all_gather | solution.py:36
  31.3 54.0 %collective-permute-start.11 = (bf16[2176,256]{1,0:T(8,128)(2,1)}, bf16[2176,256]{1,0:T(8,128)(2,1)S(1)}, u32[]{:S(2)}, u32[]{:S(2)}) collective-permute-start(bf16[2176,256]{1,0:T(8,128)(2,1)} %get-tuple-element.57), channel_id=1, source_target_pairs={{0,32},{1,33},{2,34},{3,35},{4,36},{5,37},{6,38},{7,39},{8,40},{9,... | collective-permute-start | bytes 3342344 | tf_op jit(solution)/shard_map/ppermute | solution.py:27
  34.5 27.9 %collective-permute-start.4 = (bf16[2048,256]{1,0:T(8,128)(2,1)}, bf16[2048,256]{1,0:T(8,128)(2,1)}, u32[]{:S(2)}, u32[]{:S(2)}) collective-permute-start(bf16[2048,256]{1,0:T(8,128)(2,1)} %get-tuple-element.42), channel_id=1, source_target_pairs={{0,64},{1,65},{2,66},{3,67},{4,68},{5,69},{6,70},{7,71},{8,72},{9,... | collective-permute-start | bytes 3145736 | tf_op jit(solution)/shard_map/ppermute | solution.py:27
  36.5 46.1 %collective-permute-start.3 = (bf16[2048,256]{1,0:T(8,128)(2,1)}, bf16[2048,256]{1,0:T(8,128)(2,1)}, u32[]{:S(2)}, u32[]{:S(2)}) collective-permute-start(bf16[2048,256]{1,0:T(8,128)(2,1)} %get-tuple-element.40), channel_id=1, source_target_pairs={{0,64},{1,65},{2,66},{3,67},{4,68},{5,69},{6,70},{7,71},{8,72},{9,... | collective-permute-start | bytes 3145736 | tf_op jit(solution)/shard_map/ppermute | solution.py:27
  38.1 49.7 %collective-permute-start.9 = (bf16[2176,256]{1,0:T(8,128)(2,1)S(1)}, bf16[2176,256]{1,0:T(8,128)(2,1)S(1)}, u32[]{:S(2)}, u32[]{:S(2)}) collective-permute-start(bf16[2176,256]{1,0:T(8,128)(2,1)S(1)} %copy-done.3), channel_id=1, source_target_pairs={{0,16},{1,17},{2,18},{3,19},{4,20},{5,21},{6,22},{7,23},{8,24},{9,... | collective-permute-start | bytes 3342344 | tf_op jit(solution)/shard_map/ppermute | solution.py:27
  38.8 49.1 %collective-permute-start.10 = (bf16[2176,256]{1,0:T(8,128)(2,1)}, bf16[2176,256]{1,0:T(8,128)(2,1)}, u32[]{:S(2)}, u32[]{:S(2)}) collective-permute-start(bf16[2176,256]{1,0:T(8,128)(2,1)} %get-tuple-element.56), channel_id=1, source_target_pairs={{0,48},{1,49},{2,50},{3,51},{4,52},{5,53},{6,54},{7,55},{8,56},{9,... | collective-permute-start | bytes 3342344 | tf_op jit(solution)/shard_map/ppermute | solution.py:27
  82.6 30.1 %collective-permute-start.5 = (bf16[2048,256]{1,0:T(8,128)(2,1)}, bf16[2048,256]{1,0:T(8,128)(2,1)}, u32[]{:S(2)}, u32[]{:S(2)}) collective-permute-start(bf16[2048,256]{1,0:T(8,128)(2,1)} %get-tuple-element.43), channel_id=1, source_target_pairs={{0,64},{1,65},{2,66},{3,67},{4,68},{5,69},{6,70},{7,71},{8,72},{9,... | collective-permute-start | bytes 3145736 | tf_op jit(solution)/shard_map/ppermute | solution.py:27
  84.6 28.1 %collective-permute-start.6 = (bf16[2048,256]{1,0:T(8,128)(2,1)}, bf16[2048,256]{1,0:T(8,128)(2,1)}, u32[]{:S(2)}, u32[]{:S(2)}) collective-permute-start(bf16[2048,256]{1,0:T(8,128)(2,1)} %collective-permute-done.4.h1), channel_id=1, source_target_pairs={{0,16},{1,17},{2,18},{3,19},{4,20},{5,21},{6,22},{7,23},{8,24},{9,... | collective-permute-start | bytes 3145736 | tf_op jit(solution)/shard_map/ppermute | solution.py:27
  85.2 27.4 %collective-permute-start.7 = (bf16[2048,256]{1,0:T(8,128)(2,1)}, bf16[2048,256]{1,0:T(8,128)(2,1)}, u32[]{:S(2)}, u32[]{:S(2)}) collective-permute-start(bf16[2048,256]{1,0:T(8,128)(2,1)} %collective-permute-done.3.h2), channel_id=1, source_target_pairs={{0,48},{1,49},{2,50},{3,51},{4,52},{5,53},{6,54},{7,55},{8,56},{9,... | collective-permute-start | bytes 3145736 | tf_op jit(solution)/shard_map/ppermute | solution.py:27
  87.8 16.8 %copy-start.1 = (bf16[2176,256]{1,0:T(8,128)(2,1)}, bf16[2176,256]{1,0:T(8,128)(2,1)S(1)}, u32[]{:S(2)}) copy-start(bf16[2176,256]{1,0:T(8,128)(2,1)S(1)} %collective-permute-done.9.refs_1_) | copy-start | bytes 3342340
  104.6 7.3 %collective-permute-start.13 = (bf16[4,192,128]{2,1,0:T(8,128)(2,1)S(1)}, bf16[4,192,128]{2,1,0:T(8,128)(2,1)S(1)}, u32[]{:S(2)}, u32[]{:S(2)}) collective-permute-start(bf16[4,192,128]{2,1,0:T(8,128)(2,1)S(1)} %pad_maximum_fusion.2), channel_id=1, source_target_pairs={{0,64},{1,65},{2,66},{3,67},{4,68},{5,69},{6,70},{7,71},{8,72},{9,... | collective-permute-start | bytes 589832 | tf_op jit(solution)/shard_map/ppermute | solution.py:31
  112.7 25.1 %collective-permute-start.8 = (bf16[2048,256]{1,0:T(8,128)(2,1)}, bf16[2048,256]{1,0:T(8,128)(2,1)S(1)}, u32[]{:S(2)}, u32[]{:S(2)}) collective-permute-start(bf16[2048,256]{1,0:T(8,128)(2,1)} %get-tuple-element.54), channel_id=1, source_target_pairs={{0,64},{1,65},{2,66},{3,67},{4,68},{5,69},{6,70},{7,71},{8,72},{9,... | collective-permute-start | bytes 3145736 | tf_op jit(solution)/shard_map/ppermute | solution.py:27
  114.4 27.9 %collective-permute-start.12 = (bf16[2048,256]{1,0:T(8,128)(2,1)}, bf16[2048,256]{1,0:T(8,128)(2,1)S(1)}, u32[]{:S(2)}, u32[]{:S(2)}) collective-permute-start(bf16[2048,256]{1,0:T(8,128)(2,1)} %collective-permute-done.5.h3), channel_id=1, source_target_pairs={{0,32},{1,33},{2,34},{3,35},{4,36},{5,37},{6,38},{7,39},{8,40},{9,... | collective-permute-start | bytes 3145736 | tf_op jit(solution)/shard_map/ppermute | solution.py:27
  129.8 27.1 %collective-permute-start.14 = (bf16[1024,256]{1,0:T(8,128)(2,1)}, bf16[1024,256]{1,0:T(8,128)(2,1)S(1)}, u32[]{:S(2)}, u32[]{:S(2)}) collective-permute-start(bf16[1024,256]{1,0:T(8,128)(2,1)} %get-tuple-element.66), channel_id=1, source_target_pairs={{0,16},{1,17},{2,18},{3,19},{4,20},{5,21},{6,22},{7,23},{8,24},{9,... | collective-permute-start | bytes 1572872 | tf_op jit(solution)/shard_map/ppermute | solution.py:27
  131.3 25.5 %collective-permute-start.15 = (bf16[1024,256]{1,0:T(8,128)(2,1)}, bf16[1024,256]{1,0:T(8,128)(2,1)S(1)}, u32[]{:S(2)}, u32[]{:S(2)}) collective-permute-start(bf16[1024,256]{1,0:T(8,128)(2,1)} %get-tuple-element.67), channel_id=1, source_target_pairs={{0,48},{1,49},{2,50},{3,51},{4,52},{5,53},{6,54},{7,55},{8,56},{9,... | collective-permute-start | bytes 1572872 | tf_op jit(solution)/shard_map/ppermute | solution.py:27
  134.4 26.7 %collective-permute-start.16 = (bf16[1024,256]{1,0:T(8,128)(2,1)}, bf16[1024,256]{1,0:T(8,128)(2,1)}, u32[]{:S(2)}, u32[]{:S(2)}) collective-permute-start(bf16[1024,256]{1,0:T(8,128)(2,1)} %get-tuple-element.68), channel_id=1, source_target_pairs={{0,32},{1,33},{2,34},{3,35},{4,36},{5,37},{6,38},{7,39},{8,40},{9,... | collective-permute-start | bytes 1572872 | tf_op jit(solution)/shard_map/ppermute | solution.py:27
  (9 other events, 35.3 us)
Sparse Core Ops, SparseCore 0:
  30.6 34.3 all-gather.6
  66.7 33.1 all-gather.10
  112.8 23.0 all-gather.8

commit v5 on v4

--- a/solution.py
+++ b/solution.py
@@ -85,7 +85,7 @@
     n = len(places)
     return pl.pallas_call(
         functools.partial(pack_kernel, n),
-        out_shape=[jax.ShapeDtypeStruct((BLOCK + EXTRA * (j < extra), WIDE), BF16) for j in range(n)],
+        out_shape=[jax.ShapeDtypeStruct((BLOCK + e, WIDE), BF16) for e in extra],
         in_specs=specs("sh"),
         out_specs=specs("h" * n),
         scratch_shapes=[pltpu.VMEM((n, BLOCK, WIDE), BF16), pltpu.SemaphoreType.DMA((2, n, 2))],
@@ -325,7 +325,7 @@
     partner, beside, beside_partner = swap(small, 64), swap(small, 2), swap(small, 66)
     relayed = {}
     places = [served_by(0, d) for d in SHIFTS] + [served_by(1, d) for d in SHIFTS + (0,)]
-    slices = pack(places, base, 3)
+    slices = pack(places, base, (EXTRA, EXTRA, EXTRA + 64) + (0,) * 3 + (16,))
     packed, packed_half = dict(zip(SHIFTS, slices)), dict(zip(SHIFTS + (0,), slices[3:]))
 
     wave = (partner, beside, beside_partner, packed[2])
@@ -343,7 +343,7 @@
     half[2] = move(after(packed_half[2], *wave), dz=1)
     got = [jnp.concatenate([left, beside[TOK:], right], axis=0)]
     for d in SHIFTS:
-        below = straight[d][BLOCK:]
+        below = straight[d][BLOCK : BLOCK + EXTRA]
         got.append(jnp.concatenate([below[:, :128], below[:, 128:]], axis=0))
     got = jnp.stack(got)
     places = [((zh + k) % 2) * 4 + (y - d) % 4 for d in order for k in range(2)]

time: 170 us -> 167 us (0.982)
  waiting for transfers between devices: 58.5 us -> 53.4 us
    ppermute x13, waiting for transfers between devices: 47.7 us -> 42.5 us  [move(): return lax.ppermute(a, AXES, pairs)]
  transfers between devices with their start and end apart: 20 -> 20, of which waited for: 7 -> 6; matrix products, arithmetic and copies ran while one was open for 5% -> 5% of each run, Pallas kernels for 30% -> 30%
where the time goes in v5:
time: 167 us; the launch traced here: 166 us
  waiting for transfers between devices  53.4 us (32%)
  Pallas kernels  52.5 us (31%)
  starting transfers between devices  31.6 us (19%)
  between operations  14.1 us (8%)
  local copies, waits for them, and re-layouts  7.98 us (5%)
  other arithmetic  6.76 us (4%)
    ppermute x13, waiting for transfers between devices, move(): return lax.ppermute(a, AXES, pairs)  42.5 us
    ppermute x13, starting transfers between devices, move(): return lax.ppermute(a, AXES, pairs)  24.1 us
    pallas_call x1, Pallas kernels, own_part(): pl.pallas_call(own_kernel, out_shape=[jax.ShapeDtypeStruct((4, TOK, WIDE)...  15.7 us
    pallas_call x1, Pallas kernels, partner_part(): pl.pallas_call(partner_kernel, out_shape=[send, send, send, jax.ShapeDtyp...  14.3 us
    pallas_call x1, Pallas kernels, merge(): pl.pallas_call(merge_kernel, out_shape=[jax.ShapeDtypeStruct((8 * BLOCK,...  13.6 us
    ppermute x4, waiting for transfers between devices, swap(): return lax.ppermute(a, AXES, [(i, i ^ bits) for i in range(128)])  10.1 us
    ppermute x4, starting transfers between devices, swap(): return lax.ppermute(a, AXES, [(i, i ^ bits) for i in range(128)])  7.37 us
    pallas_call x1, Pallas kernels, pack(): pl.pallas_call(functools.partial(pack_kernel, n), out_shape=[jax.ShapeDty...  6.58 us
  transfers between devices with their start and end apart: 20, of which 6 were waited for; matrix products, arithmetic and copies ran while one was open for 5% of the time, Pallas kernels for 30%

profile of v5, /device:TPU:0, one launch (start us, length us, event | category | flops | bytes accessed | tf_op | source)
XLA Modules:
  0.0 166.3 jit_solution(10717404846225100240)
XLA Ops:
  9.3 4.2 %collective-permute-start.2 = (bf16[1088,128]{1,0:T(8,128)(2,1)S(1)}, bf16[1088,128]{1,0:T(8,128)(2,1)S(1)}, u32[]{:S(2)}, u32[]{:S(2)}) collective-permute-start(bf16[1088,128]{1,0:T(8,128)(2,1)S(1)} %maximum_maximum_fusion.small), channel_id=1, source_target_pairs={{0,66},{1,67},{2,64},{3,65},{4,70},{5,71},{6,68},{7,69},{8,74},{9,... | collective-permute-start | bytes 835592 | tf_op jit(solution)/shard_map/ppermute | solution.py:31
  15.7 6.6 %pack.1 = (bf16[2176,256]{1,0:T(8,128)(2,1)}, bf16[2176,256]{1,0:T(8,128)(2,1)}, bf16[2240,256]{1,0:T(8,128)(2,1)}, bf16[2048,256]{1,0:T(8,128)(2,1)}, bf16[2048...) custom-call(s32[7]{0:T(128)} %stack.115.idx, bf16[2048,2048]{1,0:T(8,128)(2,1)} %base.5), custom_call_target="tpu_custom_call" | custom-call | bytes 14680064 | tf_op jit(solution)/shard_map/pack/pallas_call | solution.py:86
  23.1 4.3 %collective-permute-done.partner = bf16[1088,128]{1,0:T(8,128)(2,1)S(1)} collective-permute-done((bf16[1088,128]{1,0:T(8,128)(2,1)S(1)}, bf16[1088,128]{1,0:T(8,128)(2,1)S(1)}, u32[]{:S(2)}, u32[]{:S(2)}) %collective-permute-start) | collective-permute-done | bytes 278560 | tf_op jit(solution)/shard_map/ppermute | solution.py:31
  28.1 2.3 %join.1 = (bf16[2176,256]{1,0:T(8,128)(2,1)}, bf16[2176,256]{1,0:T(8,128)(2,1)}, bf16[2240,256]{1,0:T(8,128)(2,1)}, bf16[2176,128]{1,0:T(8,128)(2,1)}, bf16[2176,128]{1,0:T(8,128)(2,1)}) custom-call(bf16[64,128]{1,0:T(8,128)(2,1)} %pad_maximum_fusion.3.left, bf16[128,128]{1,0:T(8,128)(2,1)} %bitcast.76, ...), custom_call_target="tpu_custom_call", output_to_operand_aliasing={{0}: (6, {}), {1}: (7, {}), {2}: (8, {})} | custom-call | bytes 3145728 | tf_op jit(solution)/shard_map/join/pallas_call | solution.py:114
  31.3 1.6 collective-permute-start.9
  33.0 2.0 %collective-permute-start.4 = (bf16[2048,256]{1,0:T(8,128)(2,1)}, bf16[2048,256]{1,0:T(8,128)(2,1)}, u32[]{:S(2)}, u32[]{:S(2)}) collective-permute-start(bf16[2048,256]{1,0:T(8,128)(2,1)} %get-tuple-element.42), channel_id=1, source_target_pairs={{0,64},{1,65},{2,66},{3,67},{4,68},{5,69},{6,70},{7,71},{8,72},{9,... | collective-permute-start | bytes 3145736 | tf_op jit(solution)/shard_map/ppermute | solution.py:27
  36.5 1.7 collective-permute-start.10
  38.1 2.0 %collective-permute-start.11 = (bf16[2240,256]{1,0:T(8,128)(2,1)}, bf16[2240,256]{1,0:T(8,128)(2,1)S(1)}, u32[]{:S(2)}, u32[]{:S(2)}) collective-permute-start(bf16[2240,256]{1,0:T(8,128)(2,1)} %get-tuple-element.57), channel_id=1, source_target_pairs={{0,32},{1,33},{2,34},{3,35},{4,36},{5,37},{6,38},{7,39},{8,40},{9,... | collective-permute-start | bytes 3440648 | tf_op jit(solution)/shard_map/ppermute | solution.py:27
  40.9 20.0 %collective-permute-done.4.h1 = bf16[2048,256]{1,0:T(8,128)(2,1)} collective-permute-done((bf16[2048,256]{1,0:T(8,128)(2,1)}, bf16[2048,256]{1,0:T(8,128)(2,1)}, u32[]{:S(2)}, u32[]{:S(2)}) %collective-permute-start.4) | collective-permute-done | bytes 1048608 | tf_op jit(solution)/shard_map/ppermute | solution.py:27
  60.9 20.1 %collective-permute-done.3.h2 = bf16[2048,256]{1,0:T(8,128)(2,1)} collective-permute-done((bf16[2048,256]{1,0:T(8,128)(2,1)}, bf16[2048,256]{1,0:T(8,128)(2,1)}, u32[]{:S(2)}, u32[]{:S(2)}) %collective-permute-start.3) | collective-permute-done | bytes 1048608 | tf_op jit(solution)/shard_map/ppermute | solution.py:27
  81.0 2.0 %collective-permute-start.5 = (bf16[2048,256]{1,0:T(8,128)(2,1)}, bf16[2048,256]{1,0:T(8,128)(2,1)}, u32[]{:S(2)}, u32[]{:S(2)}) collective-permute-start(bf16[2048,256]{1,0:T(8,128)(2,1)} %get-tuple-element.43), channel_id=1, source_target_pairs={{0,64},{1,65},{2,66},{3,67},{4,68},{5,69},{6,70},{7,71},{8,72},{9,... | collective-permute-start | bytes 3145736 | tf_op jit(solution)/shard_map/ppermute | solution.py:27
  83.0 1.6 collective-permute-start.6
  84.6 1.7 %collective-permute-start.7 = (bf16[2048,256]{1,0:T(8,128)(2,1)}, bf16[2048,256]{1,0:T(8,128)(2,1)}, u32[]{:S(2)}, u32[]{:S(2)}) collective-permute-start(bf16[2048,256]{1,0:T(8,128)(2,1)} %collective-permute-done.3.h2), channel_id=1, source_target_pairs={{0,48},{1,49},{2,50},{3,51},{4,52},{5,53},{6,54},{7,55},{8,56},{9,... | collective-permute-start | bytes 3145736 | tf_op jit(solution)/shard_map/ppermute | solution.py:27
  87.2 15.7 %own_part.1 = (f32[4,1024,256]{2,1,0:T(8,128)}, f32[1024,64]{1,0:T(8,128)}) custom-call(s32[13]{0:T(128)} %stack.113.idx, bf16[8,2176,128]{2,1,0:T(8,128)(2,1)} %bitcast.81, bf16[2048,2048]{1,0:T(8,128)(2,1)} %base.5), custom_call_target="tpu_custom_call" | custom-call | flops 5368709120 | bytes 13631488 | tf_op jit(solution)/shard_map/own_part/pallas_call | solution.py:164
  103.0 1.6 collective-permute-start.13
  104.6 5.6 %collective-permute-done.13 = bf16[4,192,128]{2,1,0:T(8,128)(2,1)S(1)} collective-permute-done((bf16[4,192,128]{2,1,0:T(8,128)(2,1)S(1)}, bf16[4,192,128]{2,1,0:T(8,128)(2,1)S(1)}, u32[]{:S(2)}, u32[]{:S(2)}) %collective-permute-start.13) | collective-permute-done | bytes 196640 | tf_op jit(solution)/shard_map/ppermute | solution.py:31
  111.1 2.5 %collective-permute-start.12 = (bf16[2048,256]{1,0:T(8,128)(2,1)}, bf16[2048,256]{1,0:T(8,128)(2,1)S(1)}, u32[]{:S(2)}, u32[]{:S(2)}) collective-permute-start(bf16[2048,256]{1,0:T(8,128)(2,1)} %collective-permute-done.5.h3), channel_id=1, source_target_pairs={{0,32},{1,33},{2,34},{3,35},{4,36},{5,37},{6,38},{7,39},{8,40},{9,... | collective-permute-start | bytes 3145736 | tf_op jit(solution)/shard_map/ppermute | solution.py:27
  113.6 2.0 %collective-permute-start.8 = (bf16[2064,256]{1,0:T(8,128)(2,1)}, bf16[2064,256]{1,0:T(8,128)(2,1)S(1)}, u32[]{:S(2)}, u32[]{:S(2)}) collective-permute-start(bf16[2064,256]{1,0:T(8,128)(2,1)} %get-tuple-element.54), channel_id=1, source_target_pairs={{0,64},{1,65},{2,66},{3,67},{4,68},{5,69},{6,70},{7,71},{8,72},{9,... | collective-permute-start | bytes 3170312 | tf_op jit(solution)/shard_map/ppermute | solution.py:27
  116.5 14.3 %partner_part.1 = (bf16[1024,256]{1,0:T(8,128)(2,1)}, bf16[1024,256]{1,0:T(8,128)(2,1)}, bf16[1024,256]{1,0:T(8,128)(2,1)}, bf16[1024,64]{1,0:T(8,128)(2,1)}) custom-call(s32[13]{0:T(128)} %stack.113.idx, bf16[8,2176,128]{2,1,0:T(8,128)(2,1)} %bitcast.70, bf16[2048,256]{1,0:T(8,128)(2,1)} %collective-permute-done.4.h1, ...), custom_call_target="tpu_custom_call" | custom-call | flops 4294967296 | bytes 12582912 | tf_op jit(solution)/shard_map/partner_part/pallas_call | solution.py:204
  130.7 1.8 %collective-permute-start.14 = (bf16[1024,256]{1,0:T(8,128)(2,1)}, bf16[1024,256]{1,0:T(8,128)(2,1)S(1)}, u32[]{:S(2)}, u32[]{:S(2)}) collective-permute-start(bf16[1024,256]{1,0:T(8,128)(2,1)} %get-tuple-element.66), channel_id=1, source_target_pairs={{0,16},{1,17},{2,18},{3,19},{4,20},{5,21},{6,22},{7,23},{8,24},{9,... | collective-permute-start | bytes 1572872 | tf_op jit(solution)/shard_map/ppermute | solution.py:27
  132.6 2.4 %collective-permute-start.15 = (bf16[1024,256]{1,0:T(8,128)(2,1)}, bf16[1024,256]{1,0:T(8,128)(2,1)S(1)}, u32[]{:S(2)}, u32[]{:S(2)}) collective-permute-start(bf16[1024,256]{1,0:T(8,128)(2,1)} %get-tuple-element.67), channel_id=1, source_target_pairs={{0,48},{1,49},{2,50},{3,51},{4,52},{5,53},{6,54},{7,55},{8,56},{9,... | collective-permute-start | bytes 1572872 | tf_op jit(solution)/shard_map/ppermute | solution.py:27
  140.4 13.6 %merge.1 = (bf16[16384,256]{1,0:T(8,128)(2,1)}, f32[1,256]{1,0:T(1,128)}, f32[1024,256]{1,0:T(8,128)}) custom-call(s32[13]{0:T(128)} %stack.113.idx, bf16[2048,2048]{1,0:T(8,128)(2,1)} %base.5, bf16[2064,256]{1,0:T(8,128)(2,1)} %copy-done.3, bf16[2176,256]{1,0:T(8,128)(2,1)} %copy-done.1, bf16[2048,256]{1,0:T(8,128)(2,1)} %collective-permute-done.6.refs_2_, ...), custom_call_target="tpu_custom_call" | custom-call | flops 1073741824 | bytes 18874368 | tf_op jit(solution)/shard_map/merge/pallas_call | solution.py:290
  154.1 2.4 %collective-permute-done.15 = bf16[1024,256]{1,0:T(8,128)(2,1)S(1)} collective-permute-done((bf16[1024,256]{1,0:T(8,128)(2,1)}, bf16[1024,256]{1,0:T(8,128)(2,1)S(1)}, u32[]{:S(2)}, u32[]{:S(2)}) %collective-permute-start.15) | collective-permute-done | bytes 524320 | tf_op jit(solution)/shard_map/ppermute | solution.py:27
  157.8 2.0 %fusion = bf16[1,1024,256]{2,1,0:T(8,128)(2,1)} fusion(f32[1024,256]{1,0:T(8,128)S(1)} %convert_add_fusion, bf16[1024,256]{1,0:T(8,128)(2,1)} %collective-permute-done.16, f32[256]{0:T(256)S(1)} %bitcast.79), kind=kLoop, calls=%fused_computation.2 | loop fusion | flops 1048576 | bytes 2098176 | tf_op jit(solution)/shard_map/broadcast_in_dim | solution.py:384
  (86 shorter events, 18.3 us)
Async XLA Ops:
  7.2 80.1 %all-gather.7.cloned.1.call-start = ((), (), s32[]{:S(2)}) async-start(), calls=%async_computation | async-start | bytes 5013504 | tf_op jit(solution)/shard_map/all_gather | solution.py:36
  9.3 13.0 %copy-start.2 = (bf16[1088,128]{1,0:T(8,128)(2,1)}, bf16[1088,128]{1,0:T(8,128)(2,1)S(1)}, u32[]{:S(2)}) copy-start(bf16[1088,128]{1,0:T(8,128)(2,1)S(1)} %maximum_maximum_fusion.small) | copy-start | bytes 835588
  9.3 13.7 %collective-permute-start.2 = (bf16[1088,128]{1,0:T(8,128)(2,1)S(1)}, bf16[1088,128]{1,0:T(8,128)(2,1)S(1)}, u32[]{:S(2)}, u32[]{:S(2)}) collective-permute-start(bf16[1088,128]{1,0:T(8,128)(2,1)S(1)} %maximum_maximum_fusion.small), channel_id=1, source_target_pairs={{0,66},{1,67},{2,64},{3,65},{4,70},{5,71},{6,68},{7,69},{8,74},{9,... | collective-permute-start | bytes 835592 | tf_op jit(solution)/shard_map/ppermute | solution.py:31
  13.5 9.6 %collective-permute-start.1 = (bf16[1088,128]{1,0:T(8,128)(2,1)S(1)}, bf16[1088,128]{1,0:T(8,128)(2,1)S(1)}, u32[]{:S(2)}, u32[]{:S(2)}) collective-permute-start(bf16[1088,128]{1,0:T(8,128)(2,1)S(1)} %maximum_maximum_fusion.small), channel_id=1, source_target_pairs={{0,2},{1,3},{2,0},{3,1},{4,6},{5,7},{6,4},{7,5},{8,10},{9,11},{10,... | collective-permute-start | bytes 835592 | tf_op jit(solution)/shard_map/ppermute | solution.py:31
  13.5 13.9 %collective-permute-start = (bf16[1088,128]{1,0:T(8,128)(2,1)S(1)}, bf16[1088,128]{1,0:T(8,128)(2,1)S(1)}, u32[]{:S(2)}, u32[]{:S(2)}) collective-permute-start(bf16[1088,128]{1,0:T(8,128)(2,1)S(1)} %maximum_maximum_fusion.small), channel_id=1, source_target_pairs={{0,64},{1,65},{2,66},{3,67},{4,68},{5,69},{6,70},{7,71},{8,72},{9,... | collective-permute-start | bytes 835592 | tf_op jit(solution)/shard_map/ppermute | solution.py:31
  30.5 10.3 %slice-start = ((bf16[1088,128]{1,0:T(8,128)(2,1)}), bf16[64,128]{1,0:T(8,128)(2,1)S(1)}, s32[]{:S(2)}) async-start(bf16[1088,128]{1,0:T(8,128)(2,1)} %copy-done.5), calls=%async_computation.3 | async-start | bytes 32768 | tf_op jit(solution)/shard_map/slice | solution.py:344
  30.5 10.3 %copy-start.9 = (bf16[8,2048]{1,0:T(8,128)(2,1)S(1)}, bf16[8,2048]{1,0:T(8,128)(2,1)}, u32[]{:S(2)}) copy-start(bf16[8,2048]{1,0:T(8,128)(2,1)} %param.8) | copy-start | bytes 98308
  30.5 85.9 %all-gather.11.cloned.1.call-start = ((), (), s32[]{:S(2)}) async-start(), calls=%async_computation.2 | async-start | bytes 5013504 | tf_op jit(solution)/shard_map/all_gather | solution.py:36
  31.3 107.9 %all-gather.9.cloned.1.call-start = ((), (), s32[]{:S(2)}) async-start(), calls=%async_computation.1 | async-start | bytes 2359296 | tf_op jit(solution)/shard_map/all_gather | solution.py:36
  31.3 53.2 %collective-permute-start.9 = (bf16[2176,256]{1,0:T(8,128)(2,1)}, bf16[2176,256]{1,0:T(8,128)(2,1)S(1)}, u32[]{:S(2)}, u32[]{:S(2)}) collective-permute-start(bf16[2176,256]{1,0:T(8,128)(2,1)} %get-tuple-element.55), channel_id=1, source_target_pairs={{0,16},{1,17},{2,18},{3,19},{4,20},{5,21},{6,22},{7,23},{8,24},{9,... | collective-permute-start | bytes 3342344 | tf_op jit(solution)/shard_map/ppermute | solution.py:27
  33.0 27.9 %collective-permute-start.4 = (bf16[2048,256]{1,0:T(8,128)(2,1)}, bf16[2048,256]{1,0:T(8,128)(2,1)}, u32[]{:S(2)}, u32[]{:S(2)}) collective-permute-start(bf16[2048,256]{1,0:T(8,128)(2,1)} %get-tuple-element.42), channel_id=1, source_target_pairs={{0,64},{1,65},{2,66},{3,67},{4,68},{5,69},{6,70},{7,71},{8,72},{9,... | collective-permute-start | bytes 3145736 | tf_op jit(solution)/shard_map/ppermute | solution.py:27
  34.9 46.1 %collective-permute-start.3 = (bf16[2048,256]{1,0:T(8,128)(2,1)}, bf16[2048,256]{1,0:T(8,128)(2,1)}, u32[]{:S(2)}, u32[]{:S(2)}) collective-permute-start(bf16[2048,256]{1,0:T(8,128)(2,1)} %get-tuple-element.40), channel_id=1, source_target_pairs={{0,64},{1,65},{2,66},{3,67},{4,68},{5,69},{6,70},{7,71},{8,72},{9,... | collective-permute-start | bytes 3145736 | tf_op jit(solution)/shard_map/ppermute | solution.py:27
  36.5 49.8 %collective-permute-start.10 = (bf16[2176,256]{1,0:T(8,128)(2,1)}, bf16[2176,256]{1,0:T(8,128)(2,1)}, u32[]{:S(2)}, u32[]{:S(2)}) collective-permute-start(bf16[2176,256]{1,0:T(8,128)(2,1)} %get-tuple-element.56), channel_id=1, source_target_pairs={{0,48},{1,49},{2,50},{3,51},{4,52},{5,53},{6,54},{7,55},{8,56},{9,... | collective-permute-start | bytes 3342344 | tf_op jit(solution)/shard_map/ppermute | solution.py:27
  38.1 48.9 %collective-permute-start.11 = (bf16[2240,256]{1,0:T(8,128)(2,1)}, bf16[2240,256]{1,0:T(8,128)(2,1)S(1)}, u32[]{:S(2)}, u32[]{:S(2)}) collective-permute-start(bf16[2240,256]{1,0:T(8,128)(2,1)} %get-tuple-element.57), channel_id=1, source_target_pairs={{0,32},{1,33},{2,34},{3,35},{4,36},{5,37},{6,38},{7,39},{8,40},{9,... | collective-permute-start | bytes 3440648 | tf_op jit(solution)/shard_map/ppermute | solution.py:27
  81.0 30.0 %collective-permute-start.5 = (bf16[2048,256]{1,0:T(8,128)(2,1)}, bf16[2048,256]{1,0:T(8,128)(2,1)}, u32[]{:S(2)}, u32[]{:S(2)}) collective-permute-start(bf16[2048,256]{1,0:T(8,128)(2,1)} %get-tuple-element.43), channel_id=1, source_target_pairs={{0,64},{1,65},{2,66},{3,67},{4,68},{5,69},{6,70},{7,71},{8,72},{9,... | collective-permute-start | bytes 3145736 | tf_op jit(solution)/shard_map/ppermute | solution.py:27
  83.0 28.0 %collective-permute-start.6 = (bf16[2048,256]{1,0:T(8,128)(2,1)}, bf16[2048,256]{1,0:T(8,128)(2,1)}, u32[]{:S(2)}, u32[]{:S(2)}) collective-permute-start(bf16[2048,256]{1,0:T(8,128)(2,1)} %collective-permute-done.4.h1), channel_id=1, source_target_pairs={{0,16},{1,17},{2,18},{3,19},{4,20},{5,21},{6,22},{7,23},{8,24},{9,... | collective-permute-start | bytes 3145736 | tf_op jit(solution)/shard_map/ppermute | solution.py:27
  84.6 26.4 %collective-permute-start.7 = (bf16[2048,256]{1,0:T(8,128)(2,1)}, bf16[2048,256]{1,0:T(8,128)(2,1)}, u32[]{:S(2)}, u32[]{:S(2)}) collective-permute-start(bf16[2048,256]{1,0:T(8,128)(2,1)} %collective-permute-done.3.h2), channel_id=1, source_target_pairs={{0,48},{1,49},{2,50},{3,51},{4,52},{5,53},{6,54},{7,55},{8,56},{9,... | collective-permute-start | bytes 3145736 | tf_op jit(solution)/shard_map/ppermute | solution.py:27
  87.0 15.9 %copy-start = (bf16[2240,256]{1,0:T(8,128)(2,1)}, bf16[2240,256]{1,0:T(8,128)(2,1)S(1)}, u32[]{:S(2)}) copy-start(bf16[2240,256]{1,0:T(8,128)(2,1)S(1)} %collective-permute-done.11.refs_5_) | copy-start | bytes 3440644
  103.0 7.3 %collective-permute-start.13 = (bf16[4,192,128]{2,1,0:T(8,128)(2,1)S(1)}, bf16[4,192,128]{2,1,0:T(8,128)(2,1)S(1)}, u32[]{:S(2)}, u32[]{:S(2)}) collective-permute-start(bf16[4,192,128]{2,1,0:T(8,128)(2,1)S(1)} %pad_maximum_fusion.2), channel_id=1, source_target_pairs={{0,64},{1,65},{2,66},{3,67},{4,68},{5,69},{6,70},{7,71},{8,72},{9,... | collective-permute-start | bytes 589832 | tf_op jit(solution)/shard_map/ppermute | solution.py:31
  111.1 28.0 %collective-permute-start.12 = (bf16[2048,256]{1,0:T(8,128)(2,1)}, bf16[2048,256]{1,0:T(8,128)(2,1)S(1)}, u32[]{:S(2)}, u32[]{:S(2)}) collective-permute-start(bf16[2048,256]{1,0:T(8,128)(2,1)} %collective-permute-done.5.h3), channel_id=1, source_target_pairs={{0,32},{1,33},{2,34},{3,35},{4,36},{5,37},{6,38},{7,39},{8,40},{9,... | collective-permute-start | bytes 3145736 | tf_op jit(solution)/shard_map/ppermute | solution.py:27
  113.6 25.5 %collective-permute-start.8 = (bf16[2064,256]{1,0:T(8,128)(2,1)}, bf16[2064,256]{1,0:T(8,128)(2,1)S(1)}, u32[]{:S(2)}, u32[]{:S(2)}) collective-permute-start(bf16[2064,256]{1,0:T(8,128)(2,1)} %get-tuple-element.54), channel_id=1, source_target_pairs={{0,64},{1,65},{2,66},{3,67},{4,68},{5,69},{6,70},{7,71},{8,72},{9,... | collective-permute-start | bytes 3170312 | tf_op jit(solution)/shard_map/ppermute | solution.py:27
  130.7 23.4 %collective-permute-start.14 = (bf16[1024,256]{1,0:T(8,128)(2,1)}, bf16[1024,256]{1,0:T(8,128)(2,1)S(1)}, u32[]{:S(2)}, u32[]{:S(2)}) collective-permute-start(bf16[1024,256]{1,0:T(8,128)(2,1)} %get-tuple-element.66), channel_id=1, source_target_pairs={{0,16},{1,17},{2,18},{3,19},{4,20},{5,21},{6,22},{7,23},{8,24},{9,... | collective-permute-start | bytes 1572872 | tf_op jit(solution)/shard_map/ppermute | solution.py:27
  132.6 23.9 %collective-permute-start.15 = (bf16[1024,256]{1,0:T(8,128)(2,1)}, bf16[1024,256]{1,0:T(8,128)(2,1)S(1)}, u32[]{:S(2)}, u32[]{:S(2)}) collective-permute-start(bf16[1024,256]{1,0:T(8,128)(2,1)} %get-tuple-element.67), channel_id=1, source_target_pairs={{0,48},{1,49},{2,50},{3,51},{4,52},{5,53},{6,54},{7,55},{8,56},{9,... | collective-permute-start | bytes 1572872 | tf_op jit(solution)/shard_map/ppermute | solution.py:27
  136.3 21.6 %collective-permute-start.16 = (bf16[1024,256]{1,0:T(8,128)(2,1)}, bf16[1024,256]{1,0:T(8,128)(2,1)}, u32[]{:S(2)}, u32[]{:S(2)}) collective-permute-start(bf16[1024,256]{1,0:T(8,128)(2,1)} %get-tuple-element.68), channel_id=1, source_target_pairs={{0,32},{1,33},{2,34},{3,35},{4,36},{5,37},{6,38},{7,39},{8,40},{9,... | collective-permute-start | bytes 1572872 | tf_op jit(solution)/shard_map/ppermute | solution.py:27
  (8 other events, 16.5 us)
Sparse Core Ops, SparseCore 0:
  30.6 34.3 all-gather.6
  66.7 33.1 all-gather.10
  111.1 27.3 all-gather.8

commit v6 on v5

--- a/solution.py
+++ b/solution.py
@@ -380,7 +380,7 @@
         idx, base, blocks, lefts, gathered_partner, acc, rr, mag, t, right_mine
     )
 
-    product = lax.optimization_barrier(product + sums[0].astype(F32) + sums[1].astype(F32)) + sums[2].astype(F32)
+    product = lax.optimization_barrier(product + sums[0].astype(F32)) + sums[1].astype(F32) + sums[2].astype(F32)
     return serving[None], (product * scale).astype(BF16)[None]
 
 

time: 167 us -> 167 us (level)
  transfers between devices with their start and end apart: 20 -> 20, of which waited for: 6 -> 7; matrix products, arithmetic and copies ran while one was open for 5% -> 5% of each run, Pallas kernels for 30% -> 30%
where the time goes in v6:
time: 167 us; the launch traced here: 166 us
  waiting for transfers between devices  53.3 us (32%)
  Pallas kernels  52.4 us (31%)
  starting transfers between devices  31.6 us (19%)
  between operations  14.1 us (8%)
  local copies, waits for them, and re-layouts  8.04 us (5%)
  other arithmetic  6.89 us (4%)
    ppermute x13, waiting for transfers between devices, move(): return lax.ppermute(a, AXES, pairs)  42.4 us
    ppermute x13, starting transfers between devices, move(): return lax.ppermute(a, AXES, pairs)  24.1 us
    pallas_call x1, Pallas kernels, own_part(): pl.pallas_call(own_kernel, out_shape=[jax.ShapeDtypeStruct((4, TOK, WIDE)...  15.7 us
    pallas_call x1, Pallas kernels, partner_part(): pl.pallas_call(partner_kernel, out_shape=[send, send, send, jax.ShapeDtyp...  14.2 us
    pallas_call x1, Pallas kernels, merge(): pl.pallas_call(merge_kernel, out_shape=[jax.ShapeDtypeStruct((8 * BLOCK,...  13.6 us
    ppermute x4, waiting for transfers between devices, swap(): return lax.ppermute(a, AXES, [(i, i ^ bits) for i in range(128)])  10.1 us
    ppermute x4, starting transfers between devices, swap(): return lax.ppermute(a, AXES, [(i, i ^ bits) for i in range(128)])  7.37 us
    pallas_call x1, Pallas kernels, pack(): pl.pallas_call(functools.partial(pack_kernel, n), out_shape=[jax.ShapeDty...  6.58 us
  transfers between devices with their start and end apart: 20, of which 7 were waited for; matrix products, arithmetic and copies ran while one was open for 5% of the time, Pallas kernels for 30%

profile of v6, /device:TPU:0, one launch (start us, length us, event | category | flops | bytes accessed | tf_op | source)
XLA Modules:
  0.0 166.4 jit_solution(8262090558495125297)
XLA Ops:
  9.3 4.2 %collective-permute-start.2 = (bf16[1088,128]{1,0:T(8,128)(2,1)S(1)}, bf16[1088,128]{1,0:T(8,128)(2,1)S(1)}, u32[]{:S(2)}, u32[]{:S(2)}) collective-permute-start(bf16[1088,128]{1,0:T(8,128)(2,1)S(1)} %maximum_maximum_fusion.small), channel_id=1, source_target_pairs={{0,66},{1,67},{2,64},{3,65},{4,70},{5,71},{6,68},{7,69},{8,74},{9,... | collective-permute-start | bytes 835592 | tf_op jit(solution)/shard_map/ppermute | solution.py:31
  13.5 1.6 collective-permute-start
  15.7 6.6 %pack.1 = (bf16[2176,256]{1,0:T(8,128)(2,1)}, bf16[2176,256]{1,0:T(8,128)(2,1)}, bf16[2240,256]{1,0:T(8,128)(2,1)}, bf16[2048,256]{1,0:T(8,128)(2,1)}, bf16[2048...) custom-call(s32[7]{0:T(128)} %stack.115.idx, bf16[2048,2048]{1,0:T(8,128)(2,1)} %base.5), custom_call_target="tpu_custom_call" | custom-call | bytes 14680064 | tf_op jit(solution)/shard_map/pack/pallas_call | solution.py:86
  23.1 4.3 %collective-permute-done.partner = bf16[1088,128]{1,0:T(8,128)(2,1)S(1)} collective-permute-done((bf16[1088,128]{1,0:T(8,128)(2,1)S(1)}, bf16[1088,128]{1,0:T(8,128)(2,1)S(1)}, u32[]{:S(2)}, u32[]{:S(2)}) %collective-permute-start) | collective-permute-done | bytes 278560 | tf_op jit(solution)/shard_map/ppermute | solution.py:31
  28.1 2.3 %join.1 = (bf16[2176,256]{1,0:T(8,128)(2,1)}, bf16[2176,256]{1,0:T(8,128)(2,1)}, bf16[2240,256]{1,0:T(8,128)(2,1)}, bf16[2176,128]{1,0:T(8,128)(2,1)}, bf16[2176,128]{1,0:T(8,128)(2,1)}) custom-call(bf16[64,128]{1,0:T(8,128)(2,1)} %pad_maximum_fusion.3.left, bf16[128,128]{1,0:T(8,128)(2,1)} %bitcast.76, ...), custom_call_target="tpu_custom_call", output_to_operand_aliasing={{0}: (6, {}), {1}: (7, {}), {2}: (8, {})} | custom-call | bytes 3145728 | tf_op jit(solution)/shard_map/join/pallas_call | solution.py:114
  31.3 1.6 collective-permute-start.9
  33.0 2.0 %collective-permute-start.4 = (bf16[2048,256]{1,0:T(8,128)(2,1)}, bf16[2048,256]{1,0:T(8,128)(2,1)}, u32[]{:S(2)}, u32[]{:S(2)}) collective-permute-start(bf16[2048,256]{1,0:T(8,128)(2,1)} %get-tuple-element.42), channel_id=1, source_target_pairs={{0,64},{1,65},{2,66},{3,67},{4,68},{5,69},{6,70},{7,71},{8,72},{9,... | collective-permute-start | bytes 3145736 | tf_op jit(solution)/shard_map/ppermute | solution.py:27
  36.5 1.7 collective-permute-start.10
  38.1 2.0 %collective-permute-start.11 = (bf16[2240,256]{1,0:T(8,128)(2,1)}, bf16[2240,256]{1,0:T(8,128)(2,1)S(1)}, u32[]{:S(2)}, u32[]{:S(2)}) collective-permute-start(bf16[2240,256]{1,0:T(8,128)(2,1)} %get-tuple-element.57), channel_id=1, source_target_pairs={{0,32},{1,33},{2,34},{3,35},{4,36},{5,37},{6,38},{7,39},{8,40},{9,... | collective-permute-start | bytes 3440648 | tf_op jit(solution)/shard_map/ppermute | solution.py:27
  40.9 20.0 %collective-permute-done.4.h1 = bf16[2048,256]{1,0:T(8,128)(2,1)} collective-permute-done((bf16[2048,256]{1,0:T(8,128)(2,1)}, bf16[2048,256]{1,0:T(8,128)(2,1)}, u32[]{:S(2)}, u32[]{:S(2)}) %collective-permute-start.4) | collective-permute-done | bytes 1048608 | tf_op jit(solution)/shard_map/ppermute | solution.py:27
  60.9 20.1 %collective-permute-done.3.h2 = bf16[2048,256]{1,0:T(8,128)(2,1)} collective-permute-done((bf16[2048,256]{1,0:T(8,128)(2,1)}, bf16[2048,256]{1,0:T(8,128)(2,1)}, u32[]{:S(2)}, u32[]{:S(2)}) %collective-permute-start.3) | collective-permute-done | bytes 1048608 | tf_op jit(solution)/shard_map/ppermute | solution.py:27
  81.0 2.0 %collective-permute-start.5 = (bf16[2048,256]{1,0:T(8,128)(2,1)}, bf16[2048,256]{1,0:T(8,128)(2,1)}, u32[]{:S(2)}, u32[]{:S(2)}) collective-permute-start(bf16[2048,256]{1,0:T(8,128)(2,1)} %get-tuple-element.43), channel_id=1, source_target_pairs={{0,64},{1,65},{2,66},{3,67},{4,68},{5,69},{6,70},{7,71},{8,72},{9,... | collective-permute-start | bytes 3145736 | tf_op jit(solution)/shard_map/ppermute | solution.py:27
  83.0 1.6 collective-permute-start.6
  84.6 1.7 %collective-permute-start.7 = (bf16[2048,256]{1,0:T(8,128)(2,1)}, bf16[2048,256]{1,0:T(8,128)(2,1)}, u32[]{:S(2)}, u32[]{:S(2)}) collective-permute-start(bf16[2048,256]{1,0:T(8,128)(2,1)} %collective-permute-done.3.h2), channel_id=1, source_target_pairs={{0,48},{1,49},{2,50},{3,51},{4,52},{5,53},{6,54},{7,55},{8,56},{9,... | collective-permute-start | bytes 3145736 | tf_op jit(solution)/shard_map/ppermute | solution.py:27
  87.2 15.7 %own_part.1 = (f32[4,1024,256]{2,1,0:T(8,128)}, f32[1024,64]{1,0:T(8,128)}) custom-call(s32[13]{0:T(128)} %stack.113.idx, bf16[8,2176,128]{2,1,0:T(8,128)(2,1)} %bitcast.81, bf16[2048,2048]{1,0:T(8,128)(2,1)} %base.5), custom_call_target="tpu_custom_call" | custom-call | flops 5368709120 | bytes 13631488 | tf_op jit(solution)/shard_map/own_part/pallas_call | solution.py:164
  103.0 1.6 collective-permute-start.13
  104.6 5.6 %collective-permute-done.13 = bf16[4,192,128]{2,1,0:T(8,128)(2,1)S(1)} collective-permute-done((bf16[4,192,128]{2,1,0:T(8,128)(2,1)S(1)}, bf16[4,192,128]{2,1,0:T(8,128)(2,1)S(1)}, u32[]{:S(2)}, u32[]{:S(2)}) %collective-permute-start.13) | collective-permute-done | bytes 196640 | tf_op jit(solution)/shard_map/ppermute | solution.py:31
  111.1 2.5 %collective-permute-start.12 = (bf16[2048,256]{1,0:T(8,128)(2,1)}, bf16[2048,256]{1,0:T(8,128)(2,1)S(1)}, u32[]{:S(2)}, u32[]{:S(2)}) collective-permute-start(bf16[2048,256]{1,0:T(8,128)(2,1)} %collective-permute-done.5.h3), channel_id=1, source_target_pairs={{0,32},{1,33},{2,34},{3,35},{4,36},{5,37},{6,38},{7,39},{8,40},{9,... | collective-permute-start | bytes 3145736 | tf_op jit(solution)/shard_map/ppermute | solution.py:27
  113.6 2.0 %collective-permute-start.8 = (bf16[2064,256]{1,0:T(8,128)(2,1)}, bf16[2064,256]{1,0:T(8,128)(2,1)S(1)}, u32[]{:S(2)}, u32[]{:S(2)}) collective-permute-start(bf16[2064,256]{1,0:T(8,128)(2,1)} %get-tuple-element.54), channel_id=1, source_target_pairs={{0,64},{1,65},{2,66},{3,67},{4,68},{5,69},{6,70},{7,71},{8,72},{9,... | collective-permute-start | bytes 3170312 | tf_op jit(solution)/shard_map/ppermute | solution.py:27
  116.5 14.2 %partner_part.1 = (bf16[1024,256]{1,0:T(8,128)(2,1)}, bf16[1024,256]{1,0:T(8,128)(2,1)}, bf16[1024,256]{1,0:T(8,128)(2,1)}, bf16[1024,64]{1,0:T(8,128)(2,1)}) custom-call(s32[13]{0:T(128)} %stack.113.idx, bf16[8,2176,128]{2,1,0:T(8,128)(2,1)} %bitcast.70, bf16[2048,256]{1,0:T(8,128)(2,1)} %collective-permute-done.4.h1, ...), custom_call_target="tpu_custom_call" | custom-call | flops 4294967296 | bytes 12582912 | tf_op jit(solution)/shard_map/partner_part/pallas_call | solution.py:204
  130.7 1.8 %collective-permute-start.14 = (bf16[1024,256]{1,0:T(8,128)(2,1)}, bf16[1024,256]{1,0:T(8,128)(2,1)S(1)}, u32[]{:S(2)}, u32[]{:S(2)}) collective-permute-start(bf16[1024,256]{1,0:T(8,128)(2,1)} %get-tuple-element.66), channel_id=1, source_target_pairs={{0,16},{1,17},{2,18},{3,19},{4,20},{5,21},{6,22},{7,23},{8,24},{9,... | collective-permute-start | bytes 1572872 | tf_op jit(solution)/shard_map/ppermute | solution.py:27
  133.9 2.3 %collective-permute-start.15 = (bf16[1024,256]{1,0:T(8,128)(2,1)}, bf16[1024,256]{1,0:T(8,128)(2,1)S(1)}, u32[]{:S(2)}, u32[]{:S(2)}) collective-permute-start(bf16[1024,256]{1,0:T(8,128)(2,1)} %get-tuple-element.67), channel_id=1, source_target_pairs={{0,48},{1,49},{2,50},{3,51},{4,52},{5,53},{6,54},{7,55},{8,56},{9,... | collective-permute-start | bytes 1572872 | tf_op jit(solution)/shard_map/ppermute | solution.py:27
  140.4 13.6 %merge.1 = (bf16[16384,256]{1,0:T(8,128)(2,1)}, f32[1,256]{1,0:T(1,128)}, f32[1024,256]{1,0:T(8,128)}) custom-call(s32[13]{0:T(128)} %stack.113.idx, bf16[2048,2048]{1,0:T(8,128)(2,1)} %base.5, bf16[2064,256]{1,0:T(8,128)(2,1)} %copy-done.3, bf16[2176,256]{1,0:T(8,128)(2,1)} %copy-done.1, bf16[2048,256]{1,0:T(8,128)(2,1)} %collective-permute-done.6.refs_2_, ...), custom_call_target="tpu_custom_call" | custom-call | flops 1073741824 | bytes 18874368 | tf_op jit(solution)/shard_map/merge/pallas_call | solution.py:290
  157.8 2.1 %fusion = bf16[1,1024,256]{2,1,0:T(8,128)(2,1)} fusion(bf16[1024,256]{1,0:T(8,128)(2,1)} %collective-permute-done.16, f32[1024,256]{1,0:T(8,128)S(1)} %convert_add_fusion, bf16[1024,256]{1,0:T(8,128)(2,1)S(1)} %collective-permute-done.15, f32[256]{0:T(256)S(1)} %bitcast.79), kind=kLoop, calls=%fused_computation.2 | loop fusion | flops 1572864 | bytes 2622464 | tf_op jit(solution)/shard_map/broadcast_in_dim | solution.py:384
  (86 shorter events, 19.2 us)
Async XLA Ops:
  7.2 80.1 %all-gather.7.cloned.1.call-start = ((), (), s32[]{:S(2)}) async-start(), calls=%async_computation | async-start | bytes 5013504 | tf_op jit(solution)/shard_map/all_gather | solution.py:36
  9.3 13.0 %copy-start.2 = (bf16[1088,128]{1,0:T(8,128)(2,1)}, bf16[1088,128]{1,0:T(8,128)(2,1)S(1)}, u32[]{:S(2)}) copy-start(bf16[1088,128]{1,0:T(8,128)(2,1)S(1)} %maximum_maximum_fusion.small) | copy-start | bytes 835588
  9.3 13.7 %collective-permute-start.2 = (bf16[1088,128]{1,0:T(8,128)(2,1)S(1)}, bf16[1088,128]{1,0:T(8,128)(2,1)S(1)}, u32[]{:S(2)}, u32[]{:S(2)}) collective-permute-start(bf16[1088,128]{1,0:T(8,128)(2,1)S(1)} %maximum_maximum_fusion.small), channel_id=1, source_target_pairs={{0,66},{1,67},{2,64},{3,65},{4,70},{5,71},{6,68},{7,69},{8,74},{9,... | collective-permute-start | bytes 835592 | tf_op jit(solution)/shard_map/ppermute | solution.py:31
  13.5 9.6 %collective-permute-start.1 = (bf16[1088,128]{1,0:T(8,128)(2,1)S(1)}, bf16[1088,128]{1,0:T(8,128)(2,1)S(1)}, u32[]{:S(2)}, u32[]{:S(2)}) collective-permute-start(bf16[1088,128]{1,0:T(8,128)(2,1)S(1)} %maximum_maximum_fusion.small), channel_id=1, source_target_pairs={{0,2},{1,3},{2,0},{3,1},{4,6},{5,7},{6,4},{7,5},{8,10},{9,11},{10,... | collective-permute-start | bytes 835592 | tf_op jit(solution)/shard_map/ppermute | solution.py:31
  13.5 13.9 %collective-permute-start = (bf16[1088,128]{1,0:T(8,128)(2,1)S(1)}, bf16[1088,128]{1,0:T(8,128)(2,1)S(1)}, u32[]{:S(2)}, u32[]{:S(2)}) collective-permute-start(bf16[1088,128]{1,0:T(8,128)(2,1)S(1)} %maximum_maximum_fusion.small), channel_id=1, source_target_pairs={{0,64},{1,65},{2,66},{3,67},{4,68},{5,69},{6,70},{7,71},{8,72},{9,... | collective-permute-start | bytes 835592 | tf_op jit(solution)/shard_map/ppermute | solution.py:31
  30.5 10.4 %slice-start = ((bf16[1088,128]{1,0:T(8,128)(2,1)}), bf16[64,128]{1,0:T(8,128)(2,1)S(1)}, s32[]{:S(2)}) async-start(bf16[1088,128]{1,0:T(8,128)(2,1)} %copy-done.5), calls=%async_computation.3 | async-start | bytes 32768 | tf_op jit(solution)/shard_map/slice | solution.py:344
  30.5 10.3 %copy-start.9 = (bf16[8,2048]{1,0:T(8,128)(2,1)S(1)}, bf16[8,2048]{1,0:T(8,128)(2,1)}, u32[]{:S(2)}) copy-start(bf16[8,2048]{1,0:T(8,128)(2,1)} %param.8) | copy-start | bytes 98308
  30.5 85.9 %all-gather.11.cloned.1.call-start = ((), (), s32[]{:S(2)}) async-start(), calls=%async_computation.2 | async-start | bytes 5013504 | tf_op jit(solution)/shard_map/all_gather | solution.py:36
  31.3 107.8 %all-gather.9.cloned.1.call-start = ((), (), s32[]{:S(2)}) async-start(), calls=%async_computation.1 | async-start | bytes 2359296 | tf_op jit(solution)/shard_map/all_gather | solution.py:36
  31.3 53.2 %collective-permute-start.9 = (bf16[2176,256]{1,0:T(8,128)(2,1)}, bf16[2176,256]{1,0:T(8,128)(2,1)S(1)}, u32[]{:S(2)}, u32[]{:S(2)}) collective-permute-start(bf16[2176,256]{1,0:T(8,128)(2,1)} %get-tuple-element.55), channel_id=1, source_target_pairs={{0,16},{1,17},{2,18},{3,19},{4,20},{5,21},{6,22},{7,23},{8,24},{9,... | collective-permute-start | bytes 3342344 | tf_op jit(solution)/shard_map/ppermute | solution.py:27
  33.0 27.9 %collective-permute-start.4 = (bf16[2048,256]{1,0:T(8,128)(2,1)}, bf16[2048,256]{1,0:T(8,128)(2,1)}, u32[]{:S(2)}, u32[]{:S(2)}) collective-permute-start(bf16[2048,256]{1,0:T(8,128)(2,1)} %get-tuple-element.42), channel_id=1, source_target_pairs={{0,64},{1,65},{2,66},{3,67},{4,68},{5,69},{6,70},{7,71},{8,72},{9,... | collective-permute-start | bytes 3145736 | tf_op jit(solution)/shard_map/ppermute | solution.py:27
  34.9 46.1 %collective-permute-start.3 = (bf16[2048,256]{1,0:T(8,128)(2,1)}, bf16[2048,256]{1,0:T(8,128)(2,1)}, u32[]{:S(2)}, u32[]{:S(2)}) collective-permute-start(bf16[2048,256]{1,0:T(8,128)(2,1)} %get-tuple-element.40), channel_id=1, source_target_pairs={{0,64},{1,65},{2,66},{3,67},{4,68},{5,69},{6,70},{7,71},{8,72},{9,... | collective-permute-start | bytes 3145736 | tf_op jit(solution)/shard_map/ppermute | solution.py:27
  36.5 49.8 %collective-permute-start.10 = (bf16[2176,256]{1,0:T(8,128)(2,1)}, bf16[2176,256]{1,0:T(8,128)(2,1)}, u32[]{:S(2)}, u32[]{:S(2)}) collective-permute-start(bf16[2176,256]{1,0:T(8,128)(2,1)} %get-tuple-element.56), channel_id=1, source_target_pairs={{0,48},{1,49},{2,50},{3,51},{4,52},{5,53},{6,54},{7,55},{8,56},{9,... | collective-permute-start | bytes 3342344 | tf_op jit(solution)/shard_map/ppermute | solution.py:27
  38.1 48.9 %collective-permute-start.11 = (bf16[2240,256]{1,0:T(8,128)(2,1)}, bf16[2240,256]{1,0:T(8,128)(2,1)S(1)}, u32[]{:S(2)}, u32[]{:S(2)}) collective-permute-start(bf16[2240,256]{1,0:T(8,128)(2,1)} %get-tuple-element.57), channel_id=1, source_target_pairs={{0,32},{1,33},{2,34},{3,35},{4,36},{5,37},{6,38},{7,39},{8,40},{9,... | collective-permute-start | bytes 3440648 | tf_op jit(solution)/shard_map/ppermute | solution.py:27
  81.0 30.0 %collective-permute-start.5 = (bf16[2048,256]{1,0:T(8,128)(2,1)}, bf16[2048,256]{1,0:T(8,128)(2,1)}, u32[]{:S(2)}, u32[]{:S(2)}) collective-permute-start(bf16[2048,256]{1,0:T(8,128)(2,1)} %get-tuple-element.43), channel_id=1, source_target_pairs={{0,64},{1,65},{2,66},{3,67},{4,68},{5,69},{6,70},{7,71},{8,72},{9,... | collective-permute-start | bytes 3145736 | tf_op jit(solution)/shard_map/ppermute | solution.py:27
  83.0 28.0 %collective-permute-start.6 = (bf16[2048,256]{1,0:T(8,128)(2,1)}, bf16[2048,256]{1,0:T(8,128)(2,1)}, u32[]{:S(2)}, u32[]{:S(2)}) collective-permute-start(bf16[2048,256]{1,0:T(8,128)(2,1)} %collective-permute-done.4.h1), channel_id=1, source_target_pairs={{0,16},{1,17},{2,18},{3,19},{4,20},{5,21},{6,22},{7,23},{8,24},{9,... | collective-permute-start | bytes 3145736 | tf_op jit(solution)/shard_map/ppermute | solution.py:27
  84.6 26.4 %collective-permute-start.7 = (bf16[2048,256]{1,0:T(8,128)(2,1)}, bf16[2048,256]{1,0:T(8,128)(2,1)}, u32[]{:S(2)}, u32[]{:S(2)}) collective-permute-start(bf16[2048,256]{1,0:T(8,128)(2,1)} %collective-permute-done.3.h2), channel_id=1, source_target_pairs={{0,48},{1,49},{2,50},{3,51},{4,52},{5,53},{6,54},{7,55},{8,56},{9,... | collective-permute-start | bytes 3145736 | tf_op jit(solution)/shard_map/ppermute | solution.py:27
  87.0 15.9 %copy-start = (bf16[2240,256]{1,0:T(8,128)(2,1)}, bf16[2240,256]{1,0:T(8,128)(2,1)S(1)}, u32[]{:S(2)}) copy-start(bf16[2240,256]{1,0:T(8,128)(2,1)S(1)} %collective-permute-done.11.refs_5_) | copy-start | bytes 3440644
  103.0 7.3 %collective-permute-start.13 = (bf16[4,192,128]{2,1,0:T(8,128)(2,1)S(1)}, bf16[4,192,128]{2,1,0:T(8,128)(2,1)S(1)}, u32[]{:S(2)}, u32[]{:S(2)}) collective-permute-start(bf16[4,192,128]{2,1,0:T(8,128)(2,1)S(1)} %pad_maximum_fusion.2), channel_id=1, source_target_pairs={{0,64},{1,65},{2,66},{3,67},{4,68},{5,69},{6,70},{7,71},{8,72},{9,... | collective-permute-start | bytes 589832 | tf_op jit(solution)/shard_map/ppermute | solution.py:31
  111.1 28.0 %collective-permute-start.12 = (bf16[2048,256]{1,0:T(8,128)(2,1)}, bf16[2048,256]{1,0:T(8,128)(2,1)S(1)}, u32[]{:S(2)}, u32[]{:S(2)}) collective-permute-start(bf16[2048,256]{1,0:T(8,128)(2,1)} %collective-permute-done.5.h3), channel_id=1, source_target_pairs={{0,32},{1,33},{2,34},{3,35},{4,36},{5,37},{6,38},{7,39},{8,40},{9,... | collective-permute-start | bytes 3145736 | tf_op jit(solution)/shard_map/ppermute | solution.py:27
  113.6 25.5 %collective-permute-start.8 = (bf16[2064,256]{1,0:T(8,128)(2,1)}, bf16[2064,256]{1,0:T(8,128)(2,1)S(1)}, u32[]{:S(2)}, u32[]{:S(2)}) collective-permute-start(bf16[2064,256]{1,0:T(8,128)(2,1)} %get-tuple-element.54), channel_id=1, source_target_pairs={{0,64},{1,65},{2,66},{3,67},{4,68},{5,69},{6,70},{7,71},{8,72},{9,... | collective-permute-start | bytes 3170312 | tf_op jit(solution)/shard_map/ppermute | solution.py:27
  130.7 23.3 %collective-permute-start.14 = (bf16[1024,256]{1,0:T(8,128)(2,1)}, bf16[1024,256]{1,0:T(8,128)(2,1)S(1)}, u32[]{:S(2)}, u32[]{:S(2)}) collective-permute-start(bf16[1024,256]{1,0:T(8,128)(2,1)} %get-tuple-element.66), channel_id=1, source_target_pairs={{0,16},{1,17},{2,18},{3,19},{4,20},{5,21},{6,22},{7,23},{8,24},{9,... | collective-permute-start | bytes 1572872 | tf_op jit(solution)/shard_map/ppermute | solution.py:27
  133.9 22.6 %collective-permute-start.15 = (bf16[1024,256]{1,0:T(8,128)(2,1)}, bf16[1024,256]{1,0:T(8,128)(2,1)S(1)}, u32[]{:S(2)}, u32[]{:S(2)}) collective-permute-start(bf16[1024,256]{1,0:T(8,128)(2,1)} %get-tuple-element.67), channel_id=1, source_target_pairs={{0,48},{1,49},{2,50},{3,51},{4,52},{5,53},{6,54},{7,55},{8,56},{9,... | collective-permute-start | bytes 1572872 | tf_op jit(solution)/shard_map/ppermute | solution.py:27
  136.2 21.6 %collective-permute-start.16 = (bf16[1024,256]{1,0:T(8,128)(2,1)}, bf16[1024,256]{1,0:T(8,128)(2,1)}, u32[]{:S(2)}, u32[]{:S(2)}) collective-permute-start(bf16[1024,256]{1,0:T(8,128)(2,1)} %get-tuple-element.68), channel_id=1, source_target_pairs={{0,32},{1,33},{2,34},{3,35},{4,36},{5,37},{6,38},{7,39},{8,40},{9,... | collective-permute-start | bytes 1572872 | tf_op jit(solution)/shard_map/ppermute | solution.py:27
  (8 other events, 19.0 us)
Sparse Core Ops, SparseCore 0:
  30.6 34.3 all-gather.6
  66.7 33.1 all-gather.10
  111.1 27.3 all-gather.8

commit v7 on v6

--- a/solution.py
+++ b/solution.py
@@ -325,7 +325,7 @@
     partner, beside, beside_partner = swap(small, 64), swap(small, 2), swap(small, 66)
     relayed = {}
     places = [served_by(0, d) for d in SHIFTS] + [served_by(1, d) for d in SHIFTS + (0,)]
-    slices = pack(places, base, (EXTRA, EXTRA, EXTRA + 64) + (0,) * 3 + (16,))
+    slices = pack(places, base, (EXTRA, EXTRA, EXTRA + 16) + (0,) * 3 + (16,))
     packed, packed_half = dict(zip(SHIFTS, slices)), dict(zip(SHIFTS + (0,), slices[3:]))
 
     wave = (partner, beside, beside_partner, packed[2])

time: 167 us -> 167 us (level)
  transfers between devices with their start and end apart: 20 -> 20, of which waited for: 7 -> 8; matrix products, arithmetic and copies ran while one was open for 5% -> 5% of each run, Pallas kernels for 30% -> 30%
where the time goes in v7:
time: 167 us; the launch traced here: 166 us
  waiting for transfers between devices  54.3 us (33%)
  Pallas kernels  52.4 us (31%)
  starting transfers between devices  30.6 us (18%)
  between operations  14.1 us (8%)
  local copies, waits for them, and re-layouts  8.04 us (5%)
  other arithmetic  6.88 us (4%)
    ppermute x13, waiting for transfers between devices, move(): return lax.ppermute(a, AXES, pairs)  43.5 us
    ppermute x13, starting transfers between devices, move(): return lax.ppermute(a, AXES, pairs)  23.1 us
    pallas_call x1, Pallas kernels, own_part(): pl.pallas_call(own_kernel, out_shape=[jax.ShapeDtypeStruct((4, TOK, WIDE)...  15.7 us
    pallas_call x1, Pallas kernels, partner_part(): pl.pallas_call(partner_kernel, out_shape=[send, send, send, jax.ShapeDtyp...  14.2 us
    pallas_call x1, Pallas kernels, merge(): pl.pallas_call(merge_kernel, out_shape=[jax.ShapeDtypeStruct((8 * BLOCK,...  13.6 us
    ppermute x4, waiting for transfers between devices, swap(): return lax.ppermute(a, AXES, [(i, i ^ bits) for i in range(128)])  10.1 us
    ppermute x4, starting transfers between devices, swap(): return lax.ppermute(a, AXES, [(i, i ^ bits) for i in range(128)])  7.37 us
    pallas_call x1, Pallas kernels, pack(): pl.pallas_call(functools.partial(pack_kernel, n), out_shape=[jax.ShapeDty...  6.58 us
  transfers between devices with their start and end apart: 20, of which 8 were waited for; matrix products, arithmetic and copies ran while one was open for 5% of the time, Pallas kernels for 30%

profile of v7, /device:TPU:0, one launch (start us, length us, event | category | flops | bytes accessed | tf_op | source)
XLA Modules:
  0.0 166.4 jit_solution(3731010497453595577)
XLA Ops:
  9.3 4.2 %collective-permute-start.2 = (bf16[1088,128]{1,0:T(8,128)(2,1)S(1)}, bf16[1088,128]{1,0:T(8,128)(2,1)S(1)}, u32[]{:S(2)}, u32[]{:S(2)}) collective-permute-start(bf16[1088,128]{1,0:T(8,128)(2,1)S(1)} %maximum_maximum_fusion.small), channel_id=1, source_target_pairs={{0,66},{1,67},{2,64},{3,65},{4,70},{5,71},{6,68},{7,69},{8,74},{9,... | collective-permute-start | bytes 835592 | tf_op jit(solution)/shard_map/ppermute | solution.py:31
  13.5 1.6 collective-permute-start
  15.7 6.6 %pack.1 = (bf16[2176,256]{1,0:T(8,128)(2,1)}, bf16[2176,256]{1,0:T(8,128)(2,1)}, bf16[2192,256]{1,0:T(8,128)(2,1)}, bf16[2048,256]{1,0:T(8,128)(2,1)}, bf16[2048...) custom-call(s32[7]{0:T(128)} %stack.115.idx, bf16[2048,2048]{1,0:T(8,128)(2,1)} %base.5), custom_call_target="tpu_custom_call" | custom-call | bytes 14680064 | tf_op jit(solution)/shard_map/pack/pallas_call | solution.py:86
  23.1 4.3 %collective-permute-done.partner = bf16[1088,128]{1,0:T(8,128)(2,1)S(1)} collective-permute-done((bf16[1088,128]{1,0:T(8,128)(2,1)S(1)}, bf16[1088,128]{1,0:T(8,128)(2,1)S(1)}, u32[]{:S(2)}, u32[]{:S(2)}) %collective-permute-start) | collective-permute-done | bytes 278560 | tf_op jit(solution)/shard_map/ppermute | solution.py:31
  28.1 2.3 %join.1 = (bf16[2176,256]{1,0:T(8,128)(2,1)}, bf16[2176,256]{1,0:T(8,128)(2,1)}, bf16[2192,256]{1,0:T(8,128)(2,1)}, bf16[2176,128]{1,0:T(8,128)(2,1)}, bf16[2176,128]{1,0:T(8,128)(2,1)}) custom-call(bf16[64,128]{1,0:T(8,128)(2,1)} %pad_maximum_fusion.3.left, bf16[128,128]{1,0:T(8,128)(2,1)} %bitcast.76, ...), custom_call_target="tpu_custom_call", output_to_operand_aliasing={{0}: (6, {}), {1}: (7, {}), {2}: (8, {})} | custom-call | bytes 3145728 | tf_op jit(solution)/shard_map/join/pallas_call | solution.py:114
  31.3 1.6 collective-permute-start.9
  33.0 2.0 %collective-permute-start.4 = (bf16[2048,256]{1,0:T(8,128)(2,1)}, bf16[2048,256]{1,0:T(8,128)(2,1)}, u32[]{:S(2)}, u32[]{:S(2)}) collective-permute-start(bf16[2048,256]{1,0:T(8,128)(2,1)} %get-tuple-element.42), channel_id=1, source_target_pairs={{0,64},{1,65},{2,66},{3,67},{4,68},{5,69},{6,70},{7,71},{8,72},{9,... | collective-permute-start | bytes 3145736 | tf_op jit(solution)/shard_map/ppermute | solution.py:27
  36.5 1.7 collective-permute-start.10
  38.2 2.0 %collective-permute-start.11 = (bf16[2192,256]{1,0:T(8,128)(2,1)S(1)}, bf16[2192,256]{1,0:T(8,128)(2,1)S(1)}, u32[]{:S(2)}, u32[]{:S(2)}) collective-permute-start(bf16[2192,256]{1,0:T(8,128)(2,1)S(1)} %copy-done.2), channel_id=1, source_target_pairs={{0,32},{1,33},{2,34},{3,35},{4,36},{5,37},{6,38},{7,39},{8,40},{9,... | collective-permute-start | bytes 3366920 | tf_op jit(solution)/shard_map/ppermute | solution.py:27
  40.9 20.0 %collective-permute-done.4.h1 = bf16[2048,256]{1,0:T(8,128)(2,1)} collective-permute-done((bf16[2048,256]{1,0:T(8,128)(2,1)}, bf16[2048,256]{1,0:T(8,128)(2,1)}, u32[]{:S(2)}, u32[]{:S(2)}) %collective-permute-start.4) | collective-permute-done | bytes 1048608 | tf_op jit(solution)/shard_map/ppermute | solution.py:27
  60.9 20.1 %collective-permute-done.3.h2 = bf16[2048,256]{1,0:T(8,128)(2,1)} collective-permute-done((bf16[2048,256]{1,0:T(8,128)(2,1)}, bf16[2048,256]{1,0:T(8,128)(2,1)}, u32[]{:S(2)}, u32[]{:S(2)}) %collective-permute-start.3) | collective-permute-done | bytes 1048608 | tf_op jit(solution)/shard_map/ppermute | solution.py:27
  81.0 2.0 %collective-permute-start.5 = (bf16[2048,256]{1,0:T(8,128)(2,1)}, bf16[2048,256]{1,0:T(8,128)(2,1)}, u32[]{:S(2)}, u32[]{:S(2)}) collective-permute-start(bf16[2048,256]{1,0:T(8,128)(2,1)} %get-tuple-element.43), channel_id=1, source_target_pairs={{0,64},{1,65},{2,66},{3,67},{4,68},{5,69},{6,70},{7,71},{8,72},{9,... | collective-permute-start | bytes 3145736 | tf_op jit(solution)/shard_map/ppermute | solution.py:27
  83.0 1.6 collective-permute-start.6
  84.6 1.7 %collective-permute-start.7 = (bf16[2048,256]{1,0:T(8,128)(2,1)}, bf16[2048,256]{1,0:T(8,128)(2,1)}, u32[]{:S(2)}, u32[]{:S(2)}) collective-permute-start(bf16[2048,256]{1,0:T(8,128)(2,1)} %collective-permute-done.3.h2), channel_id=1, source_target_pairs={{0,48},{1,49},{2,50},{3,51},{4,52},{5,53},{6,54},{7,55},{8,56},{9,... | collective-permute-start | bytes 3145736 | tf_op jit(solution)/shard_map/ppermute | solution.py:27
  87.2 15.7 %own_part.1 = (f32[4,1024,256]{2,1,0:T(8,128)}, f32[1024,64]{1,0:T(8,128)}) custom-call(s32[13]{0:T(128)} %stack.113.idx, bf16[8,2176,128]{2,1,0:T(8,128)(2,1)} %bitcast.81, bf16[2048,2048]{1,0:T(8,128)(2,1)} %base.5), custom_call_target="tpu_custom_call" | custom-call | flops 5368709120 | bytes 13631488 | tf_op jit(solution)/shard_map/own_part/pallas_call | solution.py:164
  103.0 1.6 collective-permute-start.13
  104.6 5.6 %collective-permute-done.13 = bf16[4,192,128]{2,1,0:T(8,128)(2,1)S(1)} collective-permute-done((bf16[4,192,128]{2,1,0:T(8,128)(2,1)S(1)}, bf16[4,192,128]{2,1,0:T(8,128)(2,1)S(1)}, u32[]{:S(2)}, u32[]{:S(2)}) %collective-permute-start.13) | collective-permute-done | bytes 196640 | tf_op jit(solution)/shard_map/ppermute | solution.py:31
  111.1 2.5 %collective-permute-start.12 = (bf16[2048,256]{1,0:T(8,128)(2,1)}, bf16[2048,256]{1,0:T(8,128)(2,1)S(1)}, u32[]{:S(2)}, u32[]{:S(2)}) collective-permute-start(bf16[2048,256]{1,0:T(8,128)(2,1)} %collective-permute-done.5.h3), channel_id=1, source_target_pairs={{0,32},{1,33},{2,34},{3,35},{4,36},{5,37},{6,38},{7,39},{8,40},{9,... | collective-permute-start | bytes 3145736 | tf_op jit(solution)/shard_map/ppermute | solution.py:27
  113.6 2.0 %collective-permute-start.8 = (bf16[2064,256]{1,0:T(8,128)(2,1)}, bf16[2064,256]{1,0:T(8,128)(2,1)S(1)}, u32[]{:S(2)}, u32[]{:S(2)}) collective-permute-start(bf16[2064,256]{1,0:T(8,128)(2,1)} %get-tuple-element.54), channel_id=1, source_target_pairs={{0,64},{1,65},{2,66},{3,67},{4,68},{5,69},{6,70},{7,71},{8,72},{9,... | collective-permute-start | bytes 3170312 | tf_op jit(solution)/shard_map/ppermute | solution.py:27
  116.5 14.2 %partner_part.1 = (bf16[1024,256]{1,0:T(8,128)(2,1)}, bf16[1024,256]{1,0:T(8,128)(2,1)}, bf16[1024,256]{1,0:T(8,128)(2,1)}, bf16[1024,64]{1,0:T(8,128)(2,1)}) custom-call(s32[13]{0:T(128)} %stack.113.idx, bf16[8,2176,128]{2,1,0:T(8,128)(2,1)} %bitcast.70, bf16[2048,256]{1,0:T(8,128)(2,1)} %collective-permute-done.4.h1, ...), custom_call_target="tpu_custom_call" | custom-call | flops 4294967296 | bytes 12582912 | tf_op jit(solution)/shard_map/partner_part/pallas_call | solution.py:204
  132.8 2.5 %collective-permute-start.15 = (bf16[1024,256]{1,0:T(8,128)(2,1)}, bf16[1024,256]{1,0:T(8,128)(2,1)S(1)}, u32[]{:S(2)}, u32[]{:S(2)}) collective-permute-start(bf16[1024,256]{1,0:T(8,128)(2,1)} %get-tuple-element.67), channel_id=1, source_target_pairs={{0,48},{1,49},{2,50},{3,51},{4,52},{5,53},{6,54},{7,55},{8,56},{9,... | collective-permute-start | bytes 1572872 | tf_op jit(solution)/shard_map/ppermute | solution.py:27
  139.8 13.6 %merge.1 = (bf16[16384,256]{1,0:T(8,128)(2,1)}, f32[1,256]{1,0:T(1,128)}, f32[1024,256]{1,0:T(8,128)}) custom-call(s32[13]{0:T(128)} %stack.113.idx, bf16[2048,2048]{1,0:T(8,128)(2,1)} %base.5, bf16[2064,256]{1,0:T(8,128)(2,1)} %copy-done.4, bf16[2176,256]{1,0:T(8,128)(2,1)} %copy-done.1, bf16[2048,256]{1,0:T(8,128)(2,1)} %collective-permute-done.6.refs_2_, ...), custom_call_target="tpu_custom_call" | custom-call | flops 1073741824 | bytes 18874368 | tf_op jit(solution)/shard_map/merge/pallas_call | solution.py:290
  154.9 2.0 %collective-permute-done.15 = bf16[1024,256]{1,0:T(8,128)(2,1)S(1)} collective-permute-done((bf16[1024,256]{1,0:T(8,128)(2,1)}, bf16[1024,256]{1,0:T(8,128)(2,1)S(1)}, u32[]{:S(2)}, u32[]{:S(2)}) %collective-permute-start.15) | collective-permute-done | bytes 524320 | tf_op jit(solution)/shard_map/ppermute | solution.py:27
  157.8 2.1 %fusion = bf16[1,1024,256]{2,1,0:T(8,128)(2,1)} fusion(bf16[1024,256]{1,0:T(8,128)(2,1)} %collective-permute-done.16, f32[1024,256]{1,0:T(8,128)S(1)} %convert_add_fusion, bf16[1024,256]{1,0:T(8,128)(2,1)S(1)} %collective-permute-done.15, f32[256]{0:T(256)S(1)} %bitcast.79), kind=kLoop, calls=%fused_computation.2 | loop fusion | flops 1572864 | bytes 2622464 | tf_op jit(solution)/shard_map/broadcast_in_dim | solution.py:384
  (88 shorter events, 18.9 us)
Async XLA Ops:
  7.2 80.1 %all-gather.7.cloned.1.call-start = ((), (), s32[]{:S(2)}) async-start(), calls=%async_computation | async-start | bytes 5013504 | tf_op jit(solution)/shard_map/all_gather | solution.py:36
  9.3 13.0 %copy-start.3 = (bf16[1088,128]{1,0:T(8,128)(2,1)}, bf16[1088,128]{1,0:T(8,128)(2,1)S(1)}, u32[]{:S(2)}) copy-start(bf16[1088,128]{1,0:T(8,128)(2,1)S(1)} %maximum_maximum_fusion.small) | copy-start | bytes 835588
  9.3 13.7 %collective-permute-start.2 = (bf16[1088,128]{1,0:T(8,128)(2,1)S(1)}, bf16[1088,128]{1,0:T(8,128)(2,1)S(1)}, u32[]{:S(2)}, u32[]{:S(2)}) collective-permute-start(bf16[1088,128]{1,0:T(8,128)(2,1)S(1)} %maximum_maximum_fusion.small), channel_id=1, source_target_pairs={{0,66},{1,67},{2,64},{3,65},{4,70},{5,71},{6,68},{7,69},{8,74},{9,... | collective-permute-start | bytes 835592 | tf_op jit(solution)/shard_map/ppermute | solution.py:31
  13.5 9.6 %collective-permute-start.1 = (bf16[1088,128]{1,0:T(8,128)(2,1)S(1)}, bf16[1088,128]{1,0:T(8,128)(2,1)S(1)}, u32[]{:S(2)}, u32[]{:S(2)}) collective-permute-start(bf16[1088,128]{1,0:T(8,128)(2,1)S(1)} %maximum_maximum_fusion.small), channel_id=1, source_target_pairs={{0,2},{1,3},{2,0},{3,1},{4,6},{5,7},{6,4},{7,5},{8,10},{9,11},{10,... | collective-permute-start | bytes 835592 | tf_op jit(solution)/shard_map/ppermute | solution.py:31
  13.5 13.9 %collective-permute-start = (bf16[1088,128]{1,0:T(8,128)(2,1)S(1)}, bf16[1088,128]{1,0:T(8,128)(2,1)S(1)}, u32[]{:S(2)}, u32[]{:S(2)}) collective-permute-start(bf16[1088,128]{1,0:T(8,128)(2,1)S(1)} %maximum_maximum_fusion.small), channel_id=1, source_target_pairs={{0,64},{1,65},{2,66},{3,67},{4,68},{5,69},{6,70},{7,71},{8,72},{9,... | collective-permute-start | bytes 835592 | tf_op jit(solution)/shard_map/ppermute | solution.py:31
  30.5 10.4 %slice-start = ((bf16[1088,128]{1,0:T(8,128)(2,1)}), bf16[64,128]{1,0:T(8,128)(2,1)S(1)}, s32[]{:S(2)}) async-start(bf16[1088,128]{1,0:T(8,128)(2,1)} %copy-done.6), calls=%async_computation.3 | async-start | bytes 32768 | tf_op jit(solution)/shard_map/slice | solution.py:344
  30.5 10.4 %copy-start.10 = (bf16[8,2048]{1,0:T(8,128)(2,1)S(1)}, bf16[8,2048]{1,0:T(8,128)(2,1)}, u32[]{:S(2)}) copy-start(bf16[8,2048]{1,0:T(8,128)(2,1)} %param.8) | copy-start | bytes 98308
  30.5 85.9 %all-gather.11.cloned.1.call-start = ((), (), s32[]{:S(2)}) async-start(), calls=%async_computation.2 | async-start | bytes 5013504 | tf_op jit(solution)/shard_map/all_gather | solution.py:36
  31.3 107.3 %all-gather.9.cloned.1.call-start = ((), (), s32[]{:S(2)}) async-start(), calls=%async_computation.1 | async-start | bytes 2359296 | tf_op jit(solution)/shard_map/all_gather | solution.py:36
  31.3 53.2 %collective-permute-start.9 = (bf16[2176,256]{1,0:T(8,128)(2,1)}, bf16[2176,256]{1,0:T(8,128)(2,1)S(1)}, u32[]{:S(2)}, u32[]{:S(2)}) collective-permute-start(bf16[2176,256]{1,0:T(8,128)(2,1)} %get-tuple-element.55), channel_id=1, source_target_pairs={{0,16},{1,17},{2,18},{3,19},{4,20},{5,21},{6,22},{7,23},{8,24},{9,... | collective-permute-start | bytes 3342344 | tf_op jit(solution)/shard_map/ppermute | solution.py:27
  33.0 27.9 %collective-permute-start.4 = (bf16[2048,256]{1,0:T(8,128)(2,1)}, bf16[2048,256]{1,0:T(8,128)(2,1)}, u32[]{:S(2)}, u32[]{:S(2)}) collective-permute-start(bf16[2048,256]{1,0:T(8,128)(2,1)} %get-tuple-element.42), channel_id=1, source_target_pairs={{0,64},{1,65},{2,66},{3,67},{4,68},{5,69},{6,70},{7,71},{8,72},{9,... | collective-permute-start | bytes 3145736 | tf_op jit(solution)/shard_map/ppermute | solution.py:27
  34.9 46.1 %collective-permute-start.3 = (bf16[2048,256]{1,0:T(8,128)(2,1)}, bf16[2048,256]{1,0:T(8,128)(2,1)}, u32[]{:S(2)}, u32[]{:S(2)}) collective-permute-start(bf16[2048,256]{1,0:T(8,128)(2,1)} %get-tuple-element.40), channel_id=1, source_target_pairs={{0,64},{1,65},{2,66},{3,67},{4,68},{5,69},{6,70},{7,71},{8,72},{9,... | collective-permute-start | bytes 3145736 | tf_op jit(solution)/shard_map/ppermute | solution.py:27
  36.5 49.8 %collective-permute-start.10 = (bf16[2176,256]{1,0:T(8,128)(2,1)}, bf16[2176,256]{1,0:T(8,128)(2,1)}, u32[]{:S(2)}, u32[]{:S(2)}) collective-permute-start(bf16[2176,256]{1,0:T(8,128)(2,1)} %get-tuple-element.56), channel_id=1, source_target_pairs={{0,48},{1,49},{2,50},{3,51},{4,52},{5,53},{6,54},{7,55},{8,56},{9,... | collective-permute-start | bytes 3342344 | tf_op jit(solution)/shard_map/ppermute | solution.py:27
  38.2 48.9 %collective-permute-start.11 = (bf16[2192,256]{1,0:T(8,128)(2,1)S(1)}, bf16[2192,256]{1,0:T(8,128)(2,1)S(1)}, u32[]{:S(2)}, u32[]{:S(2)}) collective-permute-start(bf16[2192,256]{1,0:T(8,128)(2,1)S(1)} %copy-done.2), channel_id=1, source_target_pairs={{0,32},{1,33},{2,34},{3,35},{4,36},{5,37},{6,38},{7,39},{8,40},{9,... | collective-permute-start | bytes 3366920 | tf_op jit(solution)/shard_map/ppermute | solution.py:27
  81.0 30.0 %collective-permute-start.5 = (bf16[2048,256]{1,0:T(8,128)(2,1)}, bf16[2048,256]{1,0:T(8,128)(2,1)}, u32[]{:S(2)}, u32[]{:S(2)}) collective-permute-start(bf16[2048,256]{1,0:T(8,128)(2,1)} %get-tuple-element.43), channel_id=1, source_target_pairs={{0,64},{1,65},{2,66},{3,67},{4,68},{5,69},{6,70},{7,71},{8,72},{9,... | collective-permute-start | bytes 3145736 | tf_op jit(solution)/shard_map/ppermute | solution.py:27
  83.0 28.0 %collective-permute-start.6 = (bf16[2048,256]{1,0:T(8,128)(2,1)}, bf16[2048,256]{1,0:T(8,128)(2,1)}, u32[]{:S(2)}, u32[]{:S(2)}) collective-permute-start(bf16[2048,256]{1,0:T(8,128)(2,1)} %collective-permute-done.4.h1), channel_id=1, source_target_pairs={{0,16},{1,17},{2,18},{3,19},{4,20},{5,21},{6,22},{7,23},{8,24},{9,... | collective-permute-start | bytes 3145736 | tf_op jit(solution)/shard_map/ppermute | solution.py:27
  84.6 26.4 %collective-permute-start.7 = (bf16[2048,256]{1,0:T(8,128)(2,1)}, bf16[2048,256]{1,0:T(8,128)(2,1)}, u32[]{:S(2)}, u32[]{:S(2)}) collective-permute-start(bf16[2048,256]{1,0:T(8,128)(2,1)} %collective-permute-done.3.h2), channel_id=1, source_target_pairs={{0,48},{1,49},{2,50},{3,51},{4,52},{5,53},{6,54},{7,55},{8,56},{9,... | collective-permute-start | bytes 3145736 | tf_op jit(solution)/shard_map/ppermute | solution.py:27
  87.1 15.9 %copy-start = (bf16[2192,256]{1,0:T(8,128)(2,1)}, bf16[2192,256]{1,0:T(8,128)(2,1)S(1)}, u32[]{:S(2)}) copy-start(bf16[2192,256]{1,0:T(8,128)(2,1)S(1)} %collective-permute-done.11.refs_5_) | copy-start | bytes 3366916
  103.0 7.3 %collective-permute-start.13 = (bf16[4,192,128]{2,1,0:T(8,128)(2,1)S(1)}, bf16[4,192,128]{2,1,0:T(8,128)(2,1)S(1)}, u32[]{:S(2)}, u32[]{:S(2)}) collective-permute-start(bf16[4,192,128]{2,1,0:T(8,128)(2,1)S(1)} %pad_maximum_fusion.2), channel_id=1, source_target_pairs={{0,64},{1,65},{2,66},{3,67},{4,68},{5,69},{6,70},{7,71},{8,72},{9,... | collective-permute-start | bytes 589832 | tf_op jit(solution)/shard_map/ppermute | solution.py:31
  111.1 27.4 %collective-permute-start.12 = (bf16[2048,256]{1,0:T(8,128)(2,1)}, bf16[2048,256]{1,0:T(8,128)(2,1)S(1)}, u32[]{:S(2)}, u32[]{:S(2)}) collective-permute-start(bf16[2048,256]{1,0:T(8,128)(2,1)} %collective-permute-done.5.h3), channel_id=1, source_target_pairs={{0,32},{1,33},{2,34},{3,35},{4,36},{5,37},{6,38},{7,39},{8,40},{9,... | collective-permute-start | bytes 3145736 | tf_op jit(solution)/shard_map/ppermute | solution.py:27
  113.6 24.9 %collective-permute-start.8 = (bf16[2064,256]{1,0:T(8,128)(2,1)}, bf16[2064,256]{1,0:T(8,128)(2,1)S(1)}, u32[]{:S(2)}, u32[]{:S(2)}) collective-permute-start(bf16[2064,256]{1,0:T(8,128)(2,1)} %get-tuple-element.54), channel_id=1, source_target_pairs={{0,64},{1,65},{2,66},{3,67},{4,68},{5,69},{6,70},{7,71},{8,72},{9,... | collective-permute-start | bytes 3170312 | tf_op jit(solution)/shard_map/ppermute | solution.py:27
  130.7 22.8 %collective-permute-start.14 = (bf16[1024,256]{1,0:T(8,128)(2,1)}, bf16[1024,256]{1,0:T(8,128)(2,1)S(1)}, u32[]{:S(2)}, u32[]{:S(2)}) collective-permute-start(bf16[1024,256]{1,0:T(8,128)(2,1)} %get-tuple-element.66), channel_id=1, source_target_pairs={{0,16},{1,17},{2,18},{3,19},{4,20},{5,21},{6,22},{7,23},{8,24},{9,... | collective-permute-start | bytes 1572872 | tf_op jit(solution)/shard_map/ppermute | solution.py:27
  132.8 24.0 %collective-permute-start.15 = (bf16[1024,256]{1,0:T(8,128)(2,1)}, bf16[1024,256]{1,0:T(8,128)(2,1)S(1)}, u32[]{:S(2)}, u32[]{:S(2)}) collective-permute-start(bf16[1024,256]{1,0:T(8,128)(2,1)} %get-tuple-element.67), channel_id=1, source_target_pairs={{0,48},{1,49},{2,50},{3,51},{4,52},{5,53},{6,54},{7,55},{8,56},{9,... | collective-permute-start | bytes 1572872 | tf_op jit(solution)/shard_map/ppermute | solution.py:27
  135.3 22.4 %collective-permute-start.16 = (bf16[1024,256]{1,0:T(8,128)(2,1)}, bf16[1024,256]{1,0:T(8,128)(2,1)}, u32[]{:S(2)}, u32[]{:S(2)}) collective-permute-start(bf16[1024,256]{1,0:T(8,128)(2,1)} %get-tuple-element.68), channel_id=1, source_target_pairs={{0,32},{1,33},{2,34},{3,35},{4,36},{5,37},{6,38},{7,39},{8,40},{9,... | collective-permute-start | bytes 1572872 | tf_op jit(solution)/shard_map/ppermute | solution.py:27
  (9 other events, 27.7 us)
Sparse Core Ops, SparseCore 0:
  30.6 34.3 all-gather.6
  66.7 33.1 all-gather.10
  111.1 26.6 all-gather.8
